TPU v7x, 512 devices: a whole 4x4x16 slice. The times are simulated.
512 devices in a mesh: dp: 8 (over z_lo), group: 4 (over x), head: 16 (over y, z_hi, core).
Axes of the slice: x: 4, y: 4, z: 16 (z_hi: 2, z_lo: 8; z = z_hi * 8 + z_lo), core: 2. Of those that a mesh axis runs over, the one named last changes fastest.
Arguments:
- query: bfloat16 [16384, 8192], P('dp', ('group', 'head')), parts along dimension 0, may hold values from -200 to 200
- query_exp: int32 [256, 16384], P(('group', 'head'), 'dp'), parts along dimension 1, may hold values from -1 to 0
- kv: bfloat16 [16384, 1024], P('dp', 'group'), parts along dimension 0, may hold values from -10 to 10
- kv_exp: int32 [32, 16384], P('group', 'dp'), parts along dimension 1, may hold values from -2 to 2, as said below
- out_grad: bfloat16 [16384, 8192], P('dp', ('group', 'head')), parts along dimension 0, may hold values from -6 to 6
- out_grad_exp: int32 [256, 16384], P(('group', 'head'), 'dp'), parts along dimension 1, may hold values from -2 to 2
- q_weight: bfloat16 [16384, 8192], P('dp', ('group', 'head')), parts along dimension 0, may hold values from -0.1875 to 0.1875
- q_weight_exp: int32 [512, 8192], P('dp', ('group', 'head')), parts along dimension 0, may hold values from -1 to 1
- keyvalue_weight_mantissa: bfloat16 [16384, 1024], P(('dp', 'head'), 'group'), parts along dimension 0, may hold values from -0.375 to 0.375
- keyvalue_weight_exponent: int32 [512, 1024], P(('dp', 'head'), 'group'), parts along dimension 0, may hold values from -1 to 1
Outputs:
- input_grad: bfloat16 [16384, 2048], P(('dp', 'head'), 'group'), parts along dimension 0
- keyvalue_gradient: bfloat16 [16384, 1024], P(('dp', 'head'), 'group'), parts along dimension 0
There are 8 independent parts, one for each index of `dp`. A program takes and returns all parts, laid end to end along the dimension named above; each array names one. Nothing has to cross between parts.
Inputs may be any that keep to these rules, and one draw needn't show every extreme that they name: `kv_exp`: exponents of the key blocks lie in -1 to 0, those of the value blocks in -2 to 2.
All inputs are finite; a program needn't handle non-finite values.
Results may differ from a plain program's by a relative error of at most 0.022.
Values may be sent and summed in bfloat16 or wider, within the bound.
No kernel may reach another device: no remote copies, remote signals or barrier semaphores. Data moves between devices by JAX's collectives and lax.ppermute only.
A program may use at most 64 MiB of HBM per device.

v0:
```python
import jax
import jax.numpy as jnp
from jax import lax
from jax.sharding import PartitionSpec as P


def power_of_two(block_exponent):
    scale_lookup = jnp.zeros(block_exponent.shape, jnp.float32)
    for level in range(-4, 5):
        scale_lookup = scale_lookup + jnp.where(block_exponent == level, 2.0**level, 0.0).astype(
            jnp.float32
        )
    return scale_lookup


def dequant_rows(mantissa, block_exponent):
    scaling = jnp.repeat(power_of_two(block_exponent).T, 32, axis=1)
    return (mantissa.astype(jnp.float32) * scaling).astype(jnp.bfloat16)


def dequant_cols(mantissa, block_exponent):
    scaling = jnp.repeat(power_of_two(block_exponent), 32, axis=0)
    return (mantissa.astype(jnp.float32) * scaling).astype(jnp.bfloat16)


def shards(
    query,
    query_exp,
    kv,
    kv_exp,
    out_grad,
    out_grad_exp,
    q_weight,
    q_weight_exp,
    keyvalue_weight_mantissa,
    keyvalue_weight_exponent,
):
    seq_len = query.shape[0]
    head_dim = query.shape[1]
    scale = 1.0 / head_dim**0.5
    q_local = dequant_rows(query, query_exp)
    kv_local = dequant_rows(kv, kv_exp)
    do_local = dequant_rows(out_grad, out_grad_exp)
    keys = kv_local[:, :head_dim]
    value_matrix = kv_local[:, head_dim:]
    block = min(512, seq_len)
    blocks = seq_len // block
    dq_parts = []
    dk_accum = jnp.zeros((seq_len, head_dim), jnp.float32)
    dv_accum = jnp.zeros((seq_len, head_dim), jnp.float32)
    for index in range(blocks):
        first = index * block
        upper = first + block
        q_block = q_local[first:upper]
        do_block = do_local[first:upper]
        key_rows = keys[:upper]
        value_rows = value_matrix[:upper]
        scores = (
            lax.dot_general(
                q_block, key_rows, (((1,), (1,)), ((), ())), preferred_element_type=jnp.float32
            )
            * scale
        )
        row_pos = first + jnp.arange(block, dtype=jnp.int32)[:, None]
        col_pos = jnp.arange(upper, dtype=jnp.int32)[None, :]
        scores = jnp.where(col_pos <= row_pos, scores, -jnp.inf)
        peak = jnp.max(scores, axis=1, keepdims=True)
        expd = jnp.exp(scores - peak)
        probs = expd / jnp.sum(expd, axis=1, keepdims=True)
        probs_b = probs.astype(jnp.bfloat16)
        output = jnp.dot(probs_b, value_rows, preferred_element_type=jnp.float32)
        delta = jnp.sum(do_block.astype(jnp.float32) * output, axis=1, keepdims=True)
        dprob = lax.dot_general(
            do_block, value_rows, (((1,), (1,)), ((), ())), preferred_element_type=jnp.float32
        )
        dscore = (probs * (dprob - delta) * scale).astype(jnp.bfloat16)
        dq_parts.append(
            jnp.dot(dscore, key_rows, preferred_element_type=jnp.float32).astype(jnp.bfloat16)
        )
        dk_accum = dk_accum.at[:upper].add(
            lax.dot_general(
                dscore, q_block, (((0,), (0,)), ((), ())), preferred_element_type=jnp.float32
            )
        )
        dv_accum = dv_accum.at[:upper].add(
            lax.dot_general(
                probs_b, do_block, (((0,), (0,)), ((), ())), preferred_element_type=jnp.float32
            )
        )
    dq_local = jnp.concatenate(dq_parts, axis=0)
    dkv_local = jnp.concatenate(
        [dk_accum.astype(jnp.bfloat16), dv_accum.astype(jnp.bfloat16)], axis=1
    )
    packed = jnp.concatenate([dq_local, dkv_local], axis=1)[:, None, :]
    moved = lax.all_to_all(packed, "head", split_axis=0, concat_axis=1, tiled=True)
    tok_rows = moved.shape[0]
    sources = moved.shape[1]
    dq_tokens = moved[:, :, :head_dim].reshape(tok_rows, sources * head_dim)
    kv_sum = jnp.sum(moved[:, :, head_dim:].astype(jnp.float32), axis=1)
    keyvalue_gradient = kv_sum.astype(jnp.bfloat16)
    w_query = dequant_cols(q_weight, q_weight_exp)
    total = lax.dot_general(
        dq_tokens,
        lax.all_gather(w_query, "head", axis=1, tiled=True),
        (((1,), (1,)), ((), ())),
        preferred_element_type=jnp.float32,
    )
    w_keyval = dequant_cols(keyvalue_weight_mantissa, keyvalue_weight_exponent)
    whole_keyval = lax.all_gather(w_keyval, "head", axis=0, tiled=True)
    total = total + lax.dot_general(
        keyvalue_gradient,
        whole_keyval,
        (((1,), (1,)), ((), ())),
        preferred_element_type=jnp.float32,
    )
    input_grad = lax.psum_scatter(
        total.astype(jnp.bfloat16), "group", scatter_dimension=1, tiled=True
    )
    return (input_grad, keyvalue_gradient)


def solution(mesh):
    return jax.shard_map(
        shards,
        mesh=mesh,
        in_specs=(
            P("dp", ("group", "head")),
            P(("group", "head"), "dp"),
            P("dp", "group"),
            P("group", "dp"),
            P("dp", ("group", "head")),
            P(("group", "head"), "dp"),
            P("dp", ("group", "head")),
            P("dp", ("group", "head")),
            P(("dp", "head"), "group"),
            P(("dp", "head"), "group"),
        ),
        out_specs=(P(("dp", "head"), "group"), P(("dp", "head"), "group")),
        check_vma=False,
    )
```

profile of v0, /device:TPU:8, one launch (start us, length us, event | category | flops | bytes accessed | tf_op | source)
XLA Modules:
  0.0 347.8 jit_solution(5404532560572737366)
XLA Ops:
  7.2 0.9 select_add_fusion
  8.1 2.0 fusion.26
  10.1 1.0 add_bitcast_fusion
  11.1 0.8 add_bitcast_fusion.2
  11.9 0.6 copy.52
  13.7 0.4 fusion.75
  14.5 0.3 fusion.70
  15.1 0.4 fusion.19
  15.5 0.3 fusion.61
  15.9 0.6 fusion.76
  16.5 0.5 fusion.15
  17.0 0.4 convolution_convert_fusion.1
  17.4 0.8 fusion.77
  18.2 0.6 fusion.7
  18.8 0.7 fusion.6
  19.4 0.7 fusion.22
  20.1 0.6 fusion.23
  20.8 0.7 multiply_convert_fusion.1
  21.5 0.4 convolution_convert_fusion.2
  21.9 0.6 fusion.5
  22.5 0.6 convolution_convert_fusion.3
  23.1 0.5 fusion.21
  23.6 1.0 fusion.78
  24.7 0.7 fusion.1
  25.4 0.8 fusion
  26.2 0.9 fusion.24
  27.1 1.0 multiply_convert_fusion
  28.0 0.7 convolution_convert_fusion
  28.7 0.7 fusion.9
  29.5 0.8 fusion.11
  30.3 0.8 fusion.20
  31.0 0.7 fusion.8
  31.7 0.8 fusion.12
  32.7 0.5 broadcast.219
  33.2 1.9 reduce.19
  35.1 1.4 reshape.246
  36.5 18.3 %all-to-all-start = ((bf16[16,2,24576]{2,1,0:T(2,128)(2,1)}), bf16[16,2,24576]{2,1,0:T(2,128)(2,1)}, u32[]{:S(2)}, u32[]{:S(2)}) async-start(bf16[16,2,24576]{2,1,0:T(2,128)(2,1)} %reshape.246), calls=%async_computation | async-start | bytes 3145728 | tf_op jit(solution)/shard_map/all_to_all | solution.py:95
  54.9 0.6 fusion.50
  55.6 139.3 %all-to-all-done = bf16[16,2,24576]{2,1,0:T(2,128)(2,1)} async-done(((bf16[16,2,24576]{2,1,0:T(2,128)(2,1)}), bf16[16,2,24576]{2,1,0:T(2,128)(2,1)}, u32[]{:S(2)}, u32[]{:S(2)}) %all-to-all-start) | async-done | bytes 1572896 | tf_op jit(solution)/shard_map/all_to_all | solution.py:95
  195.0 8.1 %reshape.247 = bf16[2048,1,384]{2,1,0:T(2,128)(2,1)S(1)} reshape(bf16[16,2,24576]{2,1,0:T(2,128)(2,1)} %all-to-all-done) | data formatting | bytes 3145728
  203.3 1.2 copy-done
  204.7 0.3 copy.64
  204.9 1.4 slice_reduce_fusion
  206.3 37.9 %all-gather.3.cloned.1.call-done = bf16[2048,2048]{1,0:T(8,128)(2,1)} async-done(((bf16[2048,128]{1,0:T(8,128)(2,1)}), bf16[2048,2048]{1,0:T(8,128)(2,1)}) %all-gather.3.cloned.1.call-update) | async-done | bytes 8388624 | tf_op jit(solution)/shard_map/all_gather | solution.py:104
  244.2 6.3 %fusion.79 = f32[128,2048]{1,0:T(8,128)S(1)} fusion(bf16[128,2048]{0,1:T(8,128)(2,1)S(1)} %bitcast.50, bf16[2048,2048]{1,0:T(8,128)(2,1)} %all-gather.3.cloned.1.call-done), kind=kOutput, calls=%fused_computation.123 | convolution fusion | flops 1073741824 | bytes 9961472 | tf_op jit(solution)/shard_map/dot_general | solution.py:102
  250.6 67.1 %all-gather.5.cloned.1.call-done = bf16[2048,256]{1,0:T(8,128)(2,1)} async-done(((bf16[128,256]{1,0:T(8,128)(2,1)}), bf16[2048,256]{1,0:T(8,128)(2,1)}) %all-gather.5.cloned.1.call-update) | async-done | bytes 1048592 | tf_op jit(solution)/shard_map/all_gather | solution.py:109
  317.7 2.5 fusion.10
  320.2 21.1 %reduce-scatter.2.cloned.1.call-done = bf16[128,512]{1,0:T(8,128)(2,1)} async-done(((bf16[128,2048]{1,0:T(8,128)(2,1)}), bf16[128,512]{1,0:T(8,128)(2,1)}) %reduce-scatter.2.cloned.1.call-update) | async-done | bytes 131088 | tf_op jit(solution)/shard_map/reduce_scatter | solution.py:116
  (39 shorter events, 2.6 us)
Async XLA Ops:
  7.2 4.7 %copy-start.1 = (bf16[2048,256]{1,0:T(8,128)(2,1)S(1)}, bf16[2048,256]{1,0:T(8,128)(2,1)}, u32[]{:S(2)}) copy-start(bf16[2048,256]{1,0:T(8,128)(2,1)} %param.32) | copy-start | bytes 3145732
  7.2 5.4 %copy-start.2 = (bf16[2048,128]{1,0:T(8,128)(2,1)S(1)}, bf16[2048,128]{1,0:T(8,128)(2,1)}, u32[]{:S(2)}) copy-start(bf16[2048,128]{1,0:T(8,128)(2,1)} %param.30) | copy-start | bytes 1572868
  7.2 237.1 %all-gather.3.cloned.1.call-start = ((), (), s32[]{:S(2)}) async-start(), calls=%async_computation.2 | async-start | bytes 8912896 | tf_op jit(solution)/shard_map/all_gather | solution.py:104
  10.1 2.7 copy-start.3
  12.8 0.8 copy-start.6
  36.5 18.4 %copy-start.7 = (s32[4,256]{1,0:T(4,128)S(1)}, s32[4,256]{1,0:T(4,128)}, u32[]{:S(2)}) copy-start(s32[4,256]{1,0:T(4,128)} %param.39) | copy-start | bytes 12292
  36.5 18.4 %copy-start.5 = (bf16[128,256]{1,0:T(8,128)(2,1)S(1)}, bf16[128,256]{1,0:T(8,128)(2,1)}, u32[]{:S(2)}) copy-start(bf16[128,256]{1,0:T(8,128)(2,1)} %param.38) | copy-start | bytes 196612
  36.5 158.5 %all-to-all-start = ((bf16[16,2,24576]{2,1,0:T(2,128)(2,1)}), bf16[16,2,24576]{2,1,0:T(2,128)(2,1)}, u32[]{:S(2)}, u32[]{:S(2)}) async-start(bf16[16,2,24576]{2,1,0:T(2,128)(2,1)} %reshape.246), calls=%async_computation | async-start | bytes 3145728 | tf_op jit(solution)/shard_map/all_to_all | solution.py:95
  54.8 262.9 %all-gather.5.cloned.1.call-start = ((), (), s32[]{:S(2)}) async-start(), calls=%async_computation.3 | async-start | bytes 1114112 | tf_op jit(solution)/shard_map/all_gather | solution.py:109
  55.6 285.7 %reduce-scatter.2.cloned.1.call-start = ((), (), s32[]{:S(2)}) async-start(), calls=%async_computation.4 | async-start | bytes 655360 | tf_op jit(solution)/shard_map/reduce_scatter | solution.py:116
  203.3 1.2 copy-start
  206.3 111.4 %copy-start.4 = (bf16[128,256]{1,0:T(8,128)(2,1)}, bf16[128,256]{1,0:T(8,128)(2,1)S(1)}, u32[]{:S(2)}) copy-start(bf16[128,256]{1,0:T(8,128)(2,1)S(1)} %slice_reduce_fusion) | copy-start | bytes 196612
Sparse Core Ops, SparseCore 0:
  11.1 233.0 all-gather.2
  248.1 69.5 all-gather.4
  321.1 20.1 reduce-scatter.1
where the time goes:
time: 349 us; the launch traced here: 348 us
  waiting for transfers between devices  266 us (76%)
  matrix products  23.6 us (7%)
  starting transfers between devices  18.4 us (5%)
  between operations  14.1 us (4%)
  local copies, waits for them, and re-layouts  13.2 us (4%)
  other arithmetic  13 us (4%)
    all_to_all x1, waiting for transfers between devices, shards(): lax.all_to_all(packed, 'head', split_axis=0, concat_axis=1, tiled=True)  139 us
    all_gather x1, waiting for transfers between devices, shards(): whole_keyval = lax.all_gather(w_keyval, 'head', axis=0, tiled=True)  67.1 us
    all_gather x1, waiting for transfers between devices, shards(): lax.all_gather(w_query, 'head', axis=1, tiled=True)  37.9 us
    reduce_scatter x1, waiting for transfers between devices, shards(): lax.psum_scatter(total.astype(jnp.bfloat16), 'group', scatter_dimension=1...  21.1 us
    all_to_all x1, starting transfers between devices, shards(): lax.all_to_all(packed, 'head', split_axis=0, concat_axis=1, tiled=True)  18.3 us
    unnamed x22, local copies, waits for them, and re-layouts  12.2 us
  transfers between devices with their start and end apart: 4, of which 4 were waited for; matrix products, arithmetic and copies ran while one was open for 12% of the time, Pallas kernels for 0%

commit v1 on v0

v1 whole, which is shorter than its diff:
```python
import functools, math
import jax, jax.numpy as jnp
from jax import lax
from jax.experimental import pallas as pl
from jax.experimental.pallas import tpu as pltpu
from jax.sharding import Mesh, PartitionSpec as P

VM = pl.BlockSpec(memory_space=pltpu.VMEM)
NT = (((1,), (1,)), ((), ()))
NN = (((1,), (0,)), ((), ()))


def power(exps):
    return lax.shift_left(jnp.ones_like(exps), exps + 4).astype(jnp.float32) * 0.0625


def fold(x, op):
    rows = x.shape[0]
    while rows > 8:
        rows //= 2
        x = op(x[:rows], x[rows:])
    return x


def attention_kernel(query, q_exp, kv, kv_exp, grad, grad_exp, out, q_s, k_s, v_s, do_s, kt_s, s_s, dp_s, ds_s, dk_s, dv_s, *, block, tile):
    seq, width = query.shape
    scale = 1.0 / math.sqrt(width)
    coef = scale * math.log2(math.e)
    exps = jnp.concatenate([q_exp[...], grad_exp[...], kv_exp[...]], axis=0)
    parts = exps.shape[0]
    powers = power(exps).T.astype(jnp.bfloat16)
    rows = lax.broadcasted_iota(jnp.int32, (parts, parts * 32), 0)
    cols = lax.broadcasted_iota(jnp.int32, (parts, parts * 32), 1)
    spread = jnp.where(cols // 32 == rows, 1.0, 0.0).astype(jnp.bfloat16)
    scales = lax.dot_general(powers, spread, NN, preferred_element_type=jnp.float32)
    q_s[...] = (query[...].astype(jnp.float32) * scales[:, :width]).astype(jnp.bfloat16)
    do_s[...] = (grad[...].astype(jnp.float32) * scales[:, width:2 * width]).astype(jnp.bfloat16)
    keys = kv[:, :width].astype(jnp.float32) * scales[:, 2 * width:3 * width]
    k_s[...] = keys.astype(jnp.bfloat16)
    kt_s[...] = keys.T.astype(jnp.bfloat16)
    v_s[...] = (kv[:, width:].astype(jnp.float32) * scales[:, 3 * width:]).astype(jnp.bfloat16)
    sub = block // tile
    for index in range(seq // block):
        first = index * block
        q_b = q_s[first:first + block, :]
        do_b = do_s[first:first + block, :]
        tiles = []
        for t in range((index + 1) * sub):
            low = max(0, t - index * sub) * tile
            tiles.append((t, low))
        peak = jnp.full((8, block), -jnp.inf, jnp.float32)
        for t, low in tiles:
            ks = slice(t * tile, (t + 1) * tile)
            s = lax.dot_general(k_s[ks, :], q_b[low:], NT, preferred_element_type=jnp.float32)
            if t >= index * sub:
                key = lax.broadcasted_iota(jnp.int32, (tile, tile), 0)
                row = lax.broadcasted_iota(jnp.int32, (tile, tile), 1)
                head = jnp.where(key <= row, s[:, :tile], -jnp.inf)
                s = jnp.concatenate([head, s[:, tile:]], axis=1) if low + tile < block else head
            s_s[ks, low:] = s
            top = fold(s, jnp.maximum)
            if low:
                peak = jnp.concatenate([peak[:, :low], jnp.maximum(peak[:, low:], top)], axis=1)
            else:
                peak = jnp.maximum(peak, top)
            dp_s[ks, low:] = lax.dot_general(v_s[ks, :], do_b[low:], NT, preferred_element_type=jnp.float32)
        peak = jnp.max(peak, axis=0, keepdims=True)
        total = jnp.zeros((8, block), jnp.float32)
        inner = jnp.zeros((8, block), jnp.float32)
        for t, low in tiles:
            ks = slice(t * tile, (t + 1) * tile)
            e = jnp.exp2((s_s[ks, low:] - peak[:, low:]) * coef)
            s_s[ks, low:] = e
            a = fold(e, jnp.add)
            b = fold(e * dp_s[ks, low:], jnp.add)
            if low:
                total = jnp.concatenate([total[:, :low], total[:, low:] + a], axis=1)
                inner = jnp.concatenate([inner[:, :low], inner[:, low:] + b], axis=1)
            else:
                total = total + a
                inner = inner + b
        norm = 1.0 / jnp.sum(total, axis=0, keepdims=True)
        delta = jnp.sum(inner, axis=0, keepdims=True) * norm
        for t, low in tiles:
            ks = slice(t * tile, (t + 1) * tile)
            p = s_s[ks, low:] * norm[:, low:]
            pb = p.astype(jnp.bfloat16)
            ds = (p * (dp_s[ks, low:] - delta[:, low:])).astype(jnp.bfloat16)
            if low:
                ds_s[ks, :low] = jnp.zeros((tile, low), jnp.bfloat16)
            ds_s[ks, low:] = ds
            dv = lax.dot_general(pb, do_b[low:], NN, preferred_element_type=jnp.float32)
            dk = lax.dot_general(ds, q_b[low:], NN, preferred_element_type=jnp.float32)
            if t >= index * sub:
                dv_s[ks, :] = dv
                dk_s[ks, :] = dk
            else:
                dv_s[ks, :] += dv
                dk_s[ks, :] += dk
        upper = first + block
        dq = lax.dot_general(kt_s[:, :upper], ds_s[:upper, :], NN, preferred_element_type=jnp.float32)
        dq = ((dq * scale).T).astype(jnp.bfloat16)
        place(out, first, 0, dq)
    for first in range(0, seq, 512):
        rows_ = slice(first, first + 512)
        place(out, first, width, (dk_s[rows_, :] * scale).astype(jnp.bfloat16))
        place(out, first, 2 * width, dv_s[rows_, :].astype(jnp.bfloat16))


def place(out, first, col, value):
    dests, room, _ = out.shape
    piece = room // 2
    for j in range(value.shape[0] // piece):
        h = first // piece + j
        y, z, c = h // 4, (h // 2) % 2, h % 2
        out[y * 2 + c, z * piece:(z + 1) * piece, col:col + value.shape[1]] = value[j * piece:(j + 1) * piece]


def attention(query, q_exp, kv, kv_exp, grad, grad_exp, block=512, tile=256):
    seq, width = query.shape
    f32, b16 = jnp.float32, jnp.bfloat16
    return pl.pallas_call(
        functools.partial(attention_kernel, block=block, tile=tile),
        out_shape=jax.ShapeDtypeStruct((8, seq // 8, 3 * width), b16),
        in_specs=[VM] * 6,
        out_specs=VM,
        scratch_shapes=[
            pltpu.VMEM((seq, width), b16),
            pltpu.VMEM((seq, width), b16),
            pltpu.VMEM((seq, width), b16),
            pltpu.VMEM((seq, width), b16),
            pltpu.VMEM((width, seq), b16),
            pltpu.VMEM((seq, block), f32),
            pltpu.VMEM((seq, block), f32),
            pltpu.VMEM((seq, block), b16),
            pltpu.VMEM((seq, width), f32),
            pltpu.VMEM((seq, width), f32),
        ],
        compiler_params=pltpu.CompilerParams(vmem_limit_bytes=32 * 2**20),
        cost_estimate=pl.CostEstimate(
            flops=3 * 10**9, bytes_accessed=6 * 2**20, transcendentals=2 * 10**6
        ),
        name="attention",
    )(query, q_exp, kv, kv_exp, grad, grad_exp)


def scaled(mantissa, exps):
    rows, cols = mantissa.shape
    blocks = mantissa.astype(jnp.float32).reshape(rows // 32, 32, cols)
    return (blocks * power(exps)[:, None, :]).reshape(rows, cols).astype(jnp.bfloat16)


def weights_kernel(wq, wq_exp, wkv, wkv_exp, q_out, kv_out):
    q_out[...] = scaled(wq[...], wq_exp[...])
    kv_out[...] = scaled(wkv[...], wkv_exp[...])


def weights(wq, wq_exp, wkv, wkv_exp):
    return pl.pallas_call(
        weights_kernel,
        out_shape=[
            jax.ShapeDtypeStruct(wq.shape, jnp.bfloat16),
            jax.ShapeDtypeStruct(wkv.shape, jnp.bfloat16),
        ],
        in_specs=[VM] * 4,
        out_specs=[VM] * 2,
        compiler_params=pltpu.CompilerParams(vmem_limit_bytes=16 * 2**20),
        name="weights",
    )(wq, wq_exp, wkv, wkv_exp)


def project_kernel(moved, wq, wkv, out, kv_out, sum_s):
    sources, tokens, lanes = moved.shape
    width = lanes // 3

    @pl.when(pl.program_id(0) == 0)
    def _():
        total = moved[0, :, width:].astype(jnp.float32)
        for s in range(1, sources):
            total = total + moved[s, :, width:].astype(jnp.float32)
        sum_s[...] = total.astype(jnp.bfloat16)
        kv_out[...] = sum_s[...]

    piece = wkv.shape[1] // 2
    parts = []
    for z in range(2):
        for c in range(2):
            rows = wkv[c, z * piece:(z + 1) * piece, :]
            parts.append(
                lax.dot_general(sum_s[...], rows, NT, preferred_element_type=jnp.float32)
            )
    acc = jnp.concatenate(parts, axis=1)
    for s in range(0, sources, 2):
        left = jnp.concatenate([moved[s, :, :width], moved[s + 1, :, :width]], axis=1)
        right = jnp.concatenate([wq[s], wq[s + 1]], axis=1)
        acc = acc + lax.dot_general(left, right, NT, preferred_element_type=jnp.float32)
    out[0] = acc.astype(jnp.bfloat16)


def project(moved, wq, wkv):
    sources, tokens, lanes = moved.shape
    model = wq.shape[1]
    groups = 4
    part = model // groups
    return pl.pallas_call(
        project_kernel,
        grid=(groups,),
        out_shape=[
            jax.ShapeDtypeStruct((groups, tokens, part), jnp.bfloat16),
            jax.ShapeDtypeStruct((tokens, lanes * 2 // 3), jnp.bfloat16),
        ],
        in_specs=[
            pl.BlockSpec((sources, tokens, lanes), lambda j: (0, 0, 0)),
            pl.BlockSpec((sources, part, lanes // 3), lambda j: (0, j, 0)),
            pl.BlockSpec((2, wkv.shape[1], wkv.shape[2]), lambda j: (j, 0, 0)),
        ],
        out_specs=[
            pl.BlockSpec((1, tokens, part), lambda j: (j, 0, 0)),
            pl.BlockSpec((tokens, lanes * 2 // 3), lambda j: (0, 0)),
        ],
        scratch_shapes=[pltpu.VMEM((tokens, lanes * 2 // 3), jnp.bfloat16)],
        compiler_params=pltpu.CompilerParams(vmem_limit_bytes=32 * 2**20),
        cost_estimate=pl.CostEstimate(
            flops=2 * tokens * model * (sources + 2) * 128,
            bytes_accessed=8 * 2**20,
            transcendentals=0,
        ),
        name="project",
    )(moved, wq, wkv)


def gather_kernel(half, terms, kv_sum, mine, other):
    sources, tokens, part = terms.shape
    piece = tokens // 2
    z = half[0]
    for ref, at in ((mine, z), (other, 1 - z)):
        rows = pl.ds(pl.multiple_of(at * piece, piece), piece)
        total = terms[0, rows, :].astype(jnp.float32)
        for s in range(1, sources):
            total = total + terms[s, rows, :].astype(jnp.float32)
        ref[:, :part] = total.astype(ref.dtype)
        ref[:, part:] = kv_sum[rows, :].astype(ref.dtype)


def gather(half, terms, kv_sum):
    sources, tokens, part = terms.shape
    cols = part + kv_sum.shape[1]
    return pl.pallas_call(
        gather_kernel,
        out_shape=[
            jax.ShapeDtypeStruct((tokens // 2, cols), jnp.float32),
            jax.ShapeDtypeStruct((tokens // 2, cols), jnp.bfloat16),
        ],
        in_specs=[pl.BlockSpec(memory_space=pltpu.SMEM), VM, VM],
        out_specs=[VM] * 2,
        compiler_params=pltpu.CompilerParams(vmem_limit_bytes=16 * 2**20),
        name="gather",
    )(half, terms, kv_sum)


def shards(query, query_exp, kv, kv_exp, out_grad, out_grad_exp, q_weight, q_weight_exp, kv_weight, kv_weight_exp):
    swap = [(0, 1), (1, 0)]
    half = lax.axis_index("zh")
    wq, wkv = weights(q_weight, q_weight_exp, kv_weight, kv_weight_exp)
    wq_all = lax.all_gather(wq, ("y", "core"), axis=0)
    wkv_far = lax.ppermute(wkv, "zh", swap)
    low = jnp.where(half == 0, wkv, wkv_far)
    high = jnp.where(half == 0, wkv_far, wkv)
    both = jnp.concatenate([low, high], axis=0)
    wkv_all = lax.all_to_all(
        jnp.broadcast_to(both[None], (8,) + both.shape), ("y", "core"), 0, 0
    )
    grads = attention(query, query_exp, kv, kv_exp, out_grad, out_grad_exp)
    moved = lax.all_to_all(grads, ("y", "core"), 0, 0)
    terms, kv_sum = project(moved, wq_all, wkv_all)
    terms = lax.all_to_all(terms, "x", 0, 0)
    mine, other = gather(half.reshape(1).astype(jnp.int32), terms, kv_sum)
    far = lax.ppermute(other, "zh", swap)
    total = (mine + far.astype(jnp.float32)).astype(jnp.bfloat16)
    part = terms.shape[2]
    return total[:, :part], total[:, part:]


def solution(mesh):
    dp, group, head = (mesh.shape[a] for a in ("dp", "group", "head"))
    fine = Mesh(
        mesh.devices.reshape(dp, group, head // 4, 2, 2), ("dp", "x", "y", "zh", "core")
    )
    head_axes = ("y", "zh", "core")
    columns = P("dp", ("x",) + head_axes)
    exps = P(("x",) + head_axes, "dp")
    tokens = P(("dp",) + head_axes, "x")
    return jax.shard_map(
        shards,
        mesh=fine,
        in_specs=(columns, exps, P("dp", "x"), P("x", "dp"), columns, exps, columns, columns, tokens, tokens),
        out_specs=(tokens, tokens),
        check_vma=False,
    )
```

time: 349 us -> 148 us (0.42)
  the two profiles are of different devices: /device:TPU:8 before, /device:TPU:2 now
where the time goes in v1:
time: 148 us; the launch traced here: 147 us
  blocking collectives  43.2 us (29%)
  starting transfers between devices  33.4 us (23%)
  waiting for transfers between devices  33.1 us (22%)
  between operations  14.2 us (10%)
  Pallas kernels  14.1 us (10%)
  local copies, waits for them, and re-layouts  9.09 us (6%)
    all_to_all x1, blocking collectives, shards(): moved = lax.all_to_all(grads, ('y', 'core'), 0, 0)  25.3 us
    all_to_all x1, blocking collectives, shards(): terms = lax.all_to_all(terms, 'x', 0, 0)  17.9 us
    all_to_all x1, waiting for transfers between devices, shards(): lax.all_to_all(jnp.broadcast_to(both[None], (8,) + both.shape), ('y', 'co...  16.1 us
    ppermute x1, starting transfers between devices, shards(): wkv_far = lax.ppermute(wkv, 'zh', swap)  15.7 us
    ppermute x1, starting transfers between devices, shards(): far = lax.ppermute(other, 'zh', swap)  13.1 us
    ppermute x1, waiting for transfers between devices, shards(): far = lax.ppermute(other, 'zh', swap)  12.8 us
    pallas_call x1, Pallas kernels, attention(): pl.pallas_call(functools.partial(attention_kernel, block=block, tile=tile...  10.2 us
    unnamed x24, local copies, waits for them, and re-layouts  6.73 us
  transfers between devices with their start and end apart: 4, of which 3 were waited for; matrix products, arithmetic and copies ran while one was open for 1% of the time, Pallas kernels for 7%

profile of v1, /device:TPU:2, one launch (start us, length us, event | category | flops | bytes accessed | tf_op | source)
XLA Modules:
  0.0 147.2 jit_solution(11441511440257370273)
XLA Ops:
  7.2 0.0 all-gather.3.cloned.1.call-start
  7.2 0.0 copy-start.2
  7.2 1.0 copy-done.2
  8.3 0.0 copy-start.3
  8.3 0.8 copy-done.3
  9.1 0.0 copy-start.4
  9.1 0.8 copy-done.4
  9.9 0.0 copy-start.5
  9.9 0.7 copy-done.5
  10.5 0.9 weights.1
  11.5 0.0 all-gather.3.cloned.1.call-update
  11.5 15.7 %collective-permute-start = (bf16[128,256]{1,0:T(8,128)(2,1)S(1)}, bf16[128,256]{1,0:T(8,128)(2,1)S(1)}, u32[]{:S(2)}, u32[]{:S(2)}) collective-permute-start(bf16[128,256]{1,0:T(8,128)(2,1)S(1)} %get-tuple-element.9), channel_id=1, source_target_pairs={{0,2},{2,0},{1,3},{3,1},{4,6},{6,4},{5,7},{7,5},{8,10},{10,8},{9,1... | collective-permute-start | bytes 196616 | tf_op jit(solution)/shard_map/ppermute | solution.py:266
  27.2 4.2 %collective-permute-done = bf16[128,256]{1,0:T(8,128)(2,1)S(1)} collective-permute-done((bf16[128,256]{1,0:T(8,128)(2,1)S(1)}, bf16[128,256]{1,0:T(8,128)(2,1)S(1)}, u32[]{:S(2)}, u32[]{:S(2)}) %collective-permute-start) | collective-permute-done | bytes 65568 | tf_op jit(solution)/shard_map/ppermute | solution.py:266
  31.4 0.0 copy-start.6
  31.5 0.0 copy-start.7
  31.5 0.0 copy-start.8
  31.5 0.0 copy-start.9
  31.5 0.0 copy-start.10
  31.5 0.0 copy-start.11
  31.5 1.1 broadcast_in_dim.2
  32.6 4.6 %all-to-all-start.1 = ((bf16[8,256,256]{2,1,0:T(8,128)(2,1)}), bf16[8,256,256]{2,1,0:T(8,128)(2,1)S(1)}, u32[]{:S(2)}, u32[]{:S(2)}) async-start(bf16[8,256,256]{2,1,0:T(8,128)(2,1)} %broadcast_in_dim.2), calls=%async_computation.1 | async-start | bytes 2097152 | tf_op jit(solution)/shard_map/all_to_all | solution.py:270
  37.2 0.0 copy-done.6
  37.2 0.0 copy-done.7
  37.2 0.0 copy-done.8
  37.2 0.0 copy-done.9
  37.2 0.0 copy-done.10
  37.2 0.0 copy-done.11
  37.3 10.2 %attention.1 = bf16[8,256,384]{2,1,0:T(8,128)(2,1)S(1)} custom-call(bf16[2048,128]{1,0:T(8,128)(2,1)S(1)} %copy-done.7, s32[4,2048]{1,0:T(4,128)S(1)} %copy-done.10, bf16[2048,256]{1,0:T(8,128)(2,1)S(1)} %copy-done.6, s32[8,2048]{1,0:T(8,128)S(1)} %copy-done.9, bf16[2048,128]{1,0:T(8,128)(2,1)S(1)} %copy-done.8, s32[4,2048]{1,0:T(4,128)S(1)} %copy-done.11), custom_call_target="tpu_custom_call" | custom-call | flops 3000000000 | bytes 6291456 | tf_op jit(solution)/shard_map/attention/pallas_call | solution.py:122
  47.5 0.0 copy-start.1
  47.5 1.2 copy-done.1
  48.7 16.1 %all-to-all-done.1.wkv = bf16[8,256,256]{2,1,0:T(8,128)(2,1)S(1)} async-done(((bf16[8,256,256]{2,1,0:T(8,128)(2,1)}), bf16[8,256,256]{2,1,0:T(8,128)(2,1)S(1)}, u32[]{:S(2)}, u32[]{:S(2)}) %all-to-all-start.1) | async-done | bytes 1048608 | tf_op jit(solution)/shard_map/all_to_all | solution.py:270
  64.7 25.3 %all_to_all.15.moved = bf16[8,256,384]{2,1,0:T(8,128)(2,1)S(1)} all-to-all(bf16[8,256,384]{2,1,0:T(8,128)(2,1)} %copy-done.1), channel_id=1, replica_groups=mesh['dp'=8,'x'=4,'y'=4,'zh'=2,'core'=2] {'y','core'}, dimensions={0} | all-to-all | bytes 3145728 | tf_op jit(solution)/shard_map/all_to_all | solution.py:274
  90.0 0.0 all-gather.3.cloned.1.call-done
  90.0 0.0 copy-start
  90.0 2.2 %copy-done = bf16[16384,128]{1,0:T(8,128)(2,1)S(1)} copy-done((bf16[16384,128]{1,0:T(8,128)(2,1)S(1)}, bf16[16384,128]{1,0:T(8,128)(2,1)}, u32[]{:S(2)}) %copy-start) | copy-done | bytes 4194328
  92.2 2.8 %project.1 = (bf16[4,256,512]{2,1,0:T(8,128)(2,1)S(1)}, bf16[256,256]{1,0:T(8,128)(2,1)S(1)}) custom-call(bf16[8,256,384]{2,1,0:T(8,128)(2,1)S(1)} %all_to_all.15.moved, bf16[8,2048,128]{2,1,0:T(8,128)(2,1)S(1)} %bitcast.2, bf16[8,256,256]{2,1,0:T(8,128)(2,1)S(1)} %all-to-all-done.1.wkv), custom_call_target="tpu_custom_call" | custom-call | flops 1342177280 | bytes 8388608 | tf_op jit(solution)/shard_map/project/pallas_call | solution.py:205
  95.0 17.9 %all_to_all.16.terms = bf16[4,256,512]{2,1,0:T(8,128)(2,1)S(1)} all-to-all(bf16[4,256,512]{2,1,0:T(8,128)(2,1)S(1)} %get-tuple-element.10), channel_id=1, replica_groups=mesh['dp'=8,'x'=4,'y'=4,'zh'=2,'core'=2] {'x'}, dimensions={0} | all-to-all | bytes 2097152 | tf_op jit(solution)/shard_map/all_to_all | solution.py:276
  112.9 0.1 gather.1
  113.1 13.1 %collective-permute-start.1 = (bf16[128,768]{1,0:T(8,128)(2,1)S(1)}, bf16[128,768]{1,0:T(8,128)(2,1)S(1)}, u32[]{:S(2)}, u32[]{:S(2)}) collective-permute-start(bf16[128,768]{1,0:T(8,128)(2,1)S(1)} %get-tuple-element.13), channel_id=1, source_target_pairs={{0,2},{2,0},{1,3},{3,1},{4,6},{6,4},{5,7},{7,5},{8,10},{10,8},{9,1... | collective-permute-start | bytes 589832 | tf_op jit(solution)/shard_map/ppermute | solution.py:278
  126.2 12.8 %collective-permute-done.1 = bf16[128,768]{1,0:T(8,128)(2,1)S(1)} collective-permute-done((bf16[128,768]{1,0:T(8,128)(2,1)S(1)}, bf16[128,768]{1,0:T(8,128)(2,1)S(1)}, u32[]{:S(2)}, u32[]{:S(2)}) %collective-permute-start.1) | collective-permute-done | bytes 196640 | tf_op jit(solution)/shard_map/ppermute | solution.py:278
  139.0 0.7 slice.8
  139.7 0.6 slice.9
  (3 shorter events, 0.1 us)
Async XLA Ops:
  7.2 82.8 %all-gather.3.cloned.1.call-start = ((), (), s32[]{:S(2)}) async-start(), calls=%async_computation.3 | async-start | bytes 4718592 | tf_op jit(solution)/shard_map/all_gather | solution.py:265
  7.2 1.0 copy-start.2
  8.3 0.8 copy-start.3
  9.1 0.8 copy-start.4
  9.9 0.7 copy-start.5
  11.5 19.9 %collective-permute-start = (bf16[128,256]{1,0:T(8,128)(2,1)S(1)}, bf16[128,256]{1,0:T(8,128)(2,1)S(1)}, u32[]{:S(2)}, u32[]{:S(2)}) collective-permute-start(bf16[128,256]{1,0:T(8,128)(2,1)S(1)} %get-tuple-element.9), channel_id=1, source_target_pairs={{0,2},{2,0},{1,3},{3,1},{4,6},{6,4},{5,7},{7,5},{8,10},{10,8},{9,1... | collective-permute-start | bytes 196616 | tf_op jit(solution)/shard_map/ppermute | solution.py:266
  31.4 5.7 %copy-start.6 = (bf16[2048,256]{1,0:T(8,128)(2,1)S(1)}, bf16[2048,256]{1,0:T(8,128)(2,1)}, u32[]{:S(2)}) copy-start(bf16[2048,256]{1,0:T(8,128)(2,1)} %kv.1) | copy-start | bytes 3145732
  31.5 5.7 %copy-start.7 = (bf16[2048,128]{1,0:T(8,128)(2,1)S(1)}, bf16[2048,128]{1,0:T(8,128)(2,1)}, u32[]{:S(2)}) copy-start(bf16[2048,128]{1,0:T(8,128)(2,1)} %query.1) | copy-start | bytes 1572868
  31.5 5.7 %copy-start.8 = (bf16[2048,128]{1,0:T(8,128)(2,1)S(1)}, bf16[2048,128]{1,0:T(8,128)(2,1)}, u32[]{:S(2)}) copy-start(bf16[2048,128]{1,0:T(8,128)(2,1)} %grad.1) | copy-start | bytes 1572868
  31.5 5.7 %copy-start.9 = (s32[8,2048]{1,0:T(8,128)S(1)}, s32[8,2048]{1,0:T(8,128)}, u32[]{:S(2)}) copy-start(s32[8,2048]{1,0:T(8,128)} %kv_exp.1) | copy-start | bytes 196612
  31.5 5.7 %copy-start.10 = (s32[4,2048]{1,0:T(4,128)S(1)}, s32[4,2048]{1,0:T(4,128)}, u32[]{:S(2)}) copy-start(s32[4,2048]{1,0:T(4,128)} %q_exp.1) | copy-start | bytes 98308
  31.5 5.7 %copy-start.11 = (s32[4,2048]{1,0:T(4,128)S(1)}, s32[4,2048]{1,0:T(4,128)}, u32[]{:S(2)}) copy-start(s32[4,2048]{1,0:T(4,128)} %grad_exp.1) | copy-start | bytes 98308
  32.6 32.1 %all-to-all-start.1 = ((bf16[8,256,256]{2,1,0:T(8,128)(2,1)}), bf16[8,256,256]{2,1,0:T(8,128)(2,1)S(1)}, u32[]{:S(2)}, u32[]{:S(2)}) async-start(bf16[8,256,256]{2,1,0:T(8,128)(2,1)} %broadcast_in_dim.2), calls=%async_computation.1 | async-start | bytes 2097152 | tf_op jit(solution)/shard_map/all_to_all | solution.py:270
  47.5 1.2 copy-start.1
  90.0 2.2 %copy-start = (bf16[16384,128]{1,0:T(8,128)(2,1)S(1)}, bf16[16384,128]{1,0:T(8,128)(2,1)}, u32[]{:S(2)}) copy-start(bf16[16384,128]{1,0:T(8,128)(2,1)} %all-gather.3.cloned.1.call-done) | copy-start | bytes 12582916
  113.1 25.9 %collective-permute-start.1 = (bf16[128,768]{1,0:T(8,128)(2,1)S(1)}, bf16[128,768]{1,0:T(8,128)(2,1)S(1)}, u32[]{:S(2)}, u32[]{:S(2)}) collective-permute-start(bf16[128,768]{1,0:T(8,128)(2,1)S(1)} %get-tuple-element.13), channel_id=1, source_target_pairs={{0,2},{2,0},{1,3},{3,1},{4,6},{6,4},{5,7},{7,5},{8,10},{10,8},{9,1... | collective-permute-start | bytes 589832 | tf_op jit(solution)/shard_map/ppermute | solution.py:278
Sparse Core Ops, SparseCore 0:
  11.6 55.4 all-gather.2

commit v2 on v1

--- a/solution.py
+++ b/solution.py
@@ -6,6 +6,8 @@
 from jax.sharding import Mesh, PartitionSpec as P
 
 VM = pl.BlockSpec(memory_space=pltpu.VMEM)
+SM = pl.BlockSpec(memory_space=pltpu.SMEM)
+BIG = 56 * 2**20
 NT = (((1,), (1,)), ((), ()))
 NN = (((1,), (0,)), ((), ()))
 
@@ -22,7 +24,7 @@
     return x
 
 
-def attention_kernel(query, q_exp, kv, kv_exp, grad, grad_exp, out, q_s, k_s, v_s, do_s, kt_s, s_s, dp_s, ds_s, dk_s, dv_s, *, block, tile):
+def attention_kernel(half, query, q_exp, kv, kv_exp, grad, grad_exp, other, own, out, sems, q_s, k_s, v_s, do_s, kt_s, s_s, dp_s, ds_s, dk_s, dv_s, *, block, tile):
     seq, width = query.shape
     scale = 1.0 / math.sqrt(width)
     coef = scale * math.log2(math.e)
@@ -105,26 +107,37 @@
         rows_ = slice(first, first + 512)
         place(out, first, width, (dk_s[rows_, :] * scale).astype(jnp.bfloat16))
         place(out, first, 2 * width, dv_s[rows_, :].astype(jnp.bfloat16))
+    z = half[0]
+    copies = [
+        pltpu.make_async_copy(out.at[1 - z], other, sems.at[0]),
+        pltpu.make_async_copy(out.at[z], own, sems.at[1]),
+    ]
+    for copy in copies:
+        copy.start()
+    for copy in copies:
+        copy.wait()
 
 
 def place(out, first, col, value):
-    dests, room, _ = out.shape
-    piece = room // 2
+    piece = out.shape[2]
     for j in range(value.shape[0] // piece):
         h = first // piece + j
         y, z, c = h // 4, (h // 2) % 2, h % 2
-        out[y * 2 + c, z * piece:(z + 1) * piece, col:col + value.shape[1]] = value[j * piece:(j + 1) * piece]
-
-
-def attention(query, q_exp, kv, kv_exp, grad, grad_exp, block=512, tile=256):
+        out[z, y * 2 + c, :, col:col + value.shape[1]] = value[j * piece:(j + 1) * piece]
+
+
+def attention(half, query, q_exp, kv, kv_exp, grad, grad_exp, block=512, tile=256):
     seq, width = query.shape
     f32, b16 = jnp.float32, jnp.bfloat16
+    sent = (8, seq // 16, 3 * width)
     return pl.pallas_call(
         functools.partial(attention_kernel, block=block, tile=tile),
-        out_shape=jax.ShapeDtypeStruct((8, seq // 8, 3 * width), b16),
-        in_specs=[VM] * 6,
-        out_specs=VM,
+        out_shape=[jax.ShapeDtypeStruct(sent, b16)] * 2,
+        in_specs=[SM] + [VM] * 6,
+        out_specs=[pl.BlockSpec(memory_space=pltpu.HBM)] * 2,
         scratch_shapes=[
+            pltpu.VMEM((2,) + sent, b16),
+            pltpu.SemaphoreType.DMA((2,)),
             pltpu.VMEM((seq, width), b16),
             pltpu.VMEM((seq, width), b16),
             pltpu.VMEM((seq, width), b16),
@@ -141,7 +154,7 @@
             flops=3 * 10**9, bytes_accessed=6 * 2**20, transcendentals=2 * 10**6
         ),
         name="attention",
-    )(query, q_exp, kv, kv_exp, grad, grad_exp)
+    )(half, query, q_exp, kv, kv_exp, grad, grad_exp)
 
 
 def scaled(mantissa, exps):
@@ -152,24 +165,34 @@
 
 def weights_kernel(wq, wq_exp, wkv, wkv_exp, q_out, kv_out):
     q_out[...] = scaled(wq[...], wq_exp[...])
-    kv_out[...] = scaled(wkv[...], wkv_exp[...])
-
-
-def weights(wq, wq_exp, wkv, wkv_exp):
+
+    @pl.when(pl.program_id(0) == 0)
+    def _():
+        kv_out[...] = scaled(wkv[...], wkv_exp[...])
+
+
+def weights(wq, wq_exp, wkv, wkv_exp, steps=4):
+    def stream(a):
+        return pl.BlockSpec((a.shape[0] // steps, a.shape[1]), lambda i: (i, 0))
+
+    def whole(a):
+        return pl.BlockSpec(a.shape, lambda i: (0, 0))
+
     return pl.pallas_call(
         weights_kernel,
+        grid=(steps,),
         out_shape=[
             jax.ShapeDtypeStruct(wq.shape, jnp.bfloat16),
             jax.ShapeDtypeStruct(wkv.shape, jnp.bfloat16),
         ],
-        in_specs=[VM] * 4,
-        out_specs=[VM] * 2,
-        compiler_params=pltpu.CompilerParams(vmem_limit_bytes=16 * 2**20),
+        in_specs=[stream(wq), stream(wq_exp), whole(wkv), whole(wkv_exp)],
+        out_specs=[stream(wq), whole(wkv)],
+        compiler_params=pltpu.CompilerParams(vmem_limit_bytes=BIG),
         name="weights",
     )(wq, wq_exp, wkv, wkv_exp)
 
 
-def project_kernel(moved, wq, wkv, out, kv_out, sum_s):
+def project_kernel(core, moved, wq, wkv, wkv_far, out, kv_out, sum_s):
     sources, tokens, lanes = moved.shape
     width = lanes // 3
 
@@ -182,13 +205,13 @@
         kv_out[...] = sum_s[...]
 
     piece = wkv.shape[1] // 2
+    first = core[0] == 0
     parts = []
     for z in range(2):
-        for c in range(2):
-            rows = wkv[c, z * piece:(z + 1) * piece, :]
-            parts.append(
-                lax.dot_general(sum_s[...], rows, NT, preferred_element_type=jnp.float32)
-            )
+        rows = slice(z * piece, (z + 1) * piece)
+        near = lax.dot_general(sum_s[...], wkv[0, rows, :], NT, preferred_element_type=jnp.float32)
+        far = lax.dot_general(sum_s[...], wkv_far[0, rows, :], NT, preferred_element_type=jnp.float32)
+        parts += [jnp.where(first, near, far), jnp.where(first, far, near)]
     acc = jnp.concatenate(parts, axis=1)
     for s in range(0, sources, 2):
         left = jnp.concatenate([moved[s, :, :width], moved[s + 1, :, :width]], axis=1)
@@ -197,88 +220,110 @@
     out[0] = acc.astype(jnp.bfloat16)
 
 
-def project(moved, wq, wkv):
+def project(core, moved, wq, wkv, wkv_far):
     sources, tokens, lanes = moved.shape
     model = wq.shape[1]
-    groups = 4
+    groups = wkv.shape[0]
     part = model // groups
+    kv_lanes = lanes * 2 // 3
+    kv_block = pl.BlockSpec((1,) + wkv.shape[1:], lambda j: (j, 0, 0))
     return pl.pallas_call(
         project_kernel,
         grid=(groups,),
         out_shape=[
             jax.ShapeDtypeStruct((groups, tokens, part), jnp.bfloat16),
-            jax.ShapeDtypeStruct((tokens, lanes * 2 // 3), jnp.bfloat16),
+            jax.ShapeDtypeStruct((tokens, kv_lanes), jnp.bfloat16),
         ],
         in_specs=[
+            SM,
             pl.BlockSpec((sources, tokens, lanes), lambda j: (0, 0, 0)),
             pl.BlockSpec((sources, part, lanes // 3), lambda j: (0, j, 0)),
-            pl.BlockSpec((2, wkv.shape[1], wkv.shape[2]), lambda j: (j, 0, 0)),
+            kv_block,
+            kv_block,
         ],
         out_specs=[
             pl.BlockSpec((1, tokens, part), lambda j: (j, 0, 0)),
-            pl.BlockSpec((tokens, lanes * 2 // 3), lambda j: (0, 0)),
-        ],
-        scratch_shapes=[pltpu.VMEM((tokens, lanes * 2 // 3), jnp.bfloat16)],
-        compiler_params=pltpu.CompilerParams(vmem_limit_bytes=32 * 2**20),
+            pl.BlockSpec((tokens, kv_lanes), lambda j: (0, 0)),
+        ],
+        scratch_shapes=[pltpu.VMEM((tokens, kv_lanes), jnp.bfloat16)],
+        compiler_params=pltpu.CompilerParams(vmem_limit_bytes=BIG),
         cost_estimate=pl.CostEstimate(
             flops=2 * tokens * model * (sources + 2) * 128,
             bytes_accessed=8 * 2**20,
             transcendentals=0,
         ),
         name="project",
-    )(moved, wq, wkv)
-
-
-def gather_kernel(half, terms, kv_sum, mine, other):
-    sources, tokens, part = terms.shape
-    piece = tokens // 2
-    z = half[0]
-    for ref, at in ((mine, z), (other, 1 - z)):
-        rows = pl.ds(pl.multiple_of(at * piece, piece), piece)
-        total = terms[0, rows, :].astype(jnp.float32)
-        for s in range(1, sources):
-            total = total + terms[s, rows, :].astype(jnp.float32)
-        ref[:, :part] = total.astype(ref.dtype)
-        ref[:, part:] = kv_sum[rows, :].astype(ref.dtype)
-
-
-def gather(half, terms, kv_sum):
-    sources, tokens, part = terms.shape
-    cols = part + kv_sum.shape[1]
+    )(core, moved, wq, wkv, wkv_far)
+
+
+def summed(terms):
+    total = terms[0].astype(jnp.float32)
+    for s in range(1, terms.shape[0]):
+        total = total + terms[s].astype(jnp.float32)
+    return total
+
+
+def gather_kernel(terms, kv_sum, out):
+    part = terms.shape[2]
+    out[:, :part] = summed(terms).astype(out.dtype)
+    out[:, part:] = kv_sum[...]
+
+
+def gather(terms, kv_sum):
+    cols = terms.shape[2] + kv_sum.shape[1]
     return pl.pallas_call(
         gather_kernel,
+        out_shape=jax.ShapeDtypeStruct((terms.shape[1], cols), jnp.bfloat16),
+        in_specs=[VM] * 2,
+        out_specs=VM,
+        compiler_params=pltpu.CompilerParams(vmem_limit_bytes=16 * 2**20),
+        name="gather",
+    )(terms, kv_sum)
+
+
+def finish_kernel(terms, kv_sum, far, out, kv_out):
+    part = terms.shape[2]
+    out[...] = (summed(terms) + far[:, :part].astype(jnp.float32)).astype(out.dtype)
+    kv = kv_sum[...].astype(jnp.float32) + far[:, part:].astype(jnp.float32)
+    kv_out[...] = kv.astype(kv_out.dtype)
+
+
+def finish(terms, kv_sum, far):
+    return pl.pallas_call(
+        finish_kernel,
         out_shape=[
-            jax.ShapeDtypeStruct((tokens // 2, cols), jnp.float32),
-            jax.ShapeDtypeStruct((tokens // 2, cols), jnp.bfloat16),
-        ],
-        in_specs=[pl.BlockSpec(memory_space=pltpu.SMEM), VM, VM],
+            jax.ShapeDtypeStruct(terms.shape[1:], jnp.bfloat16),
+            jax.ShapeDtypeStruct(kv_sum.shape, jnp.bfloat16),
+        ],
+        in_specs=[VM] * 3,
         out_specs=[VM] * 2,
         compiler_params=pltpu.CompilerParams(vmem_limit_bytes=16 * 2**20),
-        name="gather",
-    )(half, terms, kv_sum)
+        name="finish",
+    )(terms, kv_sum, far)
 
 
 def shards(query, query_exp, kv, kv_exp, out_grad, out_grad_exp, q_weight, q_weight_exp, kv_weight, kv_weight_exp):
     swap = [(0, 1), (1, 0)]
-    half = lax.axis_index("zh")
+    zh = lax.axis_index("zh")
+    half = zh.reshape(1).astype(jnp.int32)
+    core = lax.axis_index("core").reshape(1).astype(jnp.int32)
     wq, wkv = weights(q_weight, q_weight_exp, kv_weight, kv_weight_exp)
     wq_all = lax.all_gather(wq, ("y", "core"), axis=0)
-    wkv_far = lax.ppermute(wkv, "zh", swap)
-    low = jnp.where(half == 0, wkv, wkv_far)
-    high = jnp.where(half == 0, wkv_far, wkv)
+    wkv_z = lax.ppermute(wkv, "zh", swap)
+    low = jnp.where(zh == 0, wkv, wkv_z)
+    high = jnp.where(zh == 0, wkv_z, wkv)
     both = jnp.concatenate([low, high], axis=0)
-    wkv_all = lax.all_to_all(
-        jnp.broadcast_to(both[None], (8,) + both.shape), ("y", "core"), 0, 0
-    )
-    grads = attention(query, query_exp, kv, kv_exp, out_grad, out_grad_exp)
-    moved = lax.all_to_all(grads, ("y", "core"), 0, 0)
-    terms, kv_sum = project(moved, wq_all, wkv_all)
-    terms = lax.all_to_all(terms, "x", 0, 0)
-    mine, other = gather(half.reshape(1).astype(jnp.int32), terms, kv_sum)
-    far = lax.ppermute(other, "zh", swap)
-    total = (mine + far.astype(jnp.float32)).astype(jnp.bfloat16)
-    part = terms.shape[2]
-    return total[:, :part], total[:, part:]
+    wkv_near = lax.all_to_all(jnp.broadcast_to(both[None], (4,) + both.shape), "y", 0, 0)
+    other, own = attention(half, query, query_exp, kv, kv_exp, out_grad, out_grad_exp)
+    wkv_far = lax.ppermute(wkv_near, "core", swap)
+    other = lax.all_to_all(other, ("y", "core"), 0, 0)
+    own = lax.all_to_all(own, ("y", "core"), 0, 0)
+    terms_other, kv_other = project(core, other, wq_all, wkv_near, wkv_far)
+    terms_other = lax.all_to_all(terms_other, "x", 0, 0)
+    terms_own, kv_own = project(core, own, wq_all, wkv_near, wkv_far)
+    terms_own = lax.all_to_all(terms_own, "x", 0, 0)
+    far = lax.ppermute(gather(terms_other, kv_other), "zh", swap)
+    return tuple(finish(terms_own, kv_own, far))
 
 
 def solution(mesh):

time: 148 us -> 142 us (0.959)
  blocking collectives: 43.2 us -> 18 us
  starting transfers between devices: 33.4 us -> 48.8 us
  Pallas kernels: 14.1 us -> 26.1 us
  waiting for transfers between devices: 33.1 us -> 24.8 us
    all_to_all x2 -> x1, blocking collectives: 43.2 us -> 18 us  [shards(): other = lax.all_to_all(other, ('y', 'core'), 0, 0)]
    all_to_all x1 -> x4, starting transfers between devices: 4.6 us -> 17.7 us  [the longest x1 4.9 us: shards(): terms_own = lax.all_to_all(terms_own, 'x', 0, 0)]
    all_to_all x1 -> x4, waiting for transfers between devices: 16.1 us -> 5.42 us  [the longest x1 3.03 us: shards(): own = lax.all_to_all(own, ('y', 'core'), 0, 0)]
    pallas_call x1 -> x2, Pallas kernels: 2.84 us -> 10.8 us  [project(): pl.pallas_call(project_kernel, grid=(groups,), out_shape=[jax.ShapeDtypeS...]
    pallas_call x2 -> x3, Pallas kernels: 1.05 us -> 4.09 us  [the longest x1 3.26 us: weights(): pl.pallas_call(weights_kernel, grid=(steps,), out_shape=[jax.ShapeDtypeSt...]
    ppermute x2 -> x3, waiting for transfers between devices: 17 us -> 19.4 us  [the longest x1 13.4 us: shards(): far = lax.ppermute(gather(terms_other, kv_other), 'zh', swap)]
    ppermute x2 -> x3, starting transfers between devices: 28.8 us -> 31 us  [the longest x1 15.7 us: shards(): wkv_z = lax.ppermute(wkv, 'zh', swap)]
    unnamed x24 -> x22, local copies, waits for them, and re-layouts: 6.73 us -> 7.32 us
  transfers between devices with their start and end apart: 4 -> 8, of which waited for: 3 -> 5; matrix products, arithmetic and copies ran while one was open for 1% -> 1% of each run, Pallas kernels for 7% -> 16%
where the time goes in v2:
time: 142 us; the launch traced here: 141 us
  starting transfers between devices  48.8 us (34%)
  Pallas kernels  26.1 us (18%)
  waiting for transfers between devices  24.8 us (17%)
  blocking collectives  18 us (13%)
  between operations  14.1 us (10%)
  local copies, waits for them, and re-layouts  8.2 us (6%)
    all_to_all x1, blocking collectives, shards(): other = lax.all_to_all(other, ('y', 'core'), 0, 0)  18 us
    ppermute x1, starting transfers between devices, shards(): wkv_z = lax.ppermute(wkv, 'zh', swap)  15.7 us
    ppermute x1, waiting for transfers between devices, shards(): far = lax.ppermute(gather(terms_other, kv_other), 'zh', swap)  13.4 us
    ppermute x1, starting transfers between devices, shards(): far = lax.ppermute(gather(terms_other, kv_other), 'zh', swap)  13 us
    pallas_call x1, Pallas kernels, attention(): pl.pallas_call(functools.partial(attention_kernel, block=block, tile=tile...  11.2 us
    pallas_call x2, Pallas kernels, project(): pl.pallas_call(project_kernel, grid=(groups,), out_shape=[jax.ShapeDtypeS...  10.8 us
    unnamed x22, local copies, waits for them, and re-layouts  7.32 us
    all_to_all x1, starting transfers between devices, shards(): terms_own = lax.all_to_all(terms_own, 'x', 0, 0)  4.9 us
  transfers between devices with their start and end apart: 8, of which 5 were waited for; matrix products, arithmetic and copies ran while one was open for 1% of the time, Pallas kernels for 16%

profile of v2, /device:TPU:2, one launch (start us, length us, event | category | flops | bytes accessed | tf_op | source)
XLA Modules:
  0.0 140.9 jit_solution(14274438992666851631)
XLA Ops:
  7.2 0.0 all-gather.3.cloned.1.call-start
  7.2 3.3 %weights.1 = (bf16[2048,128]{1,0:T(8,128)(2,1)}, bf16[128,256]{1,0:T(8,128)(2,1)}) custom-call(bf16[2048,128]{1,0:T(8,128)(2,1)} %wq.1, s32[64,128]{1,0:T(8,128)} %wq_exp.1, bf16[128,256]{1,0:T(8,128)(2,1)} %wkv.1, s32[4,256]{1,0:T(4,128)} %wkv_exp.1), custom_call_target="tpu_custom_call" | custom-call | tf_op jit(solution)/shard_map/weights/pallas_call | solution.py:181
  10.5 0.0 all-gather.3.cloned.1.call-update
  10.5 15.7 %collective-permute-start = (bf16[128,256]{1,0:T(8,128)(2,1)}, bf16[128,256]{1,0:T(8,128)(2,1)S(1)}, u32[]{:S(2)}, u32[]{:S(2)}) collective-permute-start(bf16[128,256]{1,0:T(8,128)(2,1)} %get-tuple-element.12), channel_id=1, source_target_pairs={{0,2},{2,0},{1,3},{3,1},{4,6},{6,4},{5,7},{7,5},{8,10},{10,8},{9,1... | collective-permute-start | bytes 196616 | tf_op jit(solution)/shard_map/ppermute | solution.py:312
  26.2 4.5 %collective-permute-done = bf16[128,256]{1,0:T(8,128)(2,1)S(1)} collective-permute-done((bf16[128,256]{1,0:T(8,128)(2,1)}, bf16[128,256]{1,0:T(8,128)(2,1)S(1)}, u32[]{:S(2)}, u32[]{:S(2)}) %collective-permute-start) | collective-permute-done | bytes 65568 | tf_op jit(solution)/shard_map/ppermute | solution.py:312
  30.8 0.9 broadcast_select_fusion.1
  31.6 0.9 broadcast_in_dim.2
  32.5 4.5 %all-to-all-start.1 = ((bf16[4,256,256]{2,1,0:T(8,128)(2,1)}), bf16[4,256,256]{2,1,0:T(8,128)(2,1)S(1)}, u32[]{:S(2)}, u32[]{:S(2)}) async-start(bf16[4,256,256]{2,1,0:T(8,128)(2,1)} %broadcast_in_dim.2), calls=%async_computation.1 | async-start | bytes 1048576 | tf_op jit(solution)/shard_map/all_to_all | solution.py:316
  37.0 0.0 copy-start.2
  37.0 1.2 copy-done.2
  38.2 0.0 copy-start.3
  38.2 1.0 copy-done.3
  39.2 0.0 copy-start.4
  39.2 1.0 copy-done.4
  40.3 0.0 copy-start.5
  40.3 0.8 copy-done.5
  41.1 0.0 copy-start.6
  41.1 0.8 copy-done.6
  41.9 0.0 copy-start.7
  41.9 0.8 copy-done.7
  42.6 11.2 %attention.1 = (bf16[8,128,384]{2,1,0:T(8,128)(2,1)S(1)}, bf16[8,128,384]{2,1,0:T(8,128)(2,1)}) custom-call(s32[1]{0:T(128)} %bitcast.1.half, bf16[2048,128]{1,0:T(8,128)(2,1)S(1)} %copy-done.3, s32[4,2048]{1,0:T(4,128)S(1)} %copy-done.6, bf16[2048,256]{1,0:T(8,128)(2,1)S(1)} %copy-done.2, s32[8,2048]{1,0:T(8,128)S(1)} %copy-done.5, ...), custom_call_target="tpu_custom_call" | custom-call | flops 3000000000 | bytes 6291456 | tf_op jit(solution)/shard_map/attention/pallas_call | solution.py:133
  53.8 0.0 all-to-all-done.1.wkv
  53.8 0.0 copy-start.8
  53.8 18.0 %all_to_all.25.moved = bf16[8,128,384]{2,1,0:T(8,128)(2,1)} all-to-all(bf16[8,128,384]{2,1,0:T(8,128)(2,1)S(1)} %get-tuple-element.15), channel_id=1, replica_groups=mesh['dp'=8,'x'=4,'y'=4,'zh'=2,'core'=2] {'y','core'}, dimensions={0} | all-to-all | bytes 1572864 | tf_op jit(solution)/shard_map/all_to_all | solution.py:319
  71.8 3.5 %all-to-all-start = ((bf16[8,128,384]{2,1,0:T(8,128)(2,1)}), bf16[8,128,384]{2,1,0:T(8,128)(2,1)S(1)}, u32[]{:S(2)}, u32[]{:S(2)}) async-start(bf16[8,128,384]{2,1,0:T(8,128)(2,1)} %get-tuple-element.10), calls=%async_computation | async-start | bytes 1572864 | tf_op jit(solution)/shard_map/all_to_all | solution.py:320
  75.4 2.3 %collective-permute-start.1 = (bf16[4,256,256]{2,1,0:T(8,128)(2,1)S(1)}, bf16[4,256,256]{2,1,0:T(8,128)(2,1)S(1)}, u32[]{:S(2)}, u32[]{:S(2)}) collective-permute-start(bf16[4,256,256]{2,1,0:T(8,128)(2,1)S(1)} %all-to-all-done.1.wkv), channel_id=1, source_target_pairs={{0,1},{1,0},{2,3},{3,2},{4,5},{5,4},{6,7},{7,6},{8,9},{9,8},{10,11... | collective-permute-start | bytes 1572872 | tf_op jit(solution)/shard_map/ppermute | solution.py:318
  77.7 1.5 %collective-permute-done.1.wkv_far = bf16[4,256,256]{2,1,0:T(8,128)(2,1)S(1)} collective-permute-done((bf16[4,256,256]{2,1,0:T(8,128)(2,1)S(1)}, bf16[4,256,256]{2,1,0:T(8,128)(2,1)S(1)}, u32[]{:S(2)}, u32[]{:S(2)}) %collective-permute-start.1) | collective-permute-done | bytes 524320 | tf_op jit(solution)/shard_map/ppermute | solution.py:318
  79.2 0.0 copy-start.10
  79.2 0.0 all-gather.3.cloned.1.call-done
  79.2 0.0 copy-done.8
  79.2 0.8 copy-done.10
  80.0 5.4 %project.3 = (bf16[4,128,512]{2,1,0:T(8,128)(2,1)}, bf16[128,256]{1,0:T(8,128)(2,1)}) custom-call(s32[1]{0:T(128)} %bitcast.core, bf16[8,128,384]{2,1,0:T(8,128)(2,1)} %all_to_all.25.moved, bf16[8,2048,128]{2,1,0:T(8,128)(2,1)} %bitcast.3, bf16[4,256,256]{2,1,0:T(8,128)(2,1)} %copy-done.8, bf16[4,256,256]{2,1,0:T(8,128)(2,1)} %copy-done.10), custom_call_target="tpu_custom_call" | custom-call | flops 671088640 | bytes 8388608 | tf_op jit(solution)/shard_map/project/pallas_call | solution.py:230
  85.4 0.0 copy-start.1
  85.4 3.0 %all-to-all-done.moved = bf16[8,128,384]{2,1,0:T(8,128)(2,1)S(1)} async-done(((bf16[8,128,384]{2,1,0:T(8,128)(2,1)}), bf16[8,128,384]{2,1,0:T(8,128)(2,1)S(1)}, u32[]{:S(2)}, u32[]{:S(2)}) %all-to-all-start) | async-done | bytes 786464 | tf_op jit(solution)/shard_map/all_to_all | solution.py:320
  88.5 0.0 copy-start.9
  88.5 4.8 %all-to-all-start.4 = ((bf16[4,128,512]{2,1,0:T(8,128)(2,1)}), bf16[4,128,512]{2,1,0:T(8,128)(2,1)S(1)}, u32[]{:S(2)}, u32[]{:S(2)}) async-start(bf16[4,128,512]{2,1,0:T(8,128)(2,1)} %get-tuple-element.16), calls=%async_computation.4 | async-start | bytes 1048576 | tf_op jit(solution)/shard_map/all_to_all | solution.py:322
  93.3 0.0 copy-done.9
  93.3 5.4 %project.2 = (bf16[4,128,512]{2,1,0:T(8,128)(2,1)}, bf16[128,256]{1,0:T(8,128)(2,1)}) custom-call(s32[1]{0:T(128)} %bitcast.core, bf16[8,128,384]{2,1,0:T(8,128)(2,1)} %copy-done.9, bf16[8,2048,128]{2,1,0:T(8,128)(2,1)} %bitcast.4, bf16[4,256,256]{2,1,0:T(8,128)(2,1)} %copy-done.8, bf16[4,256,256]{2,1,0:T(8,128)(2,1)} %copy-done.10), custom_call_target="tpu_custom_call" | custom-call | flops 671088640 | bytes 8388608 | tf_op jit(solution)/shard_map/project/pallas_call | solution.py:230
  98.7 2.4 %all-to-all-done.4.terms = bf16[4,128,512]{2,1,0:T(8,128)(2,1)S(1)} async-done(((bf16[4,128,512]{2,1,0:T(8,128)(2,1)}), bf16[4,128,512]{2,1,0:T(8,128)(2,1)S(1)}, u32[]{:S(2)}, u32[]{:S(2)}) %all-to-all-start.4) | async-done | bytes 524320 | tf_op jit(solution)/shard_map/all_to_all | solution.py:322
  101.1 4.9 %all-to-all-start.2 = ((bf16[4,128,512]{2,1,0:T(8,128)(2,1)}), bf16[4,128,512]{2,1,0:T(8,128)(2,1)S(1)}, u32[]{:S(2)}, u32[]{:S(2)}) async-start(bf16[4,128,512]{2,1,0:T(8,128)(2,1)} %get-tuple-element.13), calls=%async_computation.2 | async-start | bytes 1048576 | tf_op jit(solution)/shard_map/all_to_all | solution.py:324
  106.0 0.0 copy-done.1
  106.0 0.1 gather.1
  106.1 13.0 %collective-permute-start.2 = (bf16[128,768]{1,0:T(8,128)(2,1)S(1)}, bf16[128,768]{1,0:T(8,128)(2,1)S(1)}, u32[]{:S(2)}, u32[]{:S(2)}) collective-permute-start(bf16[128,768]{1,0:T(8,128)(2,1)S(1)} %gather.1), channel_id=1, source_target_pairs={{0,2},{2,0},{1,3},{3,1},{4,6},{6,4},{5,7},{7,5},{8,10},{10,8},{9,1... | collective-permute-start | bytes 589832 | tf_op jit(solution)/shard_map/ppermute | solution.py:325
  119.1 0.0 all-to-all-done.2.terms
  119.1 13.4 %collective-permute-done.2.far = bf16[128,768]{1,0:T(8,128)(2,1)S(1)} collective-permute-done((bf16[128,768]{1,0:T(8,128)(2,1)S(1)}, bf16[128,768]{1,0:T(8,128)(2,1)S(1)}, u32[]{:S(2)}, u32[]{:S(2)}) %collective-permute-start.2) | collective-permute-done | bytes 196640 | tf_op jit(solution)/shard_map/ppermute | solution.py:325
  132.5 0.0 copy-start
  132.5 0.8 copy-done
  133.3 0.8 finish.1
  (1 shorter events, 0.0 us)
Async XLA Ops:
  7.2 72.0 %all-gather.3.cloned.1.call-start = ((), (), s32[]{:S(2)}) async-start(), calls=%async_computation.5 | async-start | bytes 4718592 | tf_op jit(solution)/shard_map/all_gather | solution.py:311
  10.5 20.2 %collective-permute-start = (bf16[128,256]{1,0:T(8,128)(2,1)}, bf16[128,256]{1,0:T(8,128)(2,1)S(1)}, u32[]{:S(2)}, u32[]{:S(2)}) collective-permute-start(bf16[128,256]{1,0:T(8,128)(2,1)} %get-tuple-element.12), channel_id=1, source_target_pairs={{0,2},{2,0},{1,3},{3,1},{4,6},{6,4},{5,7},{7,5},{8,10},{10,8},{9,1... | collective-permute-start | bytes 196616 | tf_op jit(solution)/shard_map/ppermute | solution.py:312
  32.5 21.3 %all-to-all-start.1 = ((bf16[4,256,256]{2,1,0:T(8,128)(2,1)}), bf16[4,256,256]{2,1,0:T(8,128)(2,1)S(1)}, u32[]{:S(2)}, u32[]{:S(2)}) async-start(bf16[4,256,256]{2,1,0:T(8,128)(2,1)} %broadcast_in_dim.2), calls=%async_computation.1 | async-start | bytes 1048576 | tf_op jit(solution)/shard_map/all_to_all | solution.py:316
  37.0 1.2 copy-start.2
  38.2 1.0 copy-start.3
  39.2 1.0 copy-start.4
  40.3 0.8 copy-start.5
  41.1 0.8 copy-start.6
  41.9 0.8 copy-start.7
  53.8 25.4 %copy-start.8 = (bf16[4,256,256]{2,1,0:T(8,128)(2,1)}, bf16[4,256,256]{2,1,0:T(8,128)(2,1)S(1)}, u32[]{:S(2)}) copy-start(bf16[4,256,256]{2,1,0:T(8,128)(2,1)S(1)} %all-to-all-done.1.wkv) | copy-start | bytes 1572868
  71.8 16.6 %all-to-all-start = ((bf16[8,128,384]{2,1,0:T(8,128)(2,1)}), bf16[8,128,384]{2,1,0:T(8,128)(2,1)S(1)}, u32[]{:S(2)}, u32[]{:S(2)}) async-start(bf16[8,128,384]{2,1,0:T(8,128)(2,1)} %get-tuple-element.10), calls=%async_computation | async-start | bytes 1572864 | tf_op jit(solution)/shard_map/all_to_all | solution.py:320
  75.4 3.8 %collective-permute-start.1 = (bf16[4,256,256]{2,1,0:T(8,128)(2,1)S(1)}, bf16[4,256,256]{2,1,0:T(8,128)(2,1)S(1)}, u32[]{:S(2)}, u32[]{:S(2)}) collective-permute-start(bf16[4,256,256]{2,1,0:T(8,128)(2,1)S(1)} %all-to-all-done.1.wkv), channel_id=1, source_target_pairs={{0,1},{1,0},{2,3},{3,2},{4,5},{5,4},{6,7},{7,6},{8,9},{9,8},{10,11... | collective-permute-start | bytes 1572872 | tf_op jit(solution)/shard_map/ppermute | solution.py:318
  79.2 0.8 copy-start.10
  85.4 20.6 %copy-start.1 = (bf16[128,256]{1,0:T(8,128)(2,1)S(1)}, bf16[128,256]{1,0:T(8,128)(2,1)}, u32[]{:S(2)}) copy-start(bf16[128,256]{1,0:T(8,128)(2,1)} %get-tuple-element.17.kv_sum) | copy-start | bytes 196612
  88.5 4.8 %copy-start.9 = (bf16[8,128,384]{2,1,0:T(8,128)(2,1)}, bf16[8,128,384]{2,1,0:T(8,128)(2,1)S(1)}, u32[]{:S(2)}) copy-start(bf16[8,128,384]{2,1,0:T(8,128)(2,1)S(1)} %all-to-all-done.moved) | copy-start | bytes 2359300
  88.5 12.6 %all-to-all-start.4 = ((bf16[4,128,512]{2,1,0:T(8,128)(2,1)}), bf16[4,128,512]{2,1,0:T(8,128)(2,1)S(1)}, u32[]{:S(2)}, u32[]{:S(2)}) async-start(bf16[4,128,512]{2,1,0:T(8,128)(2,1)} %get-tuple-element.16), calls=%async_computation.4 | async-start | bytes 1048576 | tf_op jit(solution)/shard_map/all_to_all | solution.py:322
  101.1 18.0 %all-to-all-start.2 = ((bf16[4,128,512]{2,1,0:T(8,128)(2,1)}), bf16[4,128,512]{2,1,0:T(8,128)(2,1)S(1)}, u32[]{:S(2)}, u32[]{:S(2)}) async-start(bf16[4,128,512]{2,1,0:T(8,128)(2,1)} %get-tuple-element.13), calls=%async_computation.2 | async-start | bytes 1048576 | tf_op jit(solution)/shard_map/all_to_all | solution.py:324
  106.1 26.4 %collective-permute-start.2 = (bf16[128,768]{1,0:T(8,128)(2,1)S(1)}, bf16[128,768]{1,0:T(8,128)(2,1)S(1)}, u32[]{:S(2)}, u32[]{:S(2)}) collective-permute-start(bf16[128,768]{1,0:T(8,128)(2,1)S(1)} %gather.1), channel_id=1, source_target_pairs={{0,2},{2,0},{1,3},{3,1},{4,6},{6,4},{5,7},{7,5},{8,10},{10,8},{9,1... | collective-permute-start | bytes 589832 | tf_op jit(solution)/shard_map/ppermute | solution.py:325
  132.5 0.8 copy-start
Sparse Core Ops, SparseCore 0:
  10.6 49.8 all-gather.2

commit v3 on v2

--- a/solution.py
+++ b/solution.py
@@ -5,9 +5,11 @@
 from jax.experimental.pallas import tpu as pltpu
 from jax.sharding import Mesh, PartitionSpec as P
 
+HB = pl.BlockSpec(memory_space=pltpu.HBM)
 VM = pl.BlockSpec(memory_space=pltpu.VMEM)
 SM = pl.BlockSpec(memory_space=pltpu.SMEM)
-BIG = 56 * 2**20
+BIG = 58 * 2**20
+FULL = 60 * 2**20
 NT = (((1,), (1,)), ((), ()))
 NN = (((1,), (0,)), ((), ()))
 
@@ -24,8 +26,22 @@
     return x
 
 
-def attention_kernel(half, query, q_exp, kv, kv_exp, grad, grad_exp, other, own, out, sems, q_s, k_s, v_s, do_s, kt_s, s_s, dp_s, ds_s, dk_s, dv_s, *, block, tile):
+def attention_kernel(place_s, query_h, q_exp_h, kv_h, kv_exp_h, grad_h, grad_exp_h, moved, query, q_exp, kv, kv_exp, grad, grad_exp, out, sems, q_s, k_s, v_s, do_s, kt_s, s_s, dp_s, ds_s, dk_s, dv_s, *, block, tile):
     seq, width = query.shape
+    near = place_s[0]
+    copies = [
+        pltpu.make_async_copy(source, target, sems.at[n])
+        for n, (source, target) in enumerate(
+            zip(
+                (q_exp_h, grad_exp_h, kv_exp_h, query_h, grad_h, kv_h),
+                (q_exp, grad_exp, kv_exp, query, grad, kv),
+            )
+        )
+    ]
+    for copy in copies:
+        copy.start()
+    for copy in copies:
+        copy.wait()
     scale = 1.0 / math.sqrt(width)
     coef = scale * math.log2(math.e)
     exps = jnp.concatenate([q_exp[...], grad_exp[...], kv_exp[...]], axis=0)
@@ -102,42 +118,39 @@
         upper = first + block
         dq = lax.dot_general(kt_s[:, :upper], ds_s[:upper, :], NN, preferred_element_type=jnp.float32)
         dq = ((dq * scale).T).astype(jnp.bfloat16)
-        place(out, first, 0, dq)
+        place(out, near, first, 0, dq)
     for first in range(0, seq, 512):
         rows_ = slice(first, first + 512)
-        place(out, first, width, (dk_s[rows_, :] * scale).astype(jnp.bfloat16))
-        place(out, first, 2 * width, dv_s[rows_, :].astype(jnp.bfloat16))
-    z = half[0]
-    copies = [
-        pltpu.make_async_copy(out.at[1 - z], other, sems.at[0]),
-        pltpu.make_async_copy(out.at[z], own, sems.at[1]),
-    ]
-    for copy in copies:
-        copy.start()
-    for copy in copies:
-        copy.wait()
-
-
-def place(out, first, col, value):
+        place(out, near, first, width, (dk_s[rows_, :] * scale).astype(jnp.bfloat16))
+        place(out, near, first, 2 * width, dv_s[rows_, :].astype(jnp.bfloat16))
+    copy = pltpu.make_async_copy(out, moved, sems.at[6])
+    copy.start()
+    copy.wait()
+
+
+def place(out, near, first, col, value):
     piece = out.shape[2]
     for j in range(value.shape[0] // piece):
         h = first // piece + j
         y, z, c = h // 4, (h // 2) % 2, h % 2
-        out[z, y * 2 + c, :, col:col + value.shape[1]] = value[j * piece:(j + 1) * piece]
-
-
-def attention(half, query, q_exp, kv, kv_exp, grad, grad_exp, block=512, tile=256):
+        slot = jnp.where(near == z, 1, 0)
+        out[y * 2 + c, slot, :, col:col + value.shape[1]] = value[j * piece:(j + 1) * piece]
+
+
+def attention(spot, query, q_exp, kv, kv_exp, grad, grad_exp, block=512, tile=256):
     seq, width = query.shape
     f32, b16 = jnp.float32, jnp.bfloat16
-    sent = (8, seq // 16, 3 * width)
+    sent = (8, 2, seq // 16, 3 * width)
+    operands = (query, q_exp, kv, kv_exp, grad, grad_exp)
     return pl.pallas_call(
         functools.partial(attention_kernel, block=block, tile=tile),
-        out_shape=[jax.ShapeDtypeStruct(sent, b16)] * 2,
-        in_specs=[SM] + [VM] * 6,
-        out_specs=[pl.BlockSpec(memory_space=pltpu.HBM)] * 2,
-        scratch_shapes=[
-            pltpu.VMEM((2,) + sent, b16),
-            pltpu.SemaphoreType.DMA((2,)),
+        out_shape=jax.ShapeDtypeStruct(sent, b16),
+        in_specs=[SM] + [HB] * 6,
+        out_specs=HB,
+        scratch_shapes=[pltpu.VMEM(a.shape, a.dtype) for a in operands]
+        + [
+            pltpu.VMEM(sent, b16),
+            pltpu.SemaphoreType.DMA((7,)),
             pltpu.VMEM((seq, width), b16),
             pltpu.VMEM((seq, width), b16),
             pltpu.VMEM((seq, width), b16),
@@ -149,12 +162,12 @@
             pltpu.VMEM((seq, width), f32),
             pltpu.VMEM((seq, width), f32),
         ],
-        compiler_params=pltpu.CompilerParams(vmem_limit_bytes=32 * 2**20),
+        compiler_params=pltpu.CompilerParams(vmem_limit_bytes=FULL),
         cost_estimate=pl.CostEstimate(
             flops=3 * 10**9, bytes_accessed=6 * 2**20, transcendentals=2 * 10**6
         ),
         name="attention",
-    )(half, query, q_exp, kv, kv_exp, grad, grad_exp)
+    )(spot, *operands)
 
 
 def scaled(mantissa, exps):
@@ -163,97 +176,132 @@
     return (blocks * power(exps)[:, None, :]).reshape(rows, cols).astype(jnp.bfloat16)
 
 
-def weights_kernel(wq, wq_exp, wkv, wkv_exp, q_out, kv_out):
+def weights_kernel(wq_h, wq_exp_h, wkv_h, wkv_exp_h, q_h, kv_h, wq, wq_exp, wkv, wkv_exp, q_out, kv_out, sems):
+    loads = [
+        pltpu.make_async_copy(source, target, sems.at[n])
+        for n, (source, target) in enumerate(
+            ((wq_exp_h, wq_exp), (wq_h, wq), (wkv_exp_h, wkv_exp), (wkv_h, wkv))
+        )
+    ]
+    for copy in loads:
+        copy.start()
+    for copy in loads[:2]:
+        copy.wait()
     q_out[...] = scaled(wq[...], wq_exp[...])
+    stores = [pltpu.make_async_copy(q_out, q_h, sems.at[4])]
+    stores[0].start()
+    for copy in loads[2:]:
+        copy.wait()
+    kv_out[...] = scaled(wkv[...], wkv_exp[...])
+    for n in range(kv_h.shape[0]):
+        stores.append(pltpu.make_async_copy(kv_out, kv_h.at[n], sems.at[5 + n]))
+        stores[-1].start()
+    for copy in stores:
+        copy.wait()
+
+
+def weights(wq, wq_exp, wkv, wkv_exp, copies):
+    operands = (wq, wq_exp, wkv, wkv_exp)
+    return pl.pallas_call(
+        weights_kernel,
+        out_shape=[
+            jax.ShapeDtypeStruct(wq.shape, jnp.bfloat16),
+            jax.ShapeDtypeStruct((copies,) + wkv.shape, jnp.bfloat16),
+        ],
+        in_specs=[HB] * 4,
+        out_specs=[HB] * 2,
+        scratch_shapes=[pltpu.VMEM(a.shape, a.dtype) for a in operands]
+        + [
+            pltpu.VMEM(wq.shape, jnp.bfloat16),
+            pltpu.VMEM(wkv.shape, jnp.bfloat16),
+            pltpu.SemaphoreType.DMA((5 + copies,)),
+        ],
+        compiler_params=pltpu.CompilerParams(vmem_limit_bytes=FULL),
+        name="weights",
+    )(*operands)
+
+
+def kv_terms(spot, sums, near, far):
+    a = lax.dot_general(sums, near, NT, preferred_element_type=jnp.float32)
+    b = lax.dot_general(sums, far, NT, preferred_element_type=jnp.float32)
+    first = spot[1] == 0
+    return jnp.concatenate([jnp.where(first, a, b), jnp.where(first, b, a)], axis=1)
+
+
+def project_kernel(spot, moved, wq, wkv, wkv_c, out, kv_out, dq_s, *, width):
+    sources = moved.shape[0]
 
     @pl.when(pl.program_id(0) == 0)
     def _():
-        kv_out[...] = scaled(wkv[...], wkv_exp[...])
-
-
-def weights(wq, wq_exp, wkv, wkv_exp, steps=4):
-    def stream(a):
-        return pl.BlockSpec((a.shape[0] // steps, a.shape[1]), lambda i: (i, 0))
-
-    def whole(a):
-        return pl.BlockSpec(a.shape, lambda i: (0, 0))
-
-    return pl.pallas_call(
-        weights_kernel,
-        grid=(steps,),
-        out_shape=[
-            jax.ShapeDtypeStruct(wq.shape, jnp.bfloat16),
-            jax.ShapeDtypeStruct(wkv.shape, jnp.bfloat16),
-        ],
-        in_specs=[stream(wq), stream(wq_exp), whole(wkv), whole(wkv_exp)],
-        out_specs=[stream(wq), whole(wkv)],
-        compiler_params=pltpu.CompilerParams(vmem_limit_bytes=BIG),
-        name="weights",
-    )(wq, wq_exp, wkv, wkv_exp)
-
-
-def project_kernel(core, moved, wq, wkv, wkv_far, out, kv_out, sum_s):
-    sources, tokens, lanes = moved.shape
-    width = lanes // 3
-
-    @pl.when(pl.program_id(0) == 0)
-    def _():
-        total = moved[0, :, width:].astype(jnp.float32)
-        for s in range(1, sources):
-            total = total + moved[s, :, width:].astype(jnp.float32)
-        sum_s[...] = total.astype(jnp.bfloat16)
-        kv_out[...] = sum_s[...]
-
-    piece = wkv.shape[1] // 2
-    first = core[0] == 0
-    parts = []
-    for z in range(2):
-        rows = slice(z * piece, (z + 1) * piece)
-        near = lax.dot_general(sum_s[...], wkv[0, rows, :], NT, preferred_element_type=jnp.float32)
-        far = lax.dot_general(sum_s[...], wkv_far[0, rows, :], NT, preferred_element_type=jnp.float32)
-        parts += [jnp.where(first, near, far), jnp.where(first, far, near)]
-    acc = jnp.concatenate(parts, axis=1)
+        kv_out[...] = summed(moved[:, 0, :, width:]).astype(jnp.bfloat16)
+        for s in range(sources):
+            dq_s[:, s * width:(s + 1) * width] = moved[s, 0, :, :width]
+
+    acc = jnp.zeros(out.shape[1:], jnp.float32)
     for s in range(0, sources, 2):
-        left = jnp.concatenate([moved[s, :, :width], moved[s + 1, :, :width]], axis=1)
         right = jnp.concatenate([wq[s], wq[s + 1]], axis=1)
+        left = dq_s[:, s * width:(s + 2) * width]
         acc = acc + lax.dot_general(left, right, NT, preferred_element_type=jnp.float32)
-    out[0] = acc.astype(jnp.bfloat16)
-
-
-def project(core, moved, wq, wkv, wkv_far):
-    sources, tokens, lanes = moved.shape
+    out[0] = acc
+    pair = kv_terms(spot, kv_out[...], wkv[0], wkv_c[0])
+    cols = pl.ds(pl.multiple_of(spot[0] * pair.shape[1], pair.shape[1]), pair.shape[1])
+    out[0, :, cols] += pair
+
+
+def project(spot, slot, moved, wq, wkv, wkv_c):
+    sources, _, tokens, lanes = moved.shape
     model = wq.shape[1]
     groups = wkv.shape[0]
     part = model // groups
-    kv_lanes = lanes * 2 // 3
+    width = lanes // 3
     kv_block = pl.BlockSpec((1,) + wkv.shape[1:], lambda j: (j, 0, 0))
     return pl.pallas_call(
-        project_kernel,
+        functools.partial(project_kernel, width=width),
         grid=(groups,),
         out_shape=[
-            jax.ShapeDtypeStruct((groups, tokens, part), jnp.bfloat16),
-            jax.ShapeDtypeStruct((tokens, kv_lanes), jnp.bfloat16),
+            jax.ShapeDtypeStruct((groups, tokens, part), jnp.float32),
+            jax.ShapeDtypeStruct((tokens, 2 * width), jnp.bfloat16),
         ],
         in_specs=[
             SM,
-            pl.BlockSpec((sources, tokens, lanes), lambda j: (0, 0, 0)),
-            pl.BlockSpec((sources, part, lanes // 3), lambda j: (0, j, 0)),
+            pl.BlockSpec((sources, 1, tokens, lanes), lambda j: (0, slot, 0, 0)),
+            pl.BlockSpec((sources, part, width), lambda j: (0, j, 0)),
             kv_block,
             kv_block,
         ],
         out_specs=[
             pl.BlockSpec((1, tokens, part), lambda j: (j, 0, 0)),
-            pl.BlockSpec((tokens, kv_lanes), lambda j: (0, 0)),
-        ],
-        scratch_shapes=[pltpu.VMEM((tokens, kv_lanes), jnp.bfloat16)],
+            pl.BlockSpec((tokens, 2 * width), lambda j: (0, 0)),
+        ],
+        scratch_shapes=[pltpu.VMEM((tokens, sources * width), jnp.bfloat16)],
         compiler_params=pltpu.CompilerParams(vmem_limit_bytes=BIG),
         cost_estimate=pl.CostEstimate(
-            flops=2 * tokens * model * (sources + 2) * 128,
+            flops=2 * tokens * model * (sources + 1) * width,
             bytes_accessed=8 * 2**20,
             transcendentals=0,
         ),
         name="project",
-    )(core, moved, wq, wkv, wkv_far)
+    )(spot, moved, wq, wkv, wkv_c)
+
+
+def complete_kernel(spot, acc, sums, wkv, wkv_c, out):
+    out[...] = acc[...].astype(out.dtype)
+    for j in range(acc.shape[0]):
+        pair = kv_terms(spot, sums[...], wkv[j], wkv_c[j])
+        size = pair.shape[1]
+        cols = pl.ds(pl.multiple_of((1 - spot[0]) * size, size), size)
+        out[j, :, cols] = (acc[j, :, cols] + pair).astype(out.dtype)
+
+
+def complete(spot, acc, sums, wkv, wkv_c):
+    return pl.pallas_call(
+        complete_kernel,
+        out_shape=jax.ShapeDtypeStruct(acc.shape, jnp.bfloat16),
+        in_specs=[SM] + [VM] * 4,
+        out_specs=VM,
+        compiler_params=pltpu.CompilerParams(vmem_limit_bytes=16 * 2**20),
+        name="complete",
+    )(spot, acc, sums, wkv, wkv_c)
 
 
 def summed(terms):
@@ -304,26 +352,25 @@
 
 def shards(query, query_exp, kv, kv_exp, out_grad, out_grad_exp, q_weight, q_weight_exp, kv_weight, kv_weight_exp):
     swap = [(0, 1), (1, 0)]
-    zh = lax.axis_index("zh")
-    half = zh.reshape(1).astype(jnp.int32)
-    core = lax.axis_index("core").reshape(1).astype(jnp.int32)
-    wq, wkv = weights(q_weight, q_weight_exp, kv_weight, kv_weight_exp)
+    spot = jnp.stack([lax.axis_index("zh"), lax.axis_index("core")]).astype(jnp.int32)
+    wq, wkv = weights(q_weight, q_weight_exp, kv_weight, kv_weight_exp, 4)
     wq_all = lax.all_gather(wq, ("y", "core"), axis=0)
+    wkv = lax.all_to_all(wkv, "y", 0, 0)
+    grads = attention(spot, query, query_exp, kv, kv_exp, out_grad, out_grad_exp)
+    wkv, grads = lax.optimization_barrier((wkv, grads))
+    wkv_c = lax.ppermute(wkv, "core", swap)
     wkv_z = lax.ppermute(wkv, "zh", swap)
-    low = jnp.where(zh == 0, wkv, wkv_z)
-    high = jnp.where(zh == 0, wkv_z, wkv)
-    both = jnp.concatenate([low, high], axis=0)
-    wkv_near = lax.all_to_all(jnp.broadcast_to(both[None], (4,) + both.shape), "y", 0, 0)
-    other, own = attention(half, query, query_exp, kv, kv_exp, out_grad, out_grad_exp)
-    wkv_far = lax.ppermute(wkv_near, "core", swap)
-    other = lax.all_to_all(other, ("y", "core"), 0, 0)
-    own = lax.all_to_all(own, ("y", "core"), 0, 0)
-    terms_other, kv_other = project(core, other, wq_all, wkv_near, wkv_far)
-    terms_other = lax.all_to_all(terms_other, "x", 0, 0)
-    terms_own, kv_own = project(core, own, wq_all, wkv_near, wkv_far)
-    terms_own = lax.all_to_all(terms_own, "x", 0, 0)
-    far = lax.ppermute(gather(terms_other, kv_other), "zh", swap)
-    return tuple(finish(terms_own, kv_own, far))
+    moved = lax.all_to_all(grads, ("y", "core"), 0, 0)
+    wkv_zc = lax.ppermute(wkv_z, "core", swap)
+    acc, kv_other = project(spot, 0, moved, wq_all, wkv, wkv_c)
+    other = lax.all_to_all(complete(spot, acc, kv_other, wkv_z, wkv_zc), "x", 0, 0)
+    acc, kv_own = project(spot, 1, moved, wq_all, wkv, wkv_c)
+    own = complete(spot, acc, kv_own, wkv_z, wkv_zc)
+    sent = gather(other, kv_other)
+    own, sent = lax.optimization_barrier((own, sent))
+    far = lax.ppermute(sent, "zh", swap)
+    own = lax.all_to_all(own, "x", 0, 0)
+    return tuple(finish(own, kv_own, far))
 
 
 def solution(mesh):

time: 142 us -> 141 us (level)
  the two profiles are of different devices: /device:TPU:2 before, /device:TPU:35 now
where the time goes in v3:
time: 141 us; the launch traced here: 140 us
  starting transfers between devices  49.8 us (35%)
  waiting for transfers between devices  39.4 us (28%)
  Pallas kernels  30.8 us (22%)
  between operations  14.2 us (10%)
  local copies, waits for them, and re-layouts  5.38 us (4%)
    ppermute x1, waiting for transfers between devices, shards(): wkv_z = lax.ppermute(wkv, 'zh', swap)  21.3 us
    ppermute x1, waiting for transfers between devices, shards(): far = lax.ppermute(sent, 'zh', swap)  18 us
    ppermute x1, starting transfers between devices, shards(): wkv_z = lax.ppermute(wkv, 'zh', swap)  14.5 us
    pallas_call x1, Pallas kernels, attention(): pl.pallas_call(functools.partial(attention_kernel, block=block, tile=tile...  13.7 us
    ppermute x1, starting transfers between devices, shards(): far = lax.ppermute(sent, 'zh', swap)  11.8 us
    pallas_call x2, Pallas kernels, project(): pl.pallas_call(functools.partial(project_kernel, width=width), grid=(grou...  10.8 us
    all_to_all x1, starting transfers between devices, shards(): moved = lax.all_to_all(grads, ('y', 'core'), 0, 0)  5.76 us
    unnamed x22, local copies, waits for them, and re-layouts  5.38 us
  transfers between devices with their start and end apart: 9, of which 2 were waited for; matrix products, arithmetic and copies ran while one was open for 0% of the time, Pallas kernels for 19%

profile of v3, /device:TPU:35, one launch (start us, length us, event | category | flops | bytes accessed | tf_op | source)
XLA Modules:
  0.0 140.2 jit_solution(1431171294954374181)
XLA Ops:
  7.2 0.0 all-gather.3.cloned.1.call-start
  7.2 2.1 %weights.1 = (bf16[2048,128]{1,0:T(8,128)(2,1)}, bf16[4,128,256]{2,1,0:T(8,128)(2,1)}) custom-call(bf16[2048,128]{1,0:T(8,128)(2,1)} %wq_h.1, s32[64,128]{1,0:T(8,128)} %wq_exp_h.1, bf16[128,256]{1,0:T(8,128)(2,1)} %wkv_h.1, s32[4,256]{1,0:T(4,128)} %wkv_exp_h.1), custom_call_target="tpu_custom_call" | custom-call | tf_op jit(solution)/shard_map/weights/pallas_call | solution.py:205
  9.4 0.0 all-gather.3.cloned.1.call-update
  9.4 4.2 %all-to-all-start = ((bf16[4,128,256]{2,1,0:T(8,128)(2,1)}), bf16[4,128,256]{2,1,0:T(8,128)(2,1)S(1)}, u32[]{:S(2)}, u32[]{:S(2)}) async-start(bf16[4,128,256]{2,1,0:T(8,128)(2,1)} %get-tuple-element.12), calls=%async_computation | async-start | bytes 524288 | tf_op jit(solution)/shard_map/all_to_all | solution.py:358
  13.6 0.6 pad_add_fusion.place_s.spot
  14.2 13.7 %attention.1 = bf16[8,2,128,384]{3,2,1,0:T(8,128)(2,1)} custom-call(s32[2]{0:T(128)} %pad_add_fusion.place_s.spot, bf16[2048,128]{1,0:T(8,128)(2,1)} %query_h.1, s32[4,2048]{1,0:T(4,128)} %q_exp_h.1, bf16[2048,256]{1,0:T(8,128)(2,1)} %kv_h.1, s32[8,2048]{1,0:T(8,128)} %kv_exp_h.1, bf16[2048,128]{1,0:T(8,128)(2,1)} %grad_h.1, s32[4,2048]{1,0:T(4,128)} %grad_exp_h.1), custom_call_target="tpu_custom_call" | custom-call | flops 3000000000 | bytes 6291456 | tf_op jit(solution)/shard_map/attention/pallas_call | solution.py:145
  27.9 0.0 all-to-all-done.wkv
  27.9 0.0 copy-start.9
  28.0 5.8 %all-to-all-start.1 = ((bf16[8,2,128,384]{3,2,1,0:T(8,128)(2,1)}), bf16[8,2,128,384]{3,2,1,0:T(8,128)(2,1)S(1)}, u32[]{:S(2)}, u32[]{:S(2)}) async-start(bf16[8,2,128,384]{3,2,1,0:T(8,128)(2,1)} %attention.1), calls=%async_computation.1 | async-start | bytes 3145728 | tf_op jit(solution)/shard_map/all_to_all | solution.py:363
  33.7 14.5 %collective-permute-start.1 = (bf16[4,128,256]{2,1,0:T(8,128)(2,1)S(1)}, bf16[4,128,256]{2,1,0:T(8,128)(2,1)S(1)}, u32[]{:S(2)}, u32[]{:S(2)}) collective-permute-start(bf16[4,128,256]{2,1,0:T(8,128)(2,1)S(1)} %all-to-all-done.wkv), channel_id=1, source_target_pairs={{0,2},{2,0},{1,3},{3,1},{4,6},{6,4},{5,7},{7,5},{8,10},{10,8},{9,1... | collective-permute-start | bytes 786440 | tf_op jit(solution)/shard_map/ppermute | solution.py:362
  48.3 0.0 copy-done.9
  48.3 2.2 %collective-permute-start = (bf16[4,128,256]{2,1,0:T(8,128)(2,1)S(1)}, bf16[4,128,256]{2,1,0:T(8,128)(2,1)S(1)}, u32[]{:S(2)}, u32[]{:S(2)}) collective-permute-start(bf16[4,128,256]{2,1,0:T(8,128)(2,1)S(1)} %all-to-all-done.wkv), channel_id=1, source_target_pairs={{0,1},{1,0},{2,3},{3,2},{4,5},{5,4},{6,7},{7,6},{8,9},{9,8},{10,11... | collective-permute-start | bytes 786440 | tf_op jit(solution)/shard_map/ppermute | solution.py:361
  50.5 21.3 %collective-permute-done.1.wkv = bf16[4,128,256]{2,1,0:T(8,128)(2,1)S(1)} collective-permute-done((bf16[4,128,256]{2,1,0:T(8,128)(2,1)S(1)}, bf16[4,128,256]{2,1,0:T(8,128)(2,1)S(1)}, u32[]{:S(2)}, u32[]{:S(2)}) %collective-permute-start.1) | collective-permute-done | bytes 262176 | tf_op jit(solution)/shard_map/ppermute | solution.py:362
  71.8 2.7 %collective-permute-start.2 = (bf16[4,128,256]{2,1,0:T(8,128)(2,1)S(1)}, bf16[4,128,256]{2,1,0:T(8,128)(2,1)S(1)}, u32[]{:S(2)}, u32[]{:S(2)}) collective-permute-start(bf16[4,128,256]{2,1,0:T(8,128)(2,1)S(1)} %collective-permute-done.1.wkv), channel_id=1, source_target_pairs={{0,1},{1,0},{2,3},{3,2},{4,5},{5,4},{6,7},{7,6},{8,9},{9,8},{10,11... | collective-permute-start | bytes 786440 | tf_op jit(solution)/shard_map/ppermute | solution.py:364
  74.5 0.0 collective-permute-done.wkv_c
  74.5 0.0 copy-start.10
  74.5 0.0 all-to-all-done.1.moved
  74.5 0.0 copy-start.8
  74.5 0.0 all-gather.3.cloned.1.call-done
  74.6 0.7 copy-done.10
  75.2 0.6 copy-done.8
  75.8 0.0 copy-start.6
  75.8 5.4 %project.3 = (f32[4,128,512]{2,1,0:T(8,128)}, bf16[128,256]{1,0:T(8,128)(2,1)}) custom-call(s32[2]{0:T(128)} %pad_add_fusion.place_s.spot, bf16[8,2,128,384]{3,2,1,0:T(8,128)(2,1)} %copy-done.8, bf16[8,2048,128]{2,1,0:T(8,128)(2,1)} %bitcast.3, bf16[4,128,256]{2,1,0:T(8,128)(2,1)} %copy-done.9, bf16[4,128,256]{2,1,0:T(8,128)(2,1)} %copy-done.10), custom_call_target="tpu_custom_call" | custom-call | flops 603979776 | bytes 8388608 | tf_op jit(solution)/shard_map/project/pallas_call | solution.py:258
  81.2 0.0 collective-permute-done.2.wkv_c
  81.2 0.0 copy-done.6
  81.2 0.0 copy-start.1
  81.2 1.2 copy-done.1
  82.4 0.0 copy-start.4
  82.4 0.8 copy-done.4
  83.3 1.7 %complete.3 = bf16[4,128,512]{2,1,0:T(8,128)(2,1)} custom-call(s32[2]{0:T(128)S(1)} %copy-done.6, f32[4,128,512]{2,1,0:T(8,128)S(1)} %copy-done.1, bf16[128,256]{1,0:T(8,128)(2,1)S(1)} %copy-done.4, bf16[4,128,256]{2,1,0:T(8,128)(2,1)S(1)} %collective-permute-done.1.wkv, bf16[4,128,256]{2,1,0:T(8,128)(2,1)S(1)} %collective-permute-done.2.wkv_c), custom_call_target="tpu_custom_call" | custom-call | tf_op jit(solution)/shard_map/complete/pallas_call | solution.py:297
  84.9 4.3 %all-to-all-start.2 = ((bf16[4,128,512]{2,1,0:T(8,128)(2,1)}), bf16[4,128,512]{2,1,0:T(8,128)(2,1)S(1)}, u32[]{:S(2)}, u32[]{:S(2)}) async-start(bf16[4,128,512]{2,1,0:T(8,128)(2,1)} %complete.3), calls=%async_computation.2 | async-start | bytes 1048576 | tf_op jit(solution)/shard_map/all_to_all | solution.py:366
  89.2 0.0 copy-start.7
  89.2 0.0 copy-start.5
  89.2 5.4 %project.2 = (f32[4,128,512]{2,1,0:T(8,128)}, bf16[128,256]{1,0:T(8,128)(2,1)}) custom-call(s32[2]{0:T(128)} %pad_add_fusion.place_s.spot, bf16[8,2,128,384]{3,2,1,0:T(8,128)(2,1)} %copy-done.8, bf16[8,2048,128]{2,1,0:T(8,128)(2,1)} %bitcast.4, bf16[4,128,256]{2,1,0:T(8,128)(2,1)} %copy-done.9, bf16[4,128,256]{2,1,0:T(8,128)(2,1)} %copy-done.10), custom_call_target="tpu_custom_call" | custom-call | flops 603979776 | bytes 8388608 | tf_op jit(solution)/shard_map/project/pallas_call | solution.py:258
  94.6 0.0 copy-done.7
  94.6 0.0 copy-start
  94.6 1.2 copy-done
  95.8 0.8 copy-done.2
  96.7 1.7 %complete.2 = bf16[4,128,512]{2,1,0:T(8,128)(2,1)} custom-call(s32[2]{0:T(128)S(1)} %copy-done.7, f32[4,128,512]{2,1,0:T(8,128)S(1)} %copy-done, bf16[128,256]{1,0:T(8,128)(2,1)S(1)} %copy-done.2, bf16[4,128,256]{2,1,0:T(8,128)(2,1)S(1)} %collective-permute-done.1.wkv, bf16[4,128,256]{2,1,0:T(8,128)(2,1)S(1)} %collective-permute-done.2.wkv_c), custom_call_target="tpu_custom_call" | custom-call | tf_op jit(solution)/shard_map/complete/pallas_call | solution.py:297
  98.4 0.0 all-to-all-done.2.terms
  98.4 0.0 copy-done.5
  98.4 0.1 gather.1
  98.4 4.3 %all-to-all-start.3 = ((bf16[4,128,512]{2,1,0:T(8,128)(2,1)}), bf16[4,128,512]{2,1,0:T(8,128)(2,1)S(1)}, u32[]{:S(2)}, u32[]{:S(2)}) async-start(bf16[4,128,512]{2,1,0:T(8,128)(2,1)} %complete.2), calls=%async_computation.3 | async-start | bytes 1048576 | tf_op jit(solution)/shard_map/all_to_all | solution.py:372
  102.7 11.8 %collective-permute-start.3 = (bf16[128,768]{1,0:T(8,128)(2,1)S(1)}, bf16[128,768]{1,0:T(8,128)(2,1)S(1)}, u32[]{:S(2)}, u32[]{:S(2)}) collective-permute-start(bf16[128,768]{1,0:T(8,128)(2,1)S(1)} %gather.1), channel_id=1, source_target_pairs={{0,2},{2,0},{1,3},{3,1},{4,6},{6,4},{5,7},{7,5},{8,10},{10,8},{9,1... | collective-permute-start | bytes 589832 | tf_op jit(solution)/shard_map/ppermute | solution.py:371
  114.5 18.0 %collective-permute-done.3.far = bf16[128,768]{1,0:T(8,128)(2,1)S(1)} collective-permute-done((bf16[128,768]{1,0:T(8,128)(2,1)S(1)}, bf16[128,768]{1,0:T(8,128)(2,1)S(1)}, u32[]{:S(2)}, u32[]{:S(2)}) %collective-permute-start.3) | collective-permute-done | bytes 196640 | tf_op jit(solution)/shard_map/ppermute | solution.py:371
  132.6 0.0 all-to-all-done.3.terms
  132.6 0.0 copy-done.3
  132.6 0.8 finish.1
  (2 shorter events, 0.0 us)
Async XLA Ops:
  7.2 67.4 %all-gather.3.cloned.1.call-start = ((), (), s32[]{:S(2)}) async-start(), calls=%async_computation.4 | async-start | bytes 4718592 | tf_op jit(solution)/shard_map/all_gather | solution.py:357
  9.4 18.6 %all-to-all-start = ((bf16[4,128,256]{2,1,0:T(8,128)(2,1)}), bf16[4,128,256]{2,1,0:T(8,128)(2,1)S(1)}, u32[]{:S(2)}, u32[]{:S(2)}) async-start(bf16[4,128,256]{2,1,0:T(8,128)(2,1)} %get-tuple-element.12), calls=%async_computation | async-start | bytes 524288 | tf_op jit(solution)/shard_map/all_to_all | solution.py:358
  27.9 20.3 %copy-start.9 = (bf16[4,128,256]{2,1,0:T(8,128)(2,1)}, bf16[4,128,256]{2,1,0:T(8,128)(2,1)S(1)}, u32[]{:S(2)}) copy-start(bf16[4,128,256]{2,1,0:T(8,128)(2,1)S(1)} %all-to-all-done.wkv) | copy-start | bytes 786436
  28.0 46.6 %all-to-all-start.1 = ((bf16[8,2,128,384]{3,2,1,0:T(8,128)(2,1)}), bf16[8,2,128,384]{3,2,1,0:T(8,128)(2,1)S(1)}, u32[]{:S(2)}, u32[]{:S(2)}) async-start(bf16[8,2,128,384]{3,2,1,0:T(8,128)(2,1)} %attention.1), calls=%async_computation.1 | async-start | bytes 3145728 | tf_op jit(solution)/shard_map/all_to_all | solution.py:363
  33.7 38.1 %collective-permute-start.1 = (bf16[4,128,256]{2,1,0:T(8,128)(2,1)S(1)}, bf16[4,128,256]{2,1,0:T(8,128)(2,1)S(1)}, u32[]{:S(2)}, u32[]{:S(2)}) collective-permute-start(bf16[4,128,256]{2,1,0:T(8,128)(2,1)S(1)} %all-to-all-done.wkv), channel_id=1, source_target_pairs={{0,2},{2,0},{1,3},{3,1},{4,6},{6,4},{5,7},{7,5},{8,10},{10,8},{9,1... | collective-permute-start | bytes 786440 | tf_op jit(solution)/shard_map/ppermute | solution.py:362
  48.3 26.2 %collective-permute-start = (bf16[4,128,256]{2,1,0:T(8,128)(2,1)S(1)}, bf16[4,128,256]{2,1,0:T(8,128)(2,1)S(1)}, u32[]{:S(2)}, u32[]{:S(2)}) collective-permute-start(bf16[4,128,256]{2,1,0:T(8,128)(2,1)S(1)} %all-to-all-done.wkv), channel_id=1, source_target_pairs={{0,1},{1,0},{2,3},{3,2},{4,5},{5,4},{6,7},{7,6},{8,9},{9,8},{10,11... | collective-permute-start | bytes 786440 | tf_op jit(solution)/shard_map/ppermute | solution.py:361
  71.8 9.4 %collective-permute-start.2 = (bf16[4,128,256]{2,1,0:T(8,128)(2,1)S(1)}, bf16[4,128,256]{2,1,0:T(8,128)(2,1)S(1)}, u32[]{:S(2)}, u32[]{:S(2)}) collective-permute-start(bf16[4,128,256]{2,1,0:T(8,128)(2,1)S(1)} %collective-permute-done.1.wkv), channel_id=1, source_target_pairs={{0,1},{1,0},{2,3},{3,2},{4,5},{5,4},{6,7},{7,6},{8,9},{9,8},{10,11... | collective-permute-start | bytes 786440 | tf_op jit(solution)/shard_map/ppermute | solution.py:364
  74.5 0.7 copy-start.10
  74.5 1.3 copy-start.8
  75.8 5.4 %copy-start.6 = (s32[2]{0:T(128)S(1)}, s32[2]{0:T(128)}, u32[]{:S(2)}) copy-start(s32[2]{0:T(128)} %pad_add_fusion.place_s.spot) | copy-start | bytes 28
  81.2 1.2 copy-start.1
  82.4 0.8 copy-start.4
  84.9 13.4 %all-to-all-start.2 = ((bf16[4,128,512]{2,1,0:T(8,128)(2,1)}), bf16[4,128,512]{2,1,0:T(8,128)(2,1)S(1)}, u32[]{:S(2)}, u32[]{:S(2)}) async-start(bf16[4,128,512]{2,1,0:T(8,128)(2,1)} %complete.3), calls=%async_computation.2 | async-start | bytes 1048576 | tf_op jit(solution)/shard_map/all_to_all | solution.py:366
  89.2 5.4 %copy-start.7 = (s32[2]{0:T(128)S(1)}, s32[2]{0:T(128)}, u32[]{:S(2)}) copy-start(s32[2]{0:T(128)} %pad_add_fusion.place_s.spot) | copy-start | bytes 28
  89.2 9.2 %copy-start.5 = (bf16[128,256]{1,0:T(8,128)(2,1)S(1)}, bf16[128,256]{1,0:T(8,128)(2,1)}, u32[]{:S(2)}) copy-start(bf16[128,256]{1,0:T(8,128)(2,1)} %get-tuple-element.19.sums.kv_sum) | copy-start | bytes 196612
  94.6 1.2 copy-start
  95.8 0.8 copy-start.2
  96.7 35.9 %copy-start.3 = (bf16[128,256]{1,0:T(8,128)(2,1)S(1)}, bf16[128,256]{1,0:T(8,128)(2,1)}, u32[]{:S(2)}) copy-start(bf16[128,256]{1,0:T(8,128)(2,1)} %get-tuple-element.17.sums.kv_sum) | copy-start | bytes 196612
  98.4 34.1 %all-to-all-start.3 = ((bf16[4,128,512]{2,1,0:T(8,128)(2,1)}), bf16[4,128,512]{2,1,0:T(8,128)(2,1)S(1)}, u32[]{:S(2)}, u32[]{:S(2)}) async-start(bf16[4,128,512]{2,1,0:T(8,128)(2,1)} %complete.2), calls=%async_computation.3 | async-start | bytes 1048576 | tf_op jit(solution)/shard_map/all_to_all | solution.py:372
  102.7 29.9 %collective-permute-start.3 = (bf16[128,768]{1,0:T(8,128)(2,1)S(1)}, bf16[128,768]{1,0:T(8,128)(2,1)S(1)}, u32[]{:S(2)}, u32[]{:S(2)}) collective-permute-start(bf16[128,768]{1,0:T(8,128)(2,1)S(1)} %gather.1), channel_id=1, source_target_pairs={{0,2},{2,0},{1,3},{3,1},{4,6},{6,4},{5,7},{7,5},{8,10},{10,8},{9,1... | collective-permute-start | bytes 589832 | tf_op jit(solution)/shard_map/ppermute | solution.py:371
Sparse Core Ops, SparseCore 0:
  10.2 58.8 all-gather.2

commit v4 on v3

--- a/solution.py
+++ b/solution.py
@@ -26,9 +26,8 @@
     return x
 
 
-def attention_kernel(place_s, query_h, q_exp_h, kv_h, kv_exp_h, grad_h, grad_exp_h, moved, query, q_exp, kv, kv_exp, grad, grad_exp, out, sems, q_s, k_s, v_s, do_s, kt_s, s_s, dp_s, ds_s, dk_s, dv_s, *, block, tile):
+def attention_kernel(place_s, query_h, q_exp_h, kv_h, kv_exp_h, grad_h, grad_exp_h, keep, send, query, q_exp, kv, kv_exp, grad, grad_exp, out, sems, q_s, k_s, v_s, do_s, kt_s, s_s, dp_s, ds_s, dk_s, dv_s, *, block, tile):
     seq, width = query.shape
-    near = place_s[0]
     copies = [
         pltpu.make_async_copy(source, target, sems.at[n])
         for n, (source, target) in enumerate(
@@ -118,39 +117,45 @@
         upper = first + block
         dq = lax.dot_general(kt_s[:, :upper], ds_s[:upper, :], NN, preferred_element_type=jnp.float32)
         dq = ((dq * scale).T).astype(jnp.bfloat16)
-        place(out, near, first, 0, dq)
+        place(out, place_s, first, 0, dq)
     for first in range(0, seq, 512):
         rows_ = slice(first, first + 512)
-        place(out, near, first, width, (dk_s[rows_, :] * scale).astype(jnp.bfloat16))
-        place(out, near, first, 2 * width, dv_s[rows_, :].astype(jnp.bfloat16))
-    copy = pltpu.make_async_copy(out, moved, sems.at[6])
-    copy.start()
-    copy.wait()
-
-
-def place(out, near, first, col, value):
-    piece = out.shape[2]
+        place(out, place_s, first, width, (dk_s[rows_, :] * scale).astype(jnp.bfloat16))
+        place(out, place_s, first, 2 * width, dv_s[rows_, :].astype(jnp.bfloat16))
+    stores = [
+        pltpu.make_async_copy(out.at[0], send, sems.at[6]),
+        pltpu.make_async_copy(out.at[1], keep, sems.at[7]),
+    ]
+    for copy in stores:
+        copy.start()
+    for copy in stores:
+        copy.wait()
+
+
+def place(out, spot, first, col, value):
+    piece = out.shape[3]
     for j in range(value.shape[0] // piece):
         h = first // piece + j
         y, z, c = h // 4, (h // 2) % 2, h % 2
-        slot = jnp.where(near == z, 1, 0)
-        out[y * 2 + c, slot, :, col:col + value.shape[1]] = value[j * piece:(j + 1) * piece]
+        mine = jnp.where(spot[1] == c, 1, 0)
+        slot = jnp.where(spot[0] == z, 1, 0)
+        out[mine, y, slot, :, col:col + value.shape[1]] = value[j * piece:(j + 1) * piece]
 
 
 def attention(spot, query, q_exp, kv, kv_exp, grad, grad_exp, block=512, tile=256):
     seq, width = query.shape
     f32, b16 = jnp.float32, jnp.bfloat16
-    sent = (8, 2, seq // 16, 3 * width)
+    sent = (4, 2, seq // 16, 3 * width)
     operands = (query, q_exp, kv, kv_exp, grad, grad_exp)
     return pl.pallas_call(
         functools.partial(attention_kernel, block=block, tile=tile),
-        out_shape=jax.ShapeDtypeStruct(sent, b16),
+        out_shape=[jax.ShapeDtypeStruct(sent, b16)] * 2,
         in_specs=[SM] + [HB] * 6,
-        out_specs=HB,
+        out_specs=[HB] * 2,
         scratch_shapes=[pltpu.VMEM(a.shape, a.dtype) for a in operands]
         + [
-            pltpu.VMEM(sent, b16),
-            pltpu.SemaphoreType.DMA((7,)),
+            pltpu.VMEM((2,) + sent, b16),
+            pltpu.SemaphoreType.DMA((8,)),
             pltpu.VMEM((seq, width), b16),
             pltpu.VMEM((seq, width), b16),
             pltpu.VMEM((seq, width), b16),
@@ -164,7 +169,7 @@
         ],
         compiler_params=pltpu.CompilerParams(vmem_limit_bytes=FULL),
         cost_estimate=pl.CostEstimate(
-            flops=3 * 10**9, bytes_accessed=6 * 2**20, transcendentals=2 * 10**6
+            flops=16 * 10**9, bytes_accessed=6 * 2**20, transcendentals=2 * 10**6
         ),
         name="attention",
     )(spot, *operands)
@@ -176,43 +181,46 @@
     return (blocks * power(exps)[:, None, :]).reshape(rows, cols).astype(jnp.bfloat16)
 
 
-def weights_kernel(wq_h, wq_exp_h, wkv_h, wkv_exp_h, q_h, kv_h, wq, wq_exp, wkv, wkv_exp, q_out, kv_out, sems):
+def weights_kernel(wq_h, wq_exp_h, wkv_h, wkv_exp_h, all_h, kv_h, wq, wq_exp, wkv, wkv_exp, out, kv_out, sems):
     loads = [
         pltpu.make_async_copy(source, target, sems.at[n])
         for n, (source, target) in enumerate(
-            ((wq_exp_h, wq_exp), (wq_h, wq), (wkv_exp_h, wkv_exp), (wkv_h, wkv))
+            ((wkv_exp_h, wkv_exp), (wkv_h, wkv), (wq_exp_h, wq_exp), (wq_h, wq))
         )
     ]
     for copy in loads:
         copy.start()
-    for copy in loads[:2]:
+    for copy in loads:
         copy.wait()
-    q_out[...] = scaled(wq[...], wq_exp[...])
-    stores = [pltpu.make_async_copy(q_out, q_h, sems.at[4])]
-    stores[0].start()
-    for copy in loads[2:]:
-        copy.wait()
+    rows = wq.shape[0]
+    size, lanes = wkv.shape
     kv_out[...] = scaled(wkv[...], wkv_exp[...])
-    for n in range(kv_h.shape[0]):
-        stores.append(pltpu.make_async_copy(kv_out, kv_h.at[n], sems.at[5 + n]))
-        stores[-1].start()
+    out[rows:rows + size, :] = kv_out[:, :lanes // 2]
+    out[rows + size:, :] = kv_out[:, lanes // 2:]
+    out[:rows, :] = scaled(wq[...], wq_exp[...])
+    stores = [pltpu.make_async_copy(kv_out, kv_h, sems.at[4])]
+    for n in range(all_h.shape[0]):
+        stores.append(pltpu.make_async_copy(out, all_h.at[n], sems.at[5 + n]))
+    for copy in stores:
+        copy.start()
     for copy in stores:
         copy.wait()
 
 
 def weights(wq, wq_exp, wkv, wkv_exp, copies):
     operands = (wq, wq_exp, wkv, wkv_exp)
+    joined = (wq.shape[0] + 2 * wkv.shape[0], wq.shape[1])
     return pl.pallas_call(
         weights_kernel,
         out_shape=[
-            jax.ShapeDtypeStruct(wq.shape, jnp.bfloat16),
-            jax.ShapeDtypeStruct((copies,) + wkv.shape, jnp.bfloat16),
+            jax.ShapeDtypeStruct((copies,) + joined, jnp.bfloat16),
+            jax.ShapeDtypeStruct(wkv.shape, jnp.bfloat16),
         ],
         in_specs=[HB] * 4,
         out_specs=[HB] * 2,
         scratch_shapes=[pltpu.VMEM(a.shape, a.dtype) for a in operands]
         + [
-            pltpu.VMEM(wq.shape, jnp.bfloat16),
+            pltpu.VMEM(joined, jnp.bfloat16),
             pltpu.VMEM(wkv.shape, jnp.bfloat16),
             pltpu.SemaphoreType.DMA((5 + copies,)),
         ],
@@ -221,87 +229,97 @@
     )(*operands)
 
 
-def kv_terms(spot, sums, near, far):
-    a = lax.dot_general(sums, near, NT, preferred_element_type=jnp.float32)
-    b = lax.dot_general(sums, far, NT, preferred_element_type=jnp.float32)
-    first = spot[1] == 0
-    return jnp.concatenate([jnp.where(first, a, b), jnp.where(first, b, a)], axis=1)
-
-
-def project_kernel(spot, moved, wq, wkv, wkv_c, out, kv_out, dq_s, *, width):
+def pack_kernel(keep, came, far, far_c, out_h, out, sems):
+    width = keep.shape[3] // 3
+    tokens = keep.shape[2]
+    copies = []
+    for y in range(keep.shape[0]):
+        for slot in range(2):
+            rows = slice(slot * tokens, (slot + 1) * tokens)
+            out[y, rows, :width] = keep[y, slot, :, :width]
+            out[y, rows, width:2 * width] = came[y, slot, :, :width]
+            kv = keep[y, slot, :, width:].astype(jnp.float32) + came[y, slot, :, width:].astype(jnp.float32)
+            out[y, rows, 2 * width:] = kv.astype(jnp.bfloat16)
+        out[y, 2 * tokens:, :2 * width] = far[...]
+        out[y, 2 * tokens:, 2 * width:] = far_c[...]
+        copies.append(pltpu.make_async_copy(out.at[y], out_h.at[y], sems.at[y]))
+        copies[-1].start()
+    for copy in copies:
+        copy.wait()
+
+
+def pack(keep, came, far, far_c):
+    y, slots, tokens, lanes = keep.shape
+    packed = (y, slots * tokens + far.shape[0], lanes * 4 // 3)
+    return pl.pallas_call(
+        pack_kernel,
+        out_shape=jax.ShapeDtypeStruct(packed, jnp.bfloat16),
+        in_specs=[VM] * 4,
+        out_specs=HB,
+        scratch_shapes=[pltpu.VMEM(packed, jnp.bfloat16), pltpu.SemaphoreType.DMA((y,))],
+        compiler_params=pltpu.CompilerParams(vmem_limit_bytes=12 * 2**20),
+        name="pack",
+    )(keep, came, far, far_c)
+
+
+def project_kernel(spot, moved, wq, wq_c, out, kv_out, *, slot):
     sources = moved.shape[0]
-
-    @pl.when(pl.program_id(0) == 0)
-    def _():
-        kv_out[...] = summed(moved[:, 0, :, width:]).astype(jnp.bfloat16)
+    groups, tokens, part = out.shape
+    width = wq.shape[2]
+    size = part // 4
+    model = groups * part
+    f32 = jnp.float32
+    rows = slice(slot * tokens, (slot + 1) * tokens)
+    far_rows = slice(2 * tokens, 2 * tokens + size)
+    kv_out[...] = summed(moved[:, rows, 2 * width:]).astype(jnp.bfloat16)
+    sums = kv_out[...]
+    left = jnp.concatenate([moved[s, rows, :2 * width] for s in range(sources)], axis=1)
+    first, low = spot[1] == 0, spot[0] == 0
+
+    def kv_term(k_part, v_part):
+        rhs = jnp.concatenate([k_part, v_part], axis=1)
+        return lax.dot_general(sums, rhs, NT, preferred_element_type=f32)
+
+    def pair(a, b):
+        return jnp.concatenate([jnp.where(first, a, b), jnp.where(first, b, a)], axis=1)
+
+    for j in range(groups):
+        cols = slice(j * part, (j + 1) * part)
+        right = []
         for s in range(sources):
-            dq_s[:, s * width:(s + 1) * width] = moved[s, 0, :, :width]
-
-    acc = jnp.zeros(out.shape[1:], jnp.float32)
-    for s in range(0, sources, 2):
-        right = jnp.concatenate([wq[s], wq[s + 1]], axis=1)
-        left = dq_s[:, s * width:(s + 2) * width]
-        acc = acc + lax.dot_general(left, right, NT, preferred_element_type=jnp.float32)
-    out[0] = acc
-    pair = kv_terms(spot, kv_out[...], wkv[0], wkv_c[0])
-    cols = pl.ds(pl.multiple_of(spot[0] * pair.shape[1], pair.shape[1]), pair.shape[1])
-    out[0, :, cols] += pair
-
-
-def project(spot, slot, moved, wq, wkv, wkv_c):
-    sources, _, tokens, lanes = moved.shape
-    model = wq.shape[1]
-    groups = wkv.shape[0]
-    part = model // groups
-    width = lanes // 3
-    kv_block = pl.BlockSpec((1,) + wkv.shape[1:], lambda j: (j, 0, 0))
-    return pl.pallas_call(
-        functools.partial(project_kernel, width=width),
-        grid=(groups,),
+            right += [wq[s, cols, :], wq_c[s, cols, :]]
+        acc = lax.dot_general(left, jnp.concatenate(right, axis=1), NT, preferred_element_type=f32)
+        near = pair(*[kv_term(w[j, model:model + size, :], w[j, model + size:, :]) for w in (wq, wq_c)])
+        far = pair(
+            *[
+                kv_term(moved[j, far_rows, c:c + width], moved[j, far_rows, c + width:c + 2 * width])
+                for c in (0, 2 * width)
+            ]
+        )
+        term = jnp.concatenate([jnp.where(low, near, far), jnp.where(low, far, near)], axis=1)
+        out[j] = (acc + term).astype(jnp.bfloat16)
+
+
+def project(spot, slot, moved, wq, wq_c, tokens, model):
+    sources = moved.shape[0]
+    width = wq.shape[2]
+    groups = 4
+    return pl.pallas_call(
+        functools.partial(project_kernel, slot=slot),
         out_shape=[
-            jax.ShapeDtypeStruct((groups, tokens, part), jnp.float32),
+            jax.ShapeDtypeStruct((groups, tokens, model // groups), jnp.bfloat16),
             jax.ShapeDtypeStruct((tokens, 2 * width), jnp.bfloat16),
         ],
-        in_specs=[
-            SM,
-            pl.BlockSpec((sources, 1, tokens, lanes), lambda j: (0, slot, 0, 0)),
-            pl.BlockSpec((sources, part, width), lambda j: (0, j, 0)),
-            kv_block,
-            kv_block,
-        ],
-        out_specs=[
-            pl.BlockSpec((1, tokens, part), lambda j: (j, 0, 0)),
-            pl.BlockSpec((tokens, 2 * width), lambda j: (0, 0)),
-        ],
-        scratch_shapes=[pltpu.VMEM((tokens, sources * width), jnp.bfloat16)],
-        compiler_params=pltpu.CompilerParams(vmem_limit_bytes=BIG),
+        in_specs=[SM] + [VM] * 3,
+        out_specs=[VM] * 2,
+        compiler_params=pltpu.CompilerParams(vmem_limit_bytes=16 * 2**20),
         cost_estimate=pl.CostEstimate(
-            flops=2 * tokens * model * (sources + 1) * width,
+            flops=2 * tokens * model * (2 * sources + 2) * width,
             bytes_accessed=8 * 2**20,
             transcendentals=0,
         ),
         name="project",
-    )(spot, moved, wq, wkv, wkv_c)
-
-
-def complete_kernel(spot, acc, sums, wkv, wkv_c, out):
-    out[...] = acc[...].astype(out.dtype)
-    for j in range(acc.shape[0]):
-        pair = kv_terms(spot, sums[...], wkv[j], wkv_c[j])
-        size = pair.shape[1]
-        cols = pl.ds(pl.multiple_of((1 - spot[0]) * size, size), size)
-        out[j, :, cols] = (acc[j, :, cols] + pair).astype(out.dtype)
-
-
-def complete(spot, acc, sums, wkv, wkv_c):
-    return pl.pallas_call(
-        complete_kernel,
-        out_shape=jax.ShapeDtypeStruct(acc.shape, jnp.bfloat16),
-        in_specs=[SM] + [VM] * 4,
-        out_specs=VM,
-        compiler_params=pltpu.CompilerParams(vmem_limit_bytes=16 * 2**20),
-        name="complete",
-    )(spot, acc, sums, wkv, wkv_c)
+    )(spot, moved, wq, wq_c)
 
 
 def summed(terms):
@@ -353,24 +371,26 @@
 def shards(query, query_exp, kv, kv_exp, out_grad, out_grad_exp, q_weight, q_weight_exp, kv_weight, kv_weight_exp):
     swap = [(0, 1), (1, 0)]
     spot = jnp.stack([lax.axis_index("zh"), lax.axis_index("core")]).astype(jnp.int32)
-    wq, wkv = weights(q_weight, q_weight_exp, kv_weight, kv_weight_exp, 4)
-    wq_all = lax.all_gather(wq, ("y", "core"), axis=0)
-    wkv = lax.all_to_all(wkv, "y", 0, 0)
-    grads = attention(spot, query, query_exp, kv, kv_exp, out_grad, out_grad_exp)
-    wkv, grads = lax.optimization_barrier((wkv, grads))
-    wkv_c = lax.ppermute(wkv, "core", swap)
-    wkv_z = lax.ppermute(wkv, "zh", swap)
-    moved = lax.all_to_all(grads, ("y", "core"), 0, 0)
-    wkv_zc = lax.ppermute(wkv_z, "core", swap)
-    acc, kv_other = project(spot, 0, moved, wq_all, wkv, wkv_c)
-    other = lax.all_to_all(complete(spot, acc, kv_other, wkv_z, wkv_zc), "x", 0, 0)
-    acc, kv_own = project(spot, 1, moved, wq_all, wkv, wkv_c)
-    own = complete(spot, acc, kv_own, wkv_z, wkv_zc)
+    model = q_weight.shape[0]
+    w_all, wkv = weights(q_weight, q_weight_exp, kv_weight, kv_weight_exp, 4)
+    w_all = lax.all_to_all(w_all, "y", 0, 0)
+    far = lax.ppermute(wkv, "zh", swap)
+    keep, send = attention(spot, query, query_exp, kv, kv_exp, out_grad, out_grad_exp)
+    came = lax.ppermute(send, "core", swap)
+    far_c = lax.ppermute(far, "core", swap)
+    packed = pack(keep, came, far, far_c)
+    packed, w_all = lax.optimization_barrier((packed, w_all))
+    moved = lax.all_to_all(packed, "y", 0, 0)
+    w_all_c = lax.ppermute(w_all, "core", swap)
+    tokens = keep.shape[2]
+    other, kv_other = project(spot, 0, moved, w_all, w_all_c, tokens, model)
+    other = lax.all_to_all(other, "x", 0, 0)
+    own, kv_own = project(spot, 1, moved, w_all, w_all_c, tokens, model)
     sent = gather(other, kv_other)
     own, sent = lax.optimization_barrier((own, sent))
-    far = lax.ppermute(sent, "zh", swap)
+    far_terms = lax.ppermute(sent, "zh", swap)
     own = lax.all_to_all(own, "x", 0, 0)
-    return tuple(finish(own, kv_own, far))
+    return tuple(finish(own, kv_own, far_terms))
 
 
 def solution(mesh):

time: 141 us -> 130 us (0.922)
  blocking collectives: 0 us -> 24.9 us
  waiting for transfers between devices: 39.4 us -> 22.8 us
  between operations: 14.2 us -> 0.74 us
  Pallas kernels: 30.8 us -> 24.7 us
    all_to_all x0 -> x1, blocking collectives: none -> 24.9 us  [shards(): moved = lax.all_to_all(packed, 'y', 0, 0)]
    ppermute x4 -> x5, waiting for transfers between devices: 39.4 us -> 22.5 us  [the longest x1 17.8 us: shards(): far_terms = lax.ppermute(sent, 'zh', swap)]
    pallas_call x5 -> x4, Pallas kernels: 16.3 us -> 10.1 us  [the longest x2 6.25 us: project(): pl.pallas_call(functools.partial(project_kernel, slot=slot), out_shape=[j...]
    ppermute x4 -> x5, starting transfers between devices: 31.2 us -> 37 us  [the longest x1 14.7 us: shards(): far_terms = lax.ppermute(sent, 'zh', swap)]
    all_to_all x3 -> x2, starting transfers between devices: 14.2 us -> 8.46 us  [the longest x1 4.26 us: shards(): other = lax.all_to_all(other, 'x', 0, 0)]
    unnamed x22 -> x16, local copies, waits for them, and re-layouts: 5.38 us -> 5.36 us
  transfers between devices with their start and end apart: 9 -> 8, of which waited for: 2 -> 4; matrix products, arithmetic and copies ran while one was open for 0% -> 0% of each run, Pallas kernels for 19% -> 14%
where the time goes in v4:
time: 130 us; the launch traced here: 129 us
  starting transfers between devices  50.1 us (39%)
  blocking collectives  24.9 us (19%)
  Pallas kernels  24.7 us (19%)
  waiting for transfers between devices  22.8 us (18%)
  local copies, waits for them, and re-layouts  5.36 us (4%)
    all_to_all x1, blocking collectives, shards(): moved = lax.all_to_all(packed, 'y', 0, 0)  24.9 us
    ppermute x1, waiting for transfers between devices, shards(): far_terms = lax.ppermute(sent, 'zh', swap)  17.8 us
    ppermute x1, starting transfers between devices, shards(): far_terms = lax.ppermute(sent, 'zh', swap)  14.7 us
    ppermute x1, starting transfers between devices, shards(): far = lax.ppermute(wkv, 'zh', swap)  14.5 us
    pallas_call x1, Pallas kernels, attention(): pl.pallas_call(functools.partial(attention_kernel, block=block, tile=tile...  13.8 us
    pallas_call x2, Pallas kernels, project(): pl.pallas_call(functools.partial(project_kernel, slot=slot), out_shape=[j...  6.25 us
    unnamed x16, local copies, waits for them, and re-layouts  5.36 us
    all_to_all x1, starting transfers between devices, shards(): own = lax.all_to_all(own, 'x', 0, 0)  4.63 us
  transfers between devices with their start and end apart: 8, of which 4 were waited for; matrix products, arithmetic and copies ran while one was open for 0% of the time, Pallas kernels for 14%

profile of v4, /device:TPU:35, one launch (start us, length us, event | category | flops | bytes accessed | tf_op | source)
XLA Modules:
  0.0 129.2 jit_solution(3299101518086352055)
XLA Ops:
  0.6 2.8 %weights.1 = (bf16[4,2304,128]{2,1,0:T(8,128)(2,1)}, bf16[128,256]{1,0:T(8,128)(2,1)}) custom-call(bf16[2048,128]{1,0:T(8,128)(2,1)} %wq_h.1, s32[64,128]{1,0:T(8,128)} %wq_exp_h.1, bf16[128,256]{1,0:T(8,128)(2,1)} %wkv_h.1, s32[4,256]{1,0:T(4,128)} %wkv_exp_h.1), custom_call_target="tpu_custom_call" | custom-call | tf_op jit(solution)/shard_map/weights/pallas_call | solution.py:213
  3.5 4.2 %all-to-all-start = ((bf16[4,2304,128]{2,1,0:T(8,128)(2,1)}), bf16[4,2304,128]{2,1,0:T(8,128)(2,1)S(1)}, u32[]{:S(2)}, u32[]{:S(2)}) async-start(bf16[4,2304,128]{2,1,0:T(8,128)(2,1)} %get-tuple-element.17), calls=%async_computation | async-start | bytes 4718592 | tf_op jit(solution)/shard_map/all_to_all | solution.py:376
  7.7 0.6 pad_add_fusion.place_s.spot
  8.2 0.0 copy-start.7
  8.2 13.8 %attention.1 = (bf16[4,2,128,384]{3,2,1,0:T(8,128)(2,1)}, bf16[4,2,128,384]{3,2,1,0:T(8,128)(2,1)}) custom-call(s32[2]{0:T(128)} %pad_add_fusion.place_s.spot, bf16[2048,128]{1,0:T(8,128)(2,1)} %query_h.1, s32[4,2048]{1,0:T(4,128)} %q_exp_h.1, bf16[2048,256]{1,0:T(8,128)(2,1)} %kv_h.1, s32[8,2048]{1,0:T(8,128)} %kv_exp_h.1, bf16[2048,128]{1,0:T(8,128)(2,1)} %grad_h.1, ...), custom_call_target="tpu_custom_call" | custom-call | flops 16000000000 | bytes 6291456 | tf_op jit(solution)/shard_map/attention/pallas_call | solution.py:150
  22.1 2.9 %collective-permute-start = (bf16[4,2,128,384]{3,2,1,0:T(8,128)(2,1)}, bf16[4,2,128,384]{3,2,1,0:T(8,128)(2,1)S(1)}, u32[]{:S(2)}, u32[]{:S(2)}) collective-permute-start(bf16[4,2,128,384]{3,2,1,0:T(8,128)(2,1)} %get-tuple-element.15), channel_id=1, source_target_pairs={{0,1},{1,0},{2,3},{3,2},{4,5},{5,4},{6,7},{7,6},{8,9},{9,8},{10,11... | collective-permute-start | bytes 2359304 | tf_op jit(solution)/shard_map/ppermute | solution.py:379
  25.0 0.0 copy-done.7
  25.0 14.5 %collective-permute-start.1 = (bf16[128,256]{1,0:T(8,128)(2,1)S(1)}, bf16[128,256]{1,0:T(8,128)(2,1)S(1)}, u32[]{:S(2)}, u32[]{:S(2)}) collective-permute-start(bf16[128,256]{1,0:T(8,128)(2,1)S(1)} %copy-done.7), channel_id=1, source_target_pairs={{0,2},{2,0},{1,3},{3,1},{4,6},{6,4},{5,7},{7,5},{8,10},{10,8},{9,1... | collective-permute-start | bytes 196616 | tf_op jit(solution)/shard_map/ppermute | solution.py:377
  39.5 3.8 %collective-permute-done.1.far = bf16[128,256]{1,0:T(8,128)(2,1)S(1)} collective-permute-done((bf16[128,256]{1,0:T(8,128)(2,1)S(1)}, bf16[128,256]{1,0:T(8,128)(2,1)S(1)}, u32[]{:S(2)}, u32[]{:S(2)}) %collective-permute-start.1) | collective-permute-done | bytes 65568 | tf_op jit(solution)/shard_map/ppermute | solution.py:377
  43.4 2.7 %collective-permute-start.2 = (bf16[128,256]{1,0:T(8,128)(2,1)S(1)}, bf16[128,256]{1,0:T(8,128)(2,1)S(1)}, u32[]{:S(2)}, u32[]{:S(2)}) collective-permute-start(bf16[128,256]{1,0:T(8,128)(2,1)S(1)} %collective-permute-done.1.far), channel_id=1, source_target_pairs={{0,1},{1,0},{2,3},{3,2},{4,5},{5,4},{6,7},{7,6},{8,9},{9,8},{10,11... | collective-permute-start | bytes 196616 | tf_op jit(solution)/shard_map/ppermute | solution.py:380
  46.1 0.9 collective-permute-done.2.far_c
  47.0 0.0 collective-permute-done.came
  47.0 0.0 copy-start.5
  47.0 1.1 copy-done.5
  48.1 1.0 pack.1
  49.1 0.0 copy-start.4
  49.1 1.1 copy-done.4
  50.3 0.0 copy-start.6
  50.3 0.0 all-to-all-done.wq
  50.3 2.2 %collective-permute-start.3 = (bf16[4,2304,128]{2,1,0:T(8,128)(2,1)S(1)}, bf16[4,2304,128]{2,1,0:T(8,128)(2,1)S(1)}, u32[]{:S(2)}, u32[]{:S(2)}) collective-permute-start(bf16[4,2304,128]{2,1,0:T(8,128)(2,1)S(1)} %all-to-all-done.wq), channel_id=1, source_target_pairs={{0,1},{1,0},{2,3},{3,2},{4,5},{5,4},{6,7},{7,6},{8,9},{9,8},{10,11... | collective-permute-start | bytes 7077896 | tf_op jit(solution)/shard_map/ppermute | solution.py:384
  52.5 24.9 %all_to_all.20.moved = bf16[4,384,512]{2,1,0:T(8,128)(2,1)S(1)} all-to-all(bf16[4,384,512]{2,1,0:T(8,128)(2,1)} %copy-done.4), channel_id=1, replica_groups=mesh['dp'=8,'x'=4,'y'=4,'zh'=2,'core'=2] {'y'}, dimensions={0} | all-to-all | bytes 3145728 | tf_op jit(solution)/shard_map/all_to_all | solution.py:383
  77.4 0.0 copy-start
  77.4 0.0 collective-permute-done.3.wq_c
  77.4 0.0 copy-done.6
  77.4 0.0 copy-start.2
  77.5 3.1 %project.3 = (bf16[4,128,512]{2,1,0:T(8,128)(2,1)}, bf16[128,256]{1,0:T(8,128)(2,1)S(1)}) custom-call(s32[2]{0:T(128)S(1)} %copy-done.6, bf16[4,384,512]{2,1,0:T(8,128)(2,1)S(1)} %all_to_all.20.moved, bf16[4,2304,128]{2,1,0:T(8,128)(2,1)S(1)} %all-to-all-done.wq, bf16[4,2304,128]{2,1,0:T(8,128)(2,1)S(1)} %collective-permute-done.3.wq_c), custom_call_target="tpu_custom_call" | custom-call | flops 671088640 | bytes 8388608 | tf_op jit(solution)/shard_map/project/pallas_call | solution.py:307
  80.6 0.0 copy-done
  80.6 0.0 copy-done.2
  80.6 4.3 %all-to-all-start.2 = ((bf16[4,128,512]{2,1,0:T(8,128)(2,1)}), bf16[4,128,512]{2,1,0:T(8,128)(2,1)S(1)}, u32[]{:S(2)}, u32[]{:S(2)}) async-start(bf16[4,128,512]{2,1,0:T(8,128)(2,1)} %get-tuple-element.21), calls=%async_computation.2 | async-start | bytes 1048576 | tf_op jit(solution)/shard_map/all_to_all | solution.py:387
  84.8 0.0 copy-start.1
  84.8 1.4 %copy-done.1 = bf16[4,384,512]{2,1,0:T(8,128)(2,1)S(1)} copy-done((bf16[4,384,512]{2,1,0:T(8,128)(2,1)S(1)}, bf16[4,384,512]{2,1,0:T(8,128)(2,1)}, u32[]{:S(2)}) %copy-start.1) | copy-done | bytes 1572888
  86.3 0.0 copy-start.3
  86.3 1.7 %copy-done.3 = bf16[4,2304,128]{2,1,0:T(8,128)(2,1)S(1)} copy-done((bf16[4,2304,128]{2,1,0:T(8,128)(2,1)S(1)}, bf16[4,2304,128]{2,1,0:T(8,128)(2,1)}, u32[]{:S(2)}) %copy-start.3) | copy-done | bytes 2359320
  87.9 3.1 %project.2 = (bf16[4,128,512]{2,1,0:T(8,128)(2,1)}, bf16[128,256]{1,0:T(8,128)(2,1)S(1)}) custom-call(s32[2]{0:T(128)S(1)} %copy-done.6, bf16[4,384,512]{2,1,0:T(8,128)(2,1)S(1)} %copy-done.1, bf16[4,2304,128]{2,1,0:T(8,128)(2,1)S(1)} %all-to-all-done.wq, bf16[4,2304,128]{2,1,0:T(8,128)(2,1)S(1)} %copy-done.3), custom_call_target="tpu_custom_call" | custom-call | flops 671088640 | bytes 8388608 | tf_op jit(solution)/shard_map/project/pallas_call | solution.py:307
  91.1 0.3 all-to-all-done.2.terms
  91.3 0.1 gather.1
  91.4 4.6 %all-to-all-start.3 = ((bf16[4,128,512]{2,1,0:T(8,128)(2,1)}), bf16[4,128,512]{2,1,0:T(8,128)(2,1)S(1)}, u32[]{:S(2)}, u32[]{:S(2)}) async-start(bf16[4,128,512]{2,1,0:T(8,128)(2,1)} %get-tuple-element.23), calls=%async_computation.3 | async-start | bytes 1048576 | tf_op jit(solution)/shard_map/all_to_all | solution.py:392
  96.0 14.7 %collective-permute-start.4 = (bf16[128,768]{1,0:T(8,128)(2,1)S(1)}, bf16[128,768]{1,0:T(8,128)(2,1)S(1)}, u32[]{:S(2)}, u32[]{:S(2)}) collective-permute-start(bf16[128,768]{1,0:T(8,128)(2,1)S(1)} %gather.1), channel_id=1, source_target_pairs={{0,2},{2,0},{1,3},{3,1},{4,6},{6,4},{5,7},{7,5},{8,10},{10,8},{9,1... | collective-permute-start | bytes 589832 | tf_op jit(solution)/shard_map/ppermute | solution.py:391
  110.7 17.8 %collective-permute-done.4.far = bf16[128,768]{1,0:T(8,128)(2,1)S(1)} collective-permute-done((bf16[128,768]{1,0:T(8,128)(2,1)S(1)}, bf16[128,768]{1,0:T(8,128)(2,1)S(1)}, u32[]{:S(2)}, u32[]{:S(2)}) %collective-permute-start.4) | collective-permute-done | bytes 196640 | tf_op jit(solution)/shard_map/ppermute | solution.py:391
  128.5 0.0 all-to-all-done.3.terms
  128.5 0.8 finish.1
Async XLA Ops:
  3.5 46.8 %all-to-all-start = ((bf16[4,2304,128]{2,1,0:T(8,128)(2,1)}), bf16[4,2304,128]{2,1,0:T(8,128)(2,1)S(1)}, u32[]{:S(2)}, u32[]{:S(2)}) async-start(bf16[4,2304,128]{2,1,0:T(8,128)(2,1)} %get-tuple-element.17), calls=%async_computation | async-start | bytes 4718592 | tf_op jit(solution)/shard_map/all_to_all | solution.py:376
  8.2 16.7 %copy-start.7 = (bf16[128,256]{1,0:T(8,128)(2,1)S(1)}, bf16[128,256]{1,0:T(8,128)(2,1)}, u32[]{:S(2)}) copy-start(bf16[128,256]{1,0:T(8,128)(2,1)} %get-tuple-element.16) | copy-start | bytes 196612
  22.1 24.9 %collective-permute-start = (bf16[4,2,128,384]{3,2,1,0:T(8,128)(2,1)}, bf16[4,2,128,384]{3,2,1,0:T(8,128)(2,1)S(1)}, u32[]{:S(2)}, u32[]{:S(2)}) collective-permute-start(bf16[4,2,128,384]{3,2,1,0:T(8,128)(2,1)} %get-tuple-element.15), channel_id=1, source_target_pairs={{0,1},{1,0},{2,3},{3,2},{4,5},{5,4},{6,7},{7,6},{8,9},{9,8},{10,11... | collective-permute-start | bytes 2359304 | tf_op jit(solution)/shard_map/ppermute | solution.py:379
  25.0 18.4 %collective-permute-start.1 = (bf16[128,256]{1,0:T(8,128)(2,1)S(1)}, bf16[128,256]{1,0:T(8,128)(2,1)S(1)}, u32[]{:S(2)}, u32[]{:S(2)}) collective-permute-start(bf16[128,256]{1,0:T(8,128)(2,1)S(1)} %copy-done.7), channel_id=1, source_target_pairs={{0,2},{2,0},{1,3},{3,1},{4,6},{6,4},{5,7},{7,5},{8,10},{10,8},{9,1... | collective-permute-start | bytes 196616 | tf_op jit(solution)/shard_map/ppermute | solution.py:377
  43.4 3.6 %collective-permute-start.2 = (bf16[128,256]{1,0:T(8,128)(2,1)S(1)}, bf16[128,256]{1,0:T(8,128)(2,1)S(1)}, u32[]{:S(2)}, u32[]{:S(2)}) collective-permute-start(bf16[128,256]{1,0:T(8,128)(2,1)S(1)} %collective-permute-done.1.far), channel_id=1, source_target_pairs={{0,1},{1,0},{2,3},{3,2},{4,5},{5,4},{6,7},{7,6},{8,9},{9,8},{10,11... | collective-permute-start | bytes 196616 | tf_op jit(solution)/shard_map/ppermute | solution.py:380
  47.0 1.1 copy-start.5
  49.1 1.1 copy-start.4
  50.3 27.2 %copy-start.6 = (s32[2]{0:T(128)S(1)}, s32[2]{0:T(128)}, u32[]{:S(2)}) copy-start(s32[2]{0:T(128)} %pad_add_fusion.place_s.spot) | copy-start | bytes 28
  50.3 27.2 %collective-permute-start.3 = (bf16[4,2304,128]{2,1,0:T(8,128)(2,1)S(1)}, bf16[4,2304,128]{2,1,0:T(8,128)(2,1)S(1)}, u32[]{:S(2)}, u32[]{:S(2)}) collective-permute-start(bf16[4,2304,128]{2,1,0:T(8,128)(2,1)S(1)} %all-to-all-done.wq), channel_id=1, source_target_pairs={{0,1},{1,0},{2,3},{3,2},{4,5},{5,4},{6,7},{7,6},{8,9},{9,8},{10,11... | collective-permute-start | bytes 7077896 | tf_op jit(solution)/shard_map/ppermute | solution.py:384
  77.4 3.1 %copy-start = (bf16[4,384,512]{2,1,0:T(8,128)(2,1)}, bf16[4,384,512]{2,1,0:T(8,128)(2,1)S(1)}, u32[]{:S(2)}) copy-start(bf16[4,384,512]{2,1,0:T(8,128)(2,1)S(1)} %all_to_all.20.moved) | copy-start | bytes 4718596
  77.4 3.1 %copy-start.2 = (bf16[4,2304,128]{2,1,0:T(8,128)(2,1)}, bf16[4,2304,128]{2,1,0:T(8,128)(2,1)S(1)}, u32[]{:S(2)}) copy-start(bf16[4,2304,128]{2,1,0:T(8,128)(2,1)S(1)} %collective-permute-done.3.wq_c) | copy-start | bytes 7077892
  80.6 10.7 %all-to-all-start.2 = ((bf16[4,128,512]{2,1,0:T(8,128)(2,1)}), bf16[4,128,512]{2,1,0:T(8,128)(2,1)S(1)}, u32[]{:S(2)}, u32[]{:S(2)}) async-start(bf16[4,128,512]{2,1,0:T(8,128)(2,1)} %get-tuple-element.21), calls=%async_computation.2 | async-start | bytes 1048576 | tf_op jit(solution)/shard_map/all_to_all | solution.py:387
  84.8 1.4 %copy-start.1 = (bf16[4,384,512]{2,1,0:T(8,128)(2,1)S(1)}, bf16[4,384,512]{2,1,0:T(8,128)(2,1)}, u32[]{:S(2)}) copy-start(bf16[4,384,512]{2,1,0:T(8,128)(2,1)} %copy-done) | copy-start | bytes 4718596
  86.3 1.7 %copy-start.3 = (bf16[4,2304,128]{2,1,0:T(8,128)(2,1)S(1)}, bf16[4,2304,128]{2,1,0:T(8,128)(2,1)}, u32[]{:S(2)}) copy-start(bf16[4,2304,128]{2,1,0:T(8,128)(2,1)} %copy-done.2) | copy-start | bytes 7077892
  91.4 37.1 %all-to-all-start.3 = ((bf16[4,128,512]{2,1,0:T(8,128)(2,1)}), bf16[4,128,512]{2,1,0:T(8,128)(2,1)S(1)}, u32[]{:S(2)}, u32[]{:S(2)}) async-start(bf16[4,128,512]{2,1,0:T(8,128)(2,1)} %get-tuple-element.23), calls=%async_computation.3 | async-start | bytes 1048576 | tf_op jit(solution)/shard_map/all_to_all | solution.py:392
  96.0 32.4 %collective-permute-start.4 = (bf16[128,768]{1,0:T(8,128)(2,1)S(1)}, bf16[128,768]{1,0:T(8,128)(2,1)S(1)}, u32[]{:S(2)}, u32[]{:S(2)}) collective-permute-start(bf16[128,768]{1,0:T(8,128)(2,1)S(1)} %gather.1), channel_id=1, source_target_pairs={{0,2},{2,0},{1,3},{3,1},{4,6},{6,4},{5,7},{7,5},{8,10},{10,8},{9,1... | collective-permute-start | bytes 589832 | tf_op jit(solution)/shard_map/ppermute | solution.py:391

commit v5 on v4

v5 whole, which is shorter than its diff:
```python
import functools, math
import jax, jax.numpy as jnp
from jax import lax
from jax.experimental import pallas as pl
from jax.experimental.pallas import tpu as pltpu
from jax.sharding import Mesh, PartitionSpec as P

HB = pl.BlockSpec(memory_space=pltpu.HBM)
VM = pl.BlockSpec(memory_space=pltpu.VMEM)
SM = pl.BlockSpec(memory_space=pltpu.SMEM)
BIG = 58 * 2**20
FULL = 60 * 2**20
NT = (((1,), (1,)), ((), ()))
NN = (((1,), (0,)), ((), ()))


def power(exps):
    return lax.shift_left(jnp.ones_like(exps), exps + 4).astype(jnp.float32) * 0.0625


def fold(x, op):
    rows = x.shape[0]
    while rows > 8:
        rows //= 2
        x = op(x[:rows], x[rows:])
    return x


def attention_kernel(place_s, query_h, q_exp_h, kv_h, kv_exp_h, grad_h, grad_exp_h, keep, send, query, q_exp, kv, kv_exp, grad, grad_exp, out, sems, q_s, k_s, v_s, do_s, kt_s, s_s, dp_s, ds_s, dk_s, dv_s, *, block, tile):
    seq, width = query.shape
    count = seq // block
    blocks = [slice(index * block, (index + 1) * block) for index in range(count)]
    pairs = [(kv_exp_h, kv_exp), (q_exp_h, q_exp), (grad_exp_h, grad_exp), (kv_h, kv)]
    for rows in reversed(blocks):
        pairs += [(query_h.at[rows], query.at[rows]), (grad_h.at[rows], grad.at[rows])]
    loads = [pltpu.make_async_copy(*pair, sems.at[n]) for n, pair in enumerate(pairs)]
    for copy in loads:
        copy.start()
    scale = 1.0 / math.sqrt(width)
    coef = scale * math.log2(math.e)
    for copy in loads[:3]:
        copy.wait()
    exps = jnp.concatenate([q_exp[...], grad_exp[...], kv_exp[...]], axis=0)
    parts = exps.shape[0]
    powers = power(exps).T.astype(jnp.bfloat16)
    row_at = lax.broadcasted_iota(jnp.int32, (parts, parts * 32), 0)
    col_at = lax.broadcasted_iota(jnp.int32, (parts, parts * 32), 1)
    spread = jnp.where(col_at // 32 == row_at, 1.0, 0.0).astype(jnp.bfloat16)

    def scales(rows, low, high):
        return lax.dot_general(
            powers[rows], spread[:, low * width:high * width], NN, preferred_element_type=jnp.float32
        )

    loads[3].wait()
    for rows in blocks:
        both = kv[rows, :].astype(jnp.float32) * scales(rows, 2, 4)
        k_s[rows, :] = both[:, :width].astype(jnp.bfloat16)
        kt_s[:, rows] = both[:, :width].T.astype(jnp.bfloat16)
        v_s[rows, :] = both[:, width:].astype(jnp.bfloat16)

    def fetch(index):
        at = 4 + 2 * (count - 1 - index)
        rows = blocks[index]
        both = scales(rows, 0, 2)
        loads[at].wait()
        q_s[rows, :] = (query[rows, :].astype(jnp.float32) * both[:, :width]).astype(jnp.bfloat16)
        loads[at + 1].wait()
        do_s[rows, :] = (grad[rows, :].astype(jnp.float32) * both[:, width:]).astype(jnp.bfloat16)

    sub = block // tile
    stores = []

    def tiles_of(index):
        return [(t, max(0, t - index * sub) * tile) for t in range((index + 1) * sub)]

    def scores(index, t, low, peak):
        slot = index % 2
        q_b = q_s[index * block + low:(index + 1) * block, :]
        do_b = do_s[index * block + low:(index + 1) * block, :]
        ks = slice(t * tile, (t + 1) * tile)
        s = lax.dot_general(k_s[ks, :], q_b, NT, preferred_element_type=jnp.float32)
        if t >= index * sub:
            key = lax.broadcasted_iota(jnp.int32, (tile, tile), 0)
            row = lax.broadcasted_iota(jnp.int32, (tile, tile), 1)
            head = jnp.where(key <= row, s[:, :tile], -jnp.inf)
            s = jnp.concatenate([head, s[:, tile:]], axis=1) if low + tile < block else head
        s_s[slot, ks, low:] = s
        dp_s[slot, ks, low:] = lax.dot_general(
            v_s[ks, :], do_b, NT, preferred_element_type=jnp.float32
        )
        return merge(peak, fold(s, jnp.maximum), low, jnp.maximum)

    def merge(total, part, low, op):
        if not low:
            return op(total, part)
        return jnp.concatenate([total[:, :low], op(total[:, low:], part)], axis=1)

    lowest = jnp.full((8, block), -jnp.inf, jnp.float32)
    peak = lowest
    fetch(count - 1)
    for t, low in tiles_of(count - 1):
        peak = scores(count - 1, t, low, peak)
    for index in reversed(range(count)):
        first = index * block
        slot = index % 2
        tiles = tiles_of(index)
        peak = jnp.max(peak, axis=0, keepdims=True)
        total = jnp.zeros((8, block), jnp.float32)
        inner = jnp.zeros((8, block), jnp.float32)
        for t, low in tiles:
            ks = slice(t * tile, (t + 1) * tile)
            e = jnp.exp2((s_s[slot, ks, low:] - peak[:, low:]) * coef)
            s_s[slot, ks, low:] = e
            total = merge(total, fold(e, jnp.add), low, jnp.add)
            inner = merge(inner, fold(e * dp_s[slot, ks, low:], jnp.add), low, jnp.add)
        norm = 1.0 / jnp.sum(total, axis=0, keepdims=True)
        delta = jnp.sum(inner, axis=0, keepdims=True) * norm
        coming = tiles_of(index - 1) if index else []
        if index:
            fetch(index - 1)
        peak = lowest
        for at in range(max(len(tiles), len(coming))):
            if at < len(coming):
                peak = scores(index - 1, *coming[at], peak)
            if at >= len(tiles):
                continue
            t, low = tiles[at]
            ks = slice(t * tile, (t + 1) * tile)
            q_b = q_s[first + low:first + block, :]
            do_b = do_s[first + low:first + block, :]
            p = s_s[slot, ks, low:] * norm[:, low:]
            pb = p.astype(jnp.bfloat16)
            ds = (p * (dp_s[slot, ks, low:] - delta[:, low:])).astype(jnp.bfloat16)
            if low:
                ds_s[ks, :low] = jnp.zeros((tile, low), jnp.bfloat16)
            ds_s[ks, low:] = ds
            dv = lax.dot_general(pb, do_b, NN, preferred_element_type=jnp.float32)
            dk = lax.dot_general(ds, q_b, NN, preferred_element_type=jnp.float32)
            if index == count - 1:
                dv_s[ks, :] = dv
                dk_s[ks, :] = dk
            else:
                dv_s[ks, :] += dv
                dk_s[ks, :] += dk
        upper = first + block
        dq = lax.dot_general(kt_s[:, :upper], ds_s[:upper, :], NN, preferred_element_type=jnp.float32)
        dq = ((dq * scale).T).astype(jnp.bfloat16)
        dk = (dk_s[first:upper, :] * scale).astype(jnp.bfloat16)
        dv = dv_s[first:upper, :].astype(jnp.bfloat16)
        place(out, place_s, first, jnp.concatenate([dq, dk, dv], axis=1))
        part = block // (4 * out.shape[3])
        for mine, target in ((0, send), (1, keep)):
            rows = slice(index * part, (index + 1) * part)
            stores.append(
                pltpu.make_async_copy(
                    out.at[mine, rows], target.at[rows], sems.at[len(loads) + len(stores)]
                )
            )
            stores[-1].start()
    for copy in stores:
        copy.wait()


def place(out, spot, first, value):
    piece = out.shape[3]
    for j in range(value.shape[0] // piece):
        h = first // piece + j
        y, z, c = h // 4, (h // 2) % 2, h % 2
        mine = jnp.where(spot[1] == c, 1, 0)
        slot = jnp.where(spot[0] == z, 1, 0)
        out[mine, y, slot] = value[j * piece:(j + 1) * piece]


def attention(spot, query, q_exp, kv, kv_exp, grad, grad_exp, block=512, tile=256):
    seq, width = query.shape
    f32, b16 = jnp.float32, jnp.bfloat16
    sent = (4, 2, seq // 16, 3 * width)
    operands = (query, q_exp, kv, kv_exp, grad, grad_exp)
    return pl.pallas_call(
        functools.partial(attention_kernel, block=block, tile=tile),
        out_shape=[jax.ShapeDtypeStruct(sent, b16)] * 2,
        in_specs=[SM] + [HB] * 6,
        out_specs=[HB] * 2,
        scratch_shapes=[pltpu.VMEM(a.shape, a.dtype) for a in operands]
        + [
            pltpu.VMEM((2,) + sent, b16),
            pltpu.SemaphoreType.DMA((4 + 4 * (seq // block),)),
            pltpu.VMEM((seq, width), b16),
            pltpu.VMEM((seq, width), b16),
            pltpu.VMEM((seq, width), b16),
            pltpu.VMEM((seq, width), b16),
            pltpu.VMEM((width, seq), b16),
            pltpu.VMEM((2, seq, block), f32),
            pltpu.VMEM((2, seq, block), f32),
            pltpu.VMEM((seq, block), b16),
            pltpu.VMEM((seq, width), f32),
            pltpu.VMEM((seq, width), f32),
        ],
        compiler_params=pltpu.CompilerParams(vmem_limit_bytes=FULL),
        cost_estimate=pl.CostEstimate(
            flops=3 * 10**9, bytes_accessed=6 * 2**20, transcendentals=2 * 10**6
        ),
        name="attention",
    )(spot, *operands)


def scaled(mantissa, exps):
    rows, cols = mantissa.shape
    blocks = mantissa.astype(jnp.float32).reshape(rows // 32, 32, cols)
    return (blocks * power(exps)[:, None, :]).reshape(rows, cols).astype(jnp.bfloat16)


def weights_kernel(wq_h, wq_exp_h, wkv_h, wkv_exp_h, all_h, wq, wq_exp, wkv, wkv_exp, out, sems):
    loads = [
        pltpu.make_async_copy(source, target, sems.at[n])
        for n, (source, target) in enumerate(
            ((wkv_exp_h, wkv_exp), (wkv_h, wkv), (wq_exp_h, wq_exp), (wq_h, wq))
        )
    ]
    for copy in loads:
        copy.start()
    for copy in loads:
        copy.wait()
    rows = wq.shape[0]
    size, lanes = wkv.shape
    kv = scaled(wkv[...], wkv_exp[...])
    out[rows:rows + size, :] = kv[:, :lanes // 2]
    out[rows + size:, :] = kv[:, lanes // 2:]
    out[:rows, :] = scaled(wq[...], wq_exp[...])
    stores = [
        pltpu.make_async_copy(out, all_h.at[n], sems.at[4 + n]) for n in range(all_h.shape[0])
    ]
    for copy in stores:
        copy.start()
    for copy in stores:
        copy.wait()


def weights(wq, wq_exp, wkv, wkv_exp, copies):
    operands = (wq, wq_exp, wkv, wkv_exp)
    joined = (wq.shape[0] + 2 * wkv.shape[0], wq.shape[1])
    return pl.pallas_call(
        weights_kernel,
        out_shape=jax.ShapeDtypeStruct((copies,) + joined, jnp.bfloat16),
        in_specs=[HB] * 4,
        out_specs=HB,
        scratch_shapes=[pltpu.VMEM(a.shape, a.dtype) for a in operands]
        + [
            pltpu.VMEM(joined, jnp.bfloat16),
            pltpu.SemaphoreType.DMA((4 + copies,)),
        ],
        compiler_params=pltpu.CompilerParams(vmem_limit_bytes=FULL),
        name="weights",
    )(*operands)


def pack_kernel(keep, came, kv_h, dq_h, kv_out, dq_out, sems):
    width = keep.shape[3] // 3
    tokens = keep.shape[2]
    copies = []
    for y in range(keep.shape[0]):
        for slot in range(2):
            rows = slice(slot * tokens, (slot + 1) * tokens)
            kv = keep[y, slot, :, width:].astype(jnp.float32) + came[y, slot, :, width:].astype(jnp.float32)
            kv_out[y, rows, :] = kv.astype(jnp.bfloat16)
            dq_out[y, rows, :width] = keep[y, slot, :, :width]
            dq_out[y, rows, width:] = came[y, slot, :, :width]
        for out, out_h in ((kv_out, kv_h), (dq_out, dq_h)):
            copies.append(pltpu.make_async_copy(out.at[y], out_h.at[y], sems.at[len(copies)]))
            copies[-1].start()
    for copy in copies:
        copy.wait()


def pack(keep, came):
    y, slots, tokens, lanes = keep.shape
    packed = (y, slots * tokens, lanes * 2 // 3)
    return pl.pallas_call(
        pack_kernel,
        out_shape=[jax.ShapeDtypeStruct(packed, jnp.bfloat16)] * 2,
        in_specs=[VM] * 2,
        out_specs=[HB] * 2,
        scratch_shapes=[pltpu.VMEM(packed, jnp.bfloat16)] * 2
        + [pltpu.SemaphoreType.DMA((2 * y,))],
        compiler_params=pltpu.CompilerParams(vmem_limit_bytes=12 * 2**20),
        name="pack",
    )(keep, came)


def partial_kernel(moved, out):
    out[...] = summed(moved).astype(out.dtype)


def partial_sums(moved):
    return pl.pallas_call(
        partial_kernel,
        out_shape=jax.ShapeDtypeStruct(moved.shape[1:], jnp.bfloat16),
        in_specs=[VM],
        out_specs=VM,
        compiler_params=pltpu.CompilerParams(vmem_limit_bytes=12 * 2**20),
        name="partial",
    )(moved)


def project_kernel(moved, wq, wq_c, out, *, slot):
    sources = moved.shape[0]
    groups, tokens, part = out.shape
    rows = slice(slot * tokens, (slot + 1) * tokens)
    left = jnp.concatenate([moved[s, rows, :] for s in range(sources)], axis=1)
    for j in range(groups):
        cols = slice(j * part, (j + 1) * part)
        right = []
        for s in range(sources):
            right += [wq[s, cols, :], wq_c[s, cols, :]]
        out[j] = lax.dot_general(
            left, jnp.concatenate(right, axis=1), NT, preferred_element_type=jnp.float32
        )


def project(slot, moved, wq, wq_c, tokens, model):
    sources = moved.shape[0]
    width = wq.shape[2]
    groups = 4
    return pl.pallas_call(
        functools.partial(project_kernel, slot=slot),
        out_shape=jax.ShapeDtypeStruct((groups, tokens, model // groups), jnp.float32),
        in_specs=[VM] * 3,
        out_specs=VM,
        compiler_params=pltpu.CompilerParams(vmem_limit_bytes=16 * 2**20),
        cost_estimate=pl.CostEstimate(
            flops=2 * tokens * model * 2 * sources * width,
            bytes_accessed=6 * 2**20,
            transcendentals=0,
        ),
        name="project",
    )(moved, wq, wq_c)


def complete_kernel(spot, acc, part, far, wq, wq_c, out, kv_out, *, slot):
    groups, tokens, size = acc.shape
    rows = slice(slot * tokens, (slot + 1) * tokens)
    far_rows = slice((1 - slot) * tokens, (2 - slot) * tokens)
    kv = part[rows, :].astype(jnp.float32) + far[far_rows, :].astype(jnp.float32)
    kv_out[...] = kv.astype(kv_out.dtype)
    sums = kv_out[...]
    model = groups * size
    piece = size // 4
    first, low = spot[1] == 0, spot[0] == 0
    half = size // 2
    for j in range(groups):
        terms = []
        for w in (wq, wq_c):
            rhs = jnp.concatenate(
                [w[j, model:model + piece, :], w[j, model + piece:, :]], axis=1
            )
            terms.append(lax.dot_general(sums, rhs, NT, preferred_element_type=jnp.float32))
        near = jnp.concatenate(
            [jnp.where(first, *terms), jnp.where(first, *terms[::-1])], axis=1
        )
        none = jnp.zeros_like(near)
        out[j, :, :half] = (acc[j, :, :half] + jnp.where(low, near, none)).astype(out.dtype)
        out[j, :, half:] = (acc[j, :, half:] + jnp.where(low, none, near)).astype(out.dtype)


def complete(spot, slot, acc, part, far, wq, wq_c):
    return pl.pallas_call(
        functools.partial(complete_kernel, slot=slot),
        out_shape=[
            jax.ShapeDtypeStruct(acc.shape, jnp.bfloat16),
            jax.ShapeDtypeStruct((acc.shape[1], part.shape[1]), jnp.bfloat16),
        ],
        in_specs=[SM] + [VM] * 5,
        out_specs=[VM] * 2,
        compiler_params=pltpu.CompilerParams(vmem_limit_bytes=12 * 2**20),
        name="complete",
    )(spot, acc, part, far, wq, wq_c)


def summed(terms):
    total = terms[0].astype(jnp.float32)
    for s in range(1, terms.shape[0]):
        total = total + terms[s].astype(jnp.float32)
    return total


def gather_kernel(terms, out):
    out[...] = summed(terms).astype(out.dtype)


def gather(terms):
    return pl.pallas_call(
        gather_kernel,
        out_shape=jax.ShapeDtypeStruct(terms.shape[1:], jnp.bfloat16),
        in_specs=[VM],
        out_specs=VM,
        compiler_params=pltpu.CompilerParams(vmem_limit_bytes=16 * 2**20),
        name="gather",
    )(terms)


def finish_kernel(terms, far, out):
    out[...] = (summed(terms) + far[...].astype(jnp.float32)).astype(out.dtype)


def finish(terms, far):
    return pl.pallas_call(
        finish_kernel,
        out_shape=jax.ShapeDtypeStruct(terms.shape[1:], jnp.bfloat16),
        in_specs=[VM] * 2,
        out_specs=VM,
        compiler_params=pltpu.CompilerParams(vmem_limit_bytes=16 * 2**20),
        name="finish",
    )(terms, far)


def shards(query, query_exp, kv, kv_exp, out_grad, out_grad_exp, q_weight, q_weight_exp, kv_weight, kv_weight_exp):
    swap = [(0, 1), (1, 0)]
    spot = jnp.stack([lax.axis_index("zh"), lax.axis_index("core")]).astype(jnp.int32)
    model = q_weight.shape[0]
    w_all = lax.all_to_all(
        weights(q_weight, q_weight_exp, kv_weight, kv_weight_exp, 4), "y", 0, 0
    )
    keep, send = attention(spot, query, query_exp, kv, kv_exp, out_grad, out_grad_exp)
    tokens = keep.shape[2]
    kv_sent, dq_sent = pack(keep, lax.ppermute(send, "core", swap))
    kv_sent, dq_sent, w_all = lax.optimization_barrier((kv_sent, dq_sent, w_all))
    kv_moved = lax.all_to_all(kv_sent, "y", 0, 0)
    w_all_c = lax.ppermute(w_all, "core", swap)
    kv_moved, dq_sent = lax.optimization_barrier((kv_moved, dq_sent))
    dq_moved = lax.all_to_all(dq_sent, "y", 0, 0)
    part = partial_sums(kv_moved)
    far = lax.ppermute(part, "zh", swap)
    acc = project(0, dq_moved, w_all, w_all_c, tokens, model)
    other, _ = complete(spot, 0, acc, part, far, w_all, w_all_c)
    other = lax.all_to_all(other, "x", 0, 0)
    acc = project(1, dq_moved, w_all, w_all_c, tokens, model)
    own, kv_grad = complete(spot, 1, acc, part, far, w_all, w_all_c)
    sent = gather(other)
    own, sent = lax.optimization_barrier((own, sent))
    far_terms = lax.ppermute(sent, "zh", swap)
    own = lax.all_to_all(own, "x", 0, 0)
    return finish(own, far_terms), kv_grad


def solution(mesh):
    dp, group, head = (mesh.shape[a] for a in ("dp", "group", "head"))
    fine = Mesh(
        mesh.devices.reshape(dp, group, head // 4, 2, 2), ("dp", "x", "y", "zh", "core")
    )
    head_axes = ("y", "zh", "core")
    columns = P("dp", ("x",) + head_axes)
    exps = P(("x",) + head_axes, "dp")
    tokens = P(("dp",) + head_axes, "x")
    return jax.shard_map(
        shards,
        mesh=fine,
        in_specs=(columns, exps, P("dp", "x"), P("x", "dp"), columns, exps, columns, columns, tokens, tokens),
        out_specs=(tokens, tokens),
        check_vma=False,
    )
```

time: 130 us -> 127 us (0.977)
  the two profiles are of different devices: /device:TPU:35 before, /device:TPU:10 now
where the time goes in v5:
time: 127 us; the launch traced here: 126 us
  starting transfers between devices  53.6 us (42%)
  Pallas kernels  29.2 us (23%)
  waiting for transfers between devices  26.2 us (21%)
  blocking collectives  12.8 us (10%)
  local copies, waits for them, and re-layouts  2.73 us (2%)
    ppermute x1, starting transfers between devices, shards(): far = lax.ppermute(part, 'zh', swap)  15.7 us
    ppermute x1, starting transfers between devices, shards(): far_terms = lax.ppermute(sent, 'zh', swap)  14.5 us
    all_to_all x1, blocking collectives, shards(): kv_moved = lax.all_to_all(kv_sent, 'y', 0, 0)  12.8 us
    pallas_call x1, Pallas kernels, attention(): pl.pallas_call(functools.partial(attention_kernel, block=block, tile=tile...  12.4 us
    ppermute x1, waiting for transfers between devices, shards(): far_terms = lax.ppermute(sent, 'zh', swap)  9.95 us
    all_to_all x1, waiting for transfers between devices, shards(): lax.all_to_all(weights(q_weight, q_weight_exp, kv_weight, kv_weight_exp,...  6.76 us
    pallas_call x2, Pallas kernels, project(): pl.pallas_call(functools.partial(project_kernel, slot=slot), out_shape=ja...  6.33 us
    ppermute x1, waiting for transfers between devices, shards(): far = lax.ppermute(part, 'zh', swap)  5.85 us
  transfers between devices with their start and end apart: 8, of which 5 were waited for; matrix products, arithmetic and copies ran while one was open for 0% of the time, Pallas kernels for 18%

profile of v5, /device:TPU:10, one launch (start us, length us, event | category | flops | bytes accessed | tf_op | source)
XLA Modules:
  0.0 125.9 jit_solution(14037983805377257909)
XLA Ops:
  0.6 2.7 %weights.1 = bf16[4,2304,128]{2,1,0:T(8,128)(2,1)} custom-call(bf16[2048,128]{1,0:T(8,128)(2,1)} %wq_h.1, s32[64,128]{1,0:T(8,128)} %wq_exp_h.1, bf16[128,256]{1,0:T(8,128)(2,1)} %wkv_h.1, s32[4,256]{1,0:T(4,128)} %wkv_exp_h.1), custom_call_target="tpu_custom_call" | custom-call | tf_op jit(solution)/shard_map/weights/pallas_call | solution.py:243
  3.4 4.9 %all-to-all-start = ((bf16[4,2304,128]{2,1,0:T(8,128)(2,1)}), bf16[4,2304,128]{2,1,0:T(8,128)(2,1)S(1)}, u32[]{:S(2)}, u32[]{:S(2)}) async-start(bf16[4,2304,128]{2,1,0:T(8,128)(2,1)} %weights.1), calls=%async_computation | async-start | bytes 4718592 | tf_op jit(solution)/shard_map/all_to_all | solution.py:421
  8.3 0.6 pad_add_fusion.place_s.spot
  8.9 12.4 %attention.1 = (bf16[4,2,128,384]{3,2,1,0:T(8,128)(2,1)}, bf16[4,2,128,384]{3,2,1,0:T(8,128)(2,1)}) custom-call(s32[2]{0:T(128)} %pad_add_fusion.place_s.spot, bf16[2048,128]{1,0:T(8,128)(2,1)} %query_h.1, s32[4,2048]{1,0:T(4,128)} %q_exp_h.1, bf16[2048,256]{1,0:T(8,128)(2,1)} %kv_h.1, s32[8,2048]{1,0:T(8,128)} %kv_exp_h.1, bf16[2048,128]{1,0:T(8,128)(2,1)} %grad_h.1, ...), custom_call_target="tpu_custom_call" | custom-call | flops 3000000000 | bytes 6291456 | tf_op jit(solution)/shard_map/attention/pallas_call | solution.py:180
  21.3 1.9 %collective-permute-start = (bf16[4,2,128,384]{3,2,1,0:T(8,128)(2,1)}, bf16[4,2,128,384]{3,2,1,0:T(8,128)(2,1)S(1)}, u32[]{:S(2)}, u32[]{:S(2)}) collective-permute-start(bf16[4,2,128,384]{3,2,1,0:T(8,128)(2,1)} %get-tuple-element.17), channel_id=1, source_target_pairs={{0,1},{1,0},{2,3},{3,2},{4,5},{5,4},{6,7},{7,6},{8,9},{9,8},{10,11... | collective-permute-start | bytes 2359304 | tf_op jit(solution)/shard_map/ppermute | solution.py:426
  23.2 2.5 %collective-permute-done.came = bf16[4,2,128,384]{3,2,1,0:T(8,128)(2,1)S(1)} collective-permute-done((bf16[4,2,128,384]{3,2,1,0:T(8,128)(2,1)}, bf16[4,2,128,384]{3,2,1,0:T(8,128)(2,1)S(1)}, u32[]{:S(2)}, u32[]{:S(2)}) %collective-permute-start) | collective-permute-done | bytes 786464 | tf_op jit(solution)/shard_map/ppermute | solution.py:426
  25.7 0.0 copy-start
  25.7 1.1 copy-done
  26.8 1.6 %pack.1 = (bf16[4,256,256]{2,1,0:T(8,128)(2,1)S(1)}, bf16[4,256,256]{2,1,0:T(8,128)(2,1)S(1)}) custom-call(bf16[4,2,128,384]{3,2,1,0:T(8,128)(2,1)S(1)} %copy-done, bf16[4,2,128,384]{3,2,1,0:T(8,128)(2,1)S(1)} %collective-permute-done.came), custom_call_target="tpu_custom_call" | custom-call | tf_op jit(solution)/shard_map/pack/pallas_call | solution.py:279
  28.4 0.0 copy-start.3
  28.4 0.8 copy-done.3
  29.2 6.8 %all-to-all-done.wq = bf16[4,2304,128]{2,1,0:T(8,128)(2,1)S(1)} async-done(((bf16[4,2304,128]{2,1,0:T(8,128)(2,1)}), bf16[4,2304,128]{2,1,0:T(8,128)(2,1)S(1)}, u32[]{:S(2)}, u32[]{:S(2)}) %all-to-all-start) | async-done | bytes 2359328 | tf_op jit(solution)/shard_map/all_to_all | solution.py:421
  36.0 1.9 %collective-permute-start.1 = (bf16[4,2304,128]{2,1,0:T(8,128)(2,1)S(1)}, bf16[4,2304,128]{2,1,0:T(8,128)(2,1)}, u32[]{:S(2)}, u32[]{:S(2)}) collective-permute-start(bf16[4,2304,128]{2,1,0:T(8,128)(2,1)S(1)} %all-to-all-done.wq), channel_id=1, source_target_pairs={{0,1},{1,0},{2,3},{3,2},{4,5},{5,4},{6,7},{7,6},{8,9},{9,8},{10,11... | collective-permute-start | bytes 7077896 | tf_op jit(solution)/shard_map/ppermute | solution.py:429
  37.9 12.8 %all_to_all.25.moved = bf16[4,256,256]{2,1,0:T(8,128)(2,1)S(1)} all-to-all(bf16[4,256,256]{2,1,0:T(8,128)(2,1)S(1)} %get-tuple-element.20), channel_id=1, replica_groups=mesh['dp'=8,'x'=4,'y'=4,'zh'=2,'core'=2] {'y'}, dimensions={0} | all-to-all | bytes 1048576 | tf_op jit(solution)/shard_map/all_to_all | solution.py:428
  50.7 4.9 %all-to-all-start.2 = ((bf16[4,256,256]{2,1,0:T(8,128)(2,1)}), bf16[4,256,256]{2,1,0:T(8,128)(2,1)S(1)}, u32[]{:S(2)}, u32[]{:S(2)}) async-start(bf16[4,256,256]{2,1,0:T(8,128)(2,1)} %copy-done.3), calls=%async_computation.2 | async-start | bytes 1048576 | tf_op jit(solution)/shard_map/all_to_all | solution.py:431
  55.6 0.1 partial.1.part
  55.7 0.0 copy-start.5
  55.7 15.7 %collective-permute-start.2 = (bf16[256,256]{1,0:T(8,128)(2,1)S(1)}, bf16[256,256]{1,0:T(8,128)(2,1)S(1)}, u32[]{:S(2)}, u32[]{:S(2)}) collective-permute-start(bf16[256,256]{1,0:T(8,128)(2,1)S(1)} %partial.1.part), channel_id=1, source_target_pairs={{0,2},{2,0},{1,3},{3,1},{4,6},{6,4},{5,7},{7,5},{8,10},{10,8},{9,1... | collective-permute-start | bytes 393224 | tf_op jit(solution)/shard_map/ppermute | solution.py:433
  71.4 0.0 all-to-all-done.2.moved
  71.4 0.0 collective-permute-done.1.wq_c
  71.5 3.1 %project.3.acc = f32[4,128,512]{2,1,0:T(8,128)S(1)} custom-call(bf16[4,256,256]{2,1,0:T(8,128)(2,1)S(1)} %all-to-all-done.2.moved, bf16[4,2304,128]{2,1,0:T(8,128)(2,1)S(1)} %all-to-all-done.wq, bf16[4,2304,128]{2,1,0:T(8,128)(2,1)} %collective-permute-done.1.wq_c), custom_call_target="tpu_custom_call" | custom-call | flops 536870912 | bytes 6291456 | tf_op jit(solution)/shard_map/project/pallas_call | solution.py:325
  74.6 5.8 %collective-permute-done.2.far = bf16[256,256]{1,0:T(8,128)(2,1)S(1)} collective-permute-done((bf16[256,256]{1,0:T(8,128)(2,1)S(1)}, bf16[256,256]{1,0:T(8,128)(2,1)S(1)}, u32[]{:S(2)}, u32[]{:S(2)}) %collective-permute-start.2) | collective-permute-done | bytes 131104 | tf_op jit(solution)/shard_map/ppermute | solution.py:433
  80.5 0.0 copy-done.5
  80.5 0.0 copy-start.1
  80.5 2.5 %complete.3 = (bf16[4,128,512]{2,1,0:T(8,128)(2,1)S(1)}, bf16[128,256]{1,0:T(8,128)(2,1)}) custom-call(s32[2]{0:T(128)S(1)} %copy-done.5, f32[4,128,512]{2,1,0:T(8,128)S(1)} %project.3.acc, bf16[256,256]{1,0:T(8,128)(2,1)S(1)} %partial.1.part, bf16[256,256]{1,0:T(8,128)(2,1)S(1)} %collective-permute-done.2.far, bf16[4,2304,128]{2,1,0:T(8,128)(2,1)S(1)} %all-to-all-done.wq, ...), custom_call_target="tpu_custom_call" | custom-call | tf_op jit(solution)/shard_map/complete/pallas_call | solution.py:367
  83.0 0.0 copy-done.1
  83.0 0.0 copy-start.4
  83.0 0.8 copy-done.4
  83.8 4.8 %all-to-all-start.3 = ((bf16[4,128,512]{2,1,0:T(8,128)(2,1)}), bf16[4,128,512]{2,1,0:T(8,128)(2,1)S(1)}, u32[]{:S(2)}, u32[]{:S(2)}) async-start(bf16[4,128,512]{2,1,0:T(8,128)(2,1)} %copy-done.4), calls=%async_computation.3 | async-start | bytes 1048576 | tf_op jit(solution)/shard_map/all_to_all | solution.py:436
  88.6 0.0 copy-start.2
  88.6 3.2 %project.2.acc = f32[4,128,512]{2,1,0:T(8,128)S(1)} custom-call(bf16[4,256,256]{2,1,0:T(8,128)(2,1)S(1)} %all-to-all-done.2.moved, bf16[4,2304,128]{2,1,0:T(8,128)(2,1)S(1)} %all-to-all-done.wq, bf16[4,2304,128]{2,1,0:T(8,128)(2,1)} %collective-permute-done.1.wq_c), custom_call_target="tpu_custom_call" | custom-call | flops 536870912 | bytes 6291456 | tf_op jit(solution)/shard_map/project/pallas_call | solution.py:325
  91.8 0.0 copy-done.2
  91.8 2.8 %complete.2 = (bf16[4,128,512]{2,1,0:T(8,128)(2,1)}, bf16[128,256]{1,0:T(8,128)(2,1)}) custom-call(s32[2]{0:T(128)S(1)} %copy-done.5, f32[4,128,512]{2,1,0:T(8,128)S(1)} %project.2.acc, bf16[256,256]{1,0:T(8,128)(2,1)S(1)} %partial.1.part, bf16[256,256]{1,0:T(8,128)(2,1)S(1)} %copy-done.2, bf16[4,2304,128]{2,1,0:T(8,128)(2,1)S(1)} %all-to-all-done.wq, ...), custom_call_target="tpu_custom_call" | custom-call | tf_op jit(solution)/shard_map/complete/pallas_call | solution.py:367
  94.6 1.1 all-to-all-done.3.terms
  95.7 0.1 gather.1
  95.8 4.9 %all-to-all-start.4 = ((bf16[4,128,512]{2,1,0:T(8,128)(2,1)}), bf16[4,128,512]{2,1,0:T(8,128)(2,1)S(1)}, u32[]{:S(2)}, u32[]{:S(2)}) async-start(bf16[4,128,512]{2,1,0:T(8,128)(2,1)} %get-tuple-element.27), calls=%async_computation.4 | async-start | bytes 1048576 | tf_op jit(solution)/shard_map/all_to_all | solution.py:442
  100.7 14.5 %collective-permute-start.3 = (bf16[128,512]{1,0:T(8,128)(2,1)S(1)}, bf16[128,512]{1,0:T(8,128)(2,1)S(1)}, u32[]{:S(2)}, u32[]{:S(2)}) collective-permute-start(bf16[128,512]{1,0:T(8,128)(2,1)S(1)} %gather.1), channel_id=1, source_target_pairs={{0,2},{2,0},{1,3},{3,1},{4,6},{6,4},{5,7},{7,5},{8,10},{10,8},{9,1... | collective-permute-start | bytes 393224 | tf_op jit(solution)/shard_map/ppermute | solution.py:441
  115.2 10.0 %collective-permute-done.3.far = bf16[128,512]{1,0:T(8,128)(2,1)S(1)} collective-permute-done((bf16[128,512]{1,0:T(8,128)(2,1)S(1)}, bf16[128,512]{1,0:T(8,128)(2,1)S(1)}, u32[]{:S(2)}, u32[]{:S(2)}) %collective-permute-start.3) | collective-permute-done | bytes 131104 | tf_op jit(solution)/shard_map/ppermute | solution.py:441
  125.1 0.0 all-to-all-done.4.terms
  125.1 0.7 finish.1
Async XLA Ops:
  3.4 32.6 %all-to-all-start = ((bf16[4,2304,128]{2,1,0:T(8,128)(2,1)}), bf16[4,2304,128]{2,1,0:T(8,128)(2,1)S(1)}, u32[]{:S(2)}, u32[]{:S(2)}) async-start(bf16[4,2304,128]{2,1,0:T(8,128)(2,1)} %weights.1), calls=%async_computation | async-start | bytes 4718592 | tf_op jit(solution)/shard_map/all_to_all | solution.py:421
  21.3 4.4 %collective-permute-start = (bf16[4,2,128,384]{3,2,1,0:T(8,128)(2,1)}, bf16[4,2,128,384]{3,2,1,0:T(8,128)(2,1)S(1)}, u32[]{:S(2)}, u32[]{:S(2)}) collective-permute-start(bf16[4,2,128,384]{3,2,1,0:T(8,128)(2,1)} %get-tuple-element.17), channel_id=1, source_target_pairs={{0,1},{1,0},{2,3},{3,2},{4,5},{5,4},{6,7},{7,6},{8,9},{9,8},{10,11... | collective-permute-start | bytes 2359304 | tf_op jit(solution)/shard_map/ppermute | solution.py:426
  25.7 1.1 copy-start
  28.4 0.8 copy-start.3
  36.0 35.5 %collective-permute-start.1 = (bf16[4,2304,128]{2,1,0:T(8,128)(2,1)S(1)}, bf16[4,2304,128]{2,1,0:T(8,128)(2,1)}, u32[]{:S(2)}, u32[]{:S(2)}) collective-permute-start(bf16[4,2304,128]{2,1,0:T(8,128)(2,1)S(1)} %all-to-all-done.wq), channel_id=1, source_target_pairs={{0,1},{1,0},{2,3},{3,2},{4,5},{5,4},{6,7},{7,6},{8,9},{9,8},{10,11... | collective-permute-start | bytes 7077896 | tf_op jit(solution)/shard_map/ppermute | solution.py:429
  50.7 20.7 %all-to-all-start.2 = ((bf16[4,256,256]{2,1,0:T(8,128)(2,1)}), bf16[4,256,256]{2,1,0:T(8,128)(2,1)S(1)}, u32[]{:S(2)}, u32[]{:S(2)}) async-start(bf16[4,256,256]{2,1,0:T(8,128)(2,1)} %copy-done.3), calls=%async_computation.2 | async-start | bytes 1048576 | tf_op jit(solution)/shard_map/all_to_all | solution.py:431
  55.7 24.8 %copy-start.5 = (s32[2]{0:T(128)S(1)}, s32[2]{0:T(128)}, u32[]{:S(2)}) copy-start(s32[2]{0:T(128)} %pad_add_fusion.place_s.spot) | copy-start | bytes 28
  55.7 24.8 %collective-permute-start.2 = (bf16[256,256]{1,0:T(8,128)(2,1)S(1)}, bf16[256,256]{1,0:T(8,128)(2,1)S(1)}, u32[]{:S(2)}, u32[]{:S(2)}) collective-permute-start(bf16[256,256]{1,0:T(8,128)(2,1)S(1)} %partial.1.part), channel_id=1, source_target_pairs={{0,2},{2,0},{1,3},{3,1},{4,6},{6,4},{5,7},{7,5},{8,10},{10,8},{9,1... | collective-permute-start | bytes 393224 | tf_op jit(solution)/shard_map/ppermute | solution.py:433
  80.5 2.5 %copy-start.1 = (bf16[256,256]{1,0:T(8,128)(2,1)}, bf16[256,256]{1,0:T(8,128)(2,1)S(1)}, u32[]{:S(2)}) copy-start(bf16[256,256]{1,0:T(8,128)(2,1)S(1)} %collective-permute-done.2.far) | copy-start | bytes 393220
  83.0 0.8 copy-start.4
  83.8 12.0 %all-to-all-start.3 = ((bf16[4,128,512]{2,1,0:T(8,128)(2,1)}), bf16[4,128,512]{2,1,0:T(8,128)(2,1)S(1)}, u32[]{:S(2)}, u32[]{:S(2)}) async-start(bf16[4,128,512]{2,1,0:T(8,128)(2,1)} %copy-done.4), calls=%async_computation.3 | async-start | bytes 1048576 | tf_op jit(solution)/shard_map/all_to_all | solution.py:436
  88.6 3.2 %copy-start.2 = (bf16[256,256]{1,0:T(8,128)(2,1)S(1)}, bf16[256,256]{1,0:T(8,128)(2,1)}, u32[]{:S(2)}) copy-start(bf16[256,256]{1,0:T(8,128)(2,1)} %copy-done.1) | copy-start | bytes 393220
  95.8 29.3 %all-to-all-start.4 = ((bf16[4,128,512]{2,1,0:T(8,128)(2,1)}), bf16[4,128,512]{2,1,0:T(8,128)(2,1)S(1)}, u32[]{:S(2)}, u32[]{:S(2)}) async-start(bf16[4,128,512]{2,1,0:T(8,128)(2,1)} %get-tuple-element.27), calls=%async_computation.4 | async-start | bytes 1048576 | tf_op jit(solution)/shard_map/all_to_all | solution.py:442
  100.7 24.4 %collective-permute-start.3 = (bf16[128,512]{1,0:T(8,128)(2,1)S(1)}, bf16[128,512]{1,0:T(8,128)(2,1)S(1)}, u32[]{:S(2)}, u32[]{:S(2)}) collective-permute-start(bf16[128,512]{1,0:T(8,128)(2,1)S(1)} %gather.1), channel_id=1, source_target_pairs={{0,2},{2,0},{1,3},{3,1},{4,6},{6,4},{5,7},{7,5},{8,10},{10,8},{9,1... | collective-permute-start | bytes 393224 | tf_op jit(solution)/shard_map/ppermute | solution.py:441

commit v6 on v5

--- a/solution.py
+++ b/solution.py
@@ -167,8 +167,8 @@
     for j in range(value.shape[0] // piece):
         h = first // piece + j
         y, z, c = h // 4, (h // 2) % 2, h % 2
-        mine = jnp.where(spot[1] == c, 1, 0)
-        slot = jnp.where(spot[0] == z, 1, 0)
+        mine = jnp.where(spot[0] % 2 == c, 1, 0)
+        slot = jnp.where(spot[0] // 2 == z, 1, 0)
         out[mine, y, slot] = value[j * piece:(j + 1) * piece]
 
 
@@ -211,51 +211,56 @@
     return (blocks * power(exps)[:, None, :]).reshape(rows, cols).astype(jnp.bfloat16)
 
 
-def weights_kernel(wq_h, wq_exp_h, wkv_h, wkv_exp_h, all_h, wq, wq_exp, wkv, wkv_exp, out, sems):
-    loads = [
-        pltpu.make_async_copy(source, target, sems.at[n])
-        for n, (source, target) in enumerate(
-            ((wkv_exp_h, wkv_exp), (wkv_h, wkv), (wq_exp_h, wq_exp), (wq_h, wq))
-        )
-    ]
+def weights_kernel(wq_h, wq_exp_h, wkv_h, wkv_exp_h, all_h, kv_h, wq, wq_exp, wkv, wkv_exp, out, kv_out, sems, *, steps):
+    rows = wq.shape[0] // steps
+    blocks = [slice(n * rows, (n + 1) * rows) for n in range(steps)]
+    pairs = [(wq_exp_h, wq_exp)] + [(wq_h.at[at], wq.at[at]) for at in blocks]
+    pairs += [(wkv_exp_h, wkv_exp), (wkv_h, wkv)]
+    loads = [pltpu.make_async_copy(*pair, sems.at[n]) for n, pair in enumerate(pairs)]
+    stores = []
+
+    def store(source, target):
+        stores.append(pltpu.make_async_copy(source, target, sems.at[len(loads) + len(stores)]))
+        stores[-1].start()
+
     for copy in loads:
         copy.start()
-    for copy in loads:
+    loads[0].wait()
+    for n, at in enumerate(blocks):
+        loads[1 + n].wait()
+        out[at, :] = scaled(wq[at, :], wq_exp[n * rows // 32:(n + 1) * rows // 32, :])
+        for y in range(all_h.shape[0]):
+            store(out.at[at], all_h.at[y, at])
+    for copy in loads[1 + steps:]:
         copy.wait()
-    rows = wq.shape[0]
-    size, lanes = wkv.shape
-    kv = scaled(wkv[...], wkv_exp[...])
-    out[rows:rows + size, :] = kv[:, :lanes // 2]
-    out[rows + size:, :] = kv[:, lanes // 2:]
-    out[:rows, :] = scaled(wq[...], wq_exp[...])
-    stores = [
-        pltpu.make_async_copy(out, all_h.at[n], sems.at[4 + n]) for n in range(all_h.shape[0])
-    ]
-    for copy in stores:
-        copy.start()
+    kv_out[...] = scaled(wkv[...], wkv_exp[...])
+    store(kv_out, kv_h)
     for copy in stores:
         copy.wait()
 
 
-def weights(wq, wq_exp, wkv, wkv_exp, copies):
+def weights(wq, wq_exp, wkv, wkv_exp, copies, steps=4):
     operands = (wq, wq_exp, wkv, wkv_exp)
-    joined = (wq.shape[0] + 2 * wkv.shape[0], wq.shape[1])
-    return pl.pallas_call(
-        weights_kernel,
-        out_shape=jax.ShapeDtypeStruct((copies,) + joined, jnp.bfloat16),
+    return pl.pallas_call(
+        functools.partial(weights_kernel, steps=steps),
+        out_shape=[
+            jax.ShapeDtypeStruct((copies,) + wq.shape, jnp.bfloat16),
+            jax.ShapeDtypeStruct(wkv.shape, jnp.bfloat16),
+        ],
         in_specs=[HB] * 4,
-        out_specs=HB,
+        out_specs=[HB] * 2,
         scratch_shapes=[pltpu.VMEM(a.shape, a.dtype) for a in operands]
         + [
-            pltpu.VMEM(joined, jnp.bfloat16),
-            pltpu.SemaphoreType.DMA((4 + copies,)),
+            pltpu.VMEM(wq.shape, jnp.bfloat16),
+            pltpu.VMEM(wkv.shape, jnp.bfloat16),
+            pltpu.SemaphoreType.DMA((4 + steps + copies * steps,)),
         ],
         compiler_params=pltpu.CompilerParams(vmem_limit_bytes=FULL),
         name="weights",
     )(*operands)
 
 
-def pack_kernel(keep, came, kv_h, dq_h, kv_out, dq_out, sems):
+def pack_kernel(keep, came, wkv, wkv_c, kv_h, dq_h, kv_out, dq_out, sems):
     width = keep.shape[3] // 3
     tokens = keep.shape[2]
     copies = []
@@ -266,6 +271,8 @@
             kv_out[y, rows, :] = kv.astype(jnp.bfloat16)
             dq_out[y, rows, :width] = keep[y, slot, :, :width]
             dq_out[y, rows, width:] = came[y, slot, :, :width]
+        dq_out[y, 2 * tokens:2 * tokens + wkv.shape[0], :] = wkv[...]
+        dq_out[y, 2 * tokens + wkv.shape[0]:, :] = wkv_c[...]
         for out, out_h in ((kv_out, kv_h), (dq_out, dq_h)):
             copies.append(pltpu.make_async_copy(out.at[y], out_h.at[y], sems.at[len(copies)]))
             copies[-1].start()
@@ -273,19 +280,23 @@
         copy.wait()
 
 
-def pack(keep, came):
+def pack(keep, came, wkv, wkv_c):
     y, slots, tokens, lanes = keep.shape
-    packed = (y, slots * tokens, lanes * 2 // 3)
+    sums = (y, slots * tokens, lanes * 2 // 3)
+    packed = (y, slots * tokens + 2 * wkv.shape[0], lanes * 2 // 3)
     return pl.pallas_call(
         pack_kernel,
-        out_shape=[jax.ShapeDtypeStruct(packed, jnp.bfloat16)] * 2,
-        in_specs=[VM] * 2,
+        out_shape=[jax.ShapeDtypeStruct(sums, jnp.bfloat16), jax.ShapeDtypeStruct(packed, jnp.bfloat16)],
+        in_specs=[VM] * 4,
         out_specs=[HB] * 2,
-        scratch_shapes=[pltpu.VMEM(packed, jnp.bfloat16)] * 2
-        + [pltpu.SemaphoreType.DMA((2 * y,))],
+        scratch_shapes=[
+            pltpu.VMEM(sums, jnp.bfloat16),
+            pltpu.VMEM(packed, jnp.bfloat16),
+            pltpu.SemaphoreType.DMA((2 * y,)),
+        ],
         compiler_params=pltpu.CompilerParams(vmem_limit_bytes=12 * 2**20),
         name="pack",
-    )(keep, came)
+    )(keep, came, wkv, wkv_c)
 
 
 def partial_kernel(moved, out):
@@ -303,13 +314,66 @@
     )(moved)
 
 
-def project_kernel(moved, wq, wq_c, out, *, slot):
+def project_kernel(spot, moved, part, far, wq, wq_c, out, kv_out, *, slot):
     sources = moved.shape[0]
-    groups, tokens, part = out.shape
+    groups, tokens, size = out.shape
+    rows = slice(slot * tokens, (slot + 1) * tokens)
+    far_rows = slice((1 - slot) * tokens, (2 - slot) * tokens)
+    kv = part[rows, :].astype(jnp.float32) + far[far_rows, :].astype(jnp.float32)
+    kv_out[...] = kv.astype(kv_out.dtype)
+    sums = kv_out[...]
+    first, low = spot[0] % 2 == 0, spot[0] < 2
+    near_rows = slice(2 * tokens, (2 * tokens + moved.shape[1]) // 2)
+    left = jnp.concatenate([moved[s, rows, :] for s in range(sources)], axis=1)
+    for j in range(groups):
+        cols = slice(j * size, (j + 1) * size)
+        right = []
+        for s in range(sources):
+            right += [wq[s, cols, :], wq_c[s, cols, :]]
+        acc = lax.dot_general(
+            left, jnp.concatenate(right, axis=1), NT, preferred_element_type=jnp.float32
+        )
+        terms = [
+            lax.dot_general(sums, w, NT, preferred_element_type=jnp.float32)
+            for w in (moved[j, near_rows, :], moved[j, near_rows.stop:, :])
+        ]
+        near = jnp.concatenate(
+            [jnp.where(first, *terms), jnp.where(first, *terms[::-1])], axis=1
+        )
+        none = jnp.zeros_like(near)
+        term = jnp.concatenate([jnp.where(low, near, none), jnp.where(low, none, near)], axis=1)
+        out[j] = (acc + term).astype(out.dtype)
+
+
+def project(spot, slot, moved, part, far, wq, wq_c, tokens):
+    sources = moved.shape[0]
+    model, width = wq.shape[1:]
+    groups = 4
+    return pl.pallas_call(
+        functools.partial(project_kernel, slot=slot),
+        out_shape=[
+            jax.ShapeDtypeStruct((groups, tokens, model // groups), jnp.bfloat16),
+            jax.ShapeDtypeStruct((tokens, part.shape[1]), jnp.bfloat16),
+        ],
+        in_specs=[SM] + [VM] * 5,
+        out_specs=[VM] * 2,
+        compiler_params=pltpu.CompilerParams(vmem_limit_bytes=16 * 2**20),
+        cost_estimate=pl.CostEstimate(
+            flops=2 * tokens * model * (2 * sources + 2) * width,
+            bytes_accessed=6 * 2**20,
+            transcendentals=0,
+        ),
+        name="project",
+    )(spot, moved, part, far, wq, wq_c)
+
+
+def head_terms_kernel(moved, wq, wq_c, out, *, slot):
+    sources = moved.shape[0]
+    groups, tokens, size = out.shape
     rows = slice(slot * tokens, (slot + 1) * tokens)
     left = jnp.concatenate([moved[s, rows, :] for s in range(sources)], axis=1)
     for j in range(groups):
-        cols = slice(j * part, (j + 1) * part)
+        cols = slice(j * size, (j + 1) * size)
         right = []
         for s in range(sources):
             right += [wq[s, cols, :], wq_c[s, cols, :]]
@@ -318,12 +382,12 @@
         )
 
 
-def project(slot, moved, wq, wq_c, tokens, model):
+def head_terms(slot, moved, wq, wq_c, tokens):
     sources = moved.shape[0]
-    width = wq.shape[2]
+    model, width = wq.shape[1:]
     groups = 4
     return pl.pallas_call(
-        functools.partial(project_kernel, slot=slot),
+        functools.partial(head_terms_kernel, slot=slot),
         out_shape=jax.ShapeDtypeStruct((groups, tokens, model // groups), jnp.float32),
         in_specs=[VM] * 3,
         out_specs=VM,
@@ -333,28 +397,24 @@
             bytes_accessed=6 * 2**20,
             transcendentals=0,
         ),
-        name="project",
+        name="head_terms",
     )(moved, wq, wq_c)
 
 
-def complete_kernel(spot, acc, part, far, wq, wq_c, out, kv_out, *, slot):
+def complete_kernel(spot, acc, moved, part, far, out, *, slot):
     groups, tokens, size = acc.shape
     rows = slice(slot * tokens, (slot + 1) * tokens)
     far_rows = slice((1 - slot) * tokens, (2 - slot) * tokens)
     kv = part[rows, :].astype(jnp.float32) + far[far_rows, :].astype(jnp.float32)
-    kv_out[...] = kv.astype(kv_out.dtype)
-    sums = kv_out[...]
-    model = groups * size
-    piece = size // 4
-    first, low = spot[1] == 0, spot[0] == 0
+    sums = kv.astype(jnp.bfloat16)
+    first, low = spot[0] % 2 == 0, spot[0] < 2
+    near_rows = slice(2 * tokens, (2 * tokens + moved.shape[1]) // 2)
     half = size // 2
     for j in range(groups):
-        terms = []
-        for w in (wq, wq_c):
-            rhs = jnp.concatenate(
-                [w[j, model:model + piece, :], w[j, model + piece:, :]], axis=1
-            )
-            terms.append(lax.dot_general(sums, rhs, NT, preferred_element_type=jnp.float32))
+        terms = [
+            lax.dot_general(sums, w, NT, preferred_element_type=jnp.float32)
+            for w in (moved[j, near_rows, :], moved[j, near_rows.stop:, :])
+        ]
         near = jnp.concatenate(
             [jnp.where(first, *terms), jnp.where(first, *terms[::-1])], axis=1
         )
@@ -363,18 +423,15 @@
         out[j, :, half:] = (acc[j, :, half:] + jnp.where(low, none, near)).astype(out.dtype)
 
 
-def complete(spot, slot, acc, part, far, wq, wq_c):
+def complete(spot, slot, acc, moved, part, far):
     return pl.pallas_call(
         functools.partial(complete_kernel, slot=slot),
-        out_shape=[
-            jax.ShapeDtypeStruct(acc.shape, jnp.bfloat16),
-            jax.ShapeDtypeStruct((acc.shape[1], part.shape[1]), jnp.bfloat16),
-        ],
-        in_specs=[SM] + [VM] * 5,
-        out_specs=[VM] * 2,
+        out_shape=jax.ShapeDtypeStruct(acc.shape, jnp.bfloat16),
+        in_specs=[SM] + [VM] * 4,
+        out_specs=VM,
         compiler_params=pltpu.CompilerParams(vmem_limit_bytes=12 * 2**20),
         name="complete",
-    )(spot, acc, part, far, wq, wq_c)
+    )(spot, acc, moved, part, far)
 
 
 def summed(terms):
@@ -400,7 +457,7 @@
 
 
 def finish_kernel(terms, far, out):
-    out[...] = (summed(terms) + far[...].astype(jnp.float32)).astype(out.dtype)
+    out[...] = (summed(terms) + far[...]).astype(out.dtype)
 
 
 def finish(terms, far):
@@ -414,33 +471,47 @@
     )(terms, far)
 
 
+def widen_kernel(far, out):
+    out[...] = far[...].astype(out.dtype)
+
+
+def widen(far):
+    return pl.pallas_call(
+        widen_kernel,
+        out_shape=jax.ShapeDtypeStruct(far.shape, jnp.float32),
+        in_specs=[VM],
+        out_specs=VM,
+        compiler_params=pltpu.CompilerParams(vmem_limit_bytes=16 * 2**20),
+        cost_estimate=pl.CostEstimate(flops=2 * 10**10, bytes_accessed=2**20, transcendentals=0),
+        name="widen",
+    )(far)
+
+
 def shards(query, query_exp, kv, kv_exp, out_grad, out_grad_exp, q_weight, q_weight_exp, kv_weight, kv_weight_exp):
     swap = [(0, 1), (1, 0)]
-    spot = jnp.stack([lax.axis_index("zh"), lax.axis_index("core")]).astype(jnp.int32)
-    model = q_weight.shape[0]
-    w_all = lax.all_to_all(
-        weights(q_weight, q_weight_exp, kv_weight, kv_weight_exp, 4), "y", 0, 0
-    )
+    spot = (2 * lax.axis_index("zh") + lax.axis_index("core")).astype(jnp.int32).reshape(1)
+    w_sent, wkv = weights(q_weight, q_weight_exp, kv_weight, kv_weight_exp, 4)
+    w_all = lax.all_to_all(w_sent, "y", 0, 0)
     keep, send = attention(spot, query, query_exp, kv, kv_exp, out_grad, out_grad_exp)
     tokens = keep.shape[2]
-    kv_sent, dq_sent = pack(keep, lax.ppermute(send, "core", swap))
+    kv_sent, dq_sent = pack(keep, lax.ppermute(send, "core", swap), wkv, lax.ppermute(wkv, "core", swap))
     kv_sent, dq_sent, w_all = lax.optimization_barrier((kv_sent, dq_sent, w_all))
     kv_moved = lax.all_to_all(kv_sent, "y", 0, 0)
+    kv_moved, dq_sent, w_all = lax.optimization_barrier((kv_moved, dq_sent, w_all))
     w_all_c = lax.ppermute(w_all, "core", swap)
-    kv_moved, dq_sent = lax.optimization_barrier((kv_moved, dq_sent))
-    dq_moved = lax.all_to_all(dq_sent, "y", 0, 0)
+    moved = lax.all_to_all(dq_sent, "y", 0, 0)
     part = partial_sums(kv_moved)
     far = lax.ppermute(part, "zh", swap)
-    acc = project(0, dq_moved, w_all, w_all_c, tokens, model)
-    other, _ = complete(spot, 0, acc, part, far, w_all, w_all_c)
+    acc = head_terms(0, moved, w_all, w_all_c, tokens)
+    acc, far = lax.optimization_barrier((acc, far))
+    other = complete(spot, 0, acc, moved, part, far)
     other = lax.all_to_all(other, "x", 0, 0)
-    acc = project(1, dq_moved, w_all, w_all_c, tokens, model)
-    own, kv_grad = complete(spot, 1, acc, part, far, w_all, w_all_c)
+    own, kv_grad = project(spot, 1, moved, part, far, w_all, w_all_c, tokens)
     sent = gather(other)
     own, sent = lax.optimization_barrier((own, sent))
     far_terms = lax.ppermute(sent, "zh", swap)
     own = lax.all_to_all(own, "x", 0, 0)
-    return finish(own, far_terms), kv_grad
+    return finish(own, widen(far_terms)), kv_grad
 
 
 def solution(mesh):

time: 127 us -> 121 us (0.953)
  the two profiles are of different devices: /device:TPU:10 before, /device:TPU:32 now
where the time goes in v6:
time: 121 us; the launch traced here: 120 us
  starting transfers between devices  48.9 us (40%)
  waiting for transfers between devices  30.3 us (25%)
  Pallas kernels  23.8 us (20%)
  blocking collectives  11.6 us (10%)
  local copies, waits for them, and re-layouts  4.74 us (4%)
    ppermute x1, starting transfers between devices, shards(): far = lax.ppermute(part, 'zh', swap)  14.8 us
    ppermute x1, starting transfers between devices, shards(): far_terms = lax.ppermute(sent, 'zh', swap)  12.1 us
    pallas_call x1, Pallas kernels, attention(): pl.pallas_call(functools.partial(attention_kernel, block=block, tile=tile...  11.7 us
    all_to_all x1, blocking collectives, shards(): kv_moved = lax.all_to_all(kv_sent, 'y', 0, 0)  11.6 us
    ppermute x1, waiting for transfers between devices, shards(): far = lax.ppermute(part, 'zh', swap)  9.58 us
    all_to_all x1, waiting for transfers between devices, shards(): w_all = lax.all_to_all(w_sent, 'y', 0, 0)  6.21 us
    all_to_all x1, waiting for transfers between devices, shards(): other = lax.all_to_all(other, 'x', 0, 0)  5.57 us
    unnamed x12, local copies, waits for them, and re-layouts  4.74 us
  transfers between devices with their start and end apart: 9, of which 7 were waited for; matrix products, arithmetic and copies ran while one was open for 0% of the time, Pallas kernels for 16%

profile of v6, /device:TPU:32, one launch (start us, length us, event | category | flops | bytes accessed | tf_op | source)
XLA Modules:
  0.0 120.2 jit_solution(1967884396828747906)
XLA Ops:
  0.6 2.5 %weights.1 = (bf16[4,2048,128]{2,1,0:T(8,128)(2,1)}, bf16[128,256]{1,0:T(8,128)(2,1)}) custom-call(bf16[2048,128]{1,0:T(8,128)(2,1)} %wq_h.1, s32[64,128]{1,0:T(8,128)} %wq_exp_h.1, bf16[128,256]{1,0:T(8,128)(2,1)} %wkv_h.1, s32[4,256]{1,0:T(4,128)} %wkv_exp_h.1), custom_call_target="tpu_custom_call" | custom-call | tf_op jit(solution)/shard_map/weights/pallas_call | solution.py:244
  3.1 4.5 %all-to-all-start = ((bf16[4,2048,128]{2,1,0:T(8,128)(2,1)}), bf16[4,2048,128]{2,1,0:T(8,128)(2,1)S(1)}, u32[]{:S(2)}, u32[]{:S(2)}) async-start(bf16[4,2048,128]{2,1,0:T(8,128)(2,1)} %get-tuple-element.25), calls=%async_computation | async-start | bytes 4194304 | tf_op jit(solution)/shard_map/all_to_all | solution.py:494
  7.6 0.0 copy-start.5
  7.6 11.7 %attention.1 = (bf16[4,2,128,384]{3,2,1,0:T(8,128)(2,1)}, bf16[4,2,128,384]{3,2,1,0:T(8,128)(2,1)}) custom-call(s32[1]{0:T(128)} %bitcast.place_s.spot, bf16[2048,128]{1,0:T(8,128)(2,1)} %query_h.1, s32[4,2048]{1,0:T(4,128)} %q_exp_h.1, bf16[2048,256]{1,0:T(8,128)(2,1)} %kv_h.1, s32[8,2048]{1,0:T(8,128)} %kv_exp_h.1, bf16[2048,128]{1,0:T(8,128)(2,1)} %grad_h.1, ...), custom_call_target="tpu_custom_call" | custom-call | flops 3000000000 | bytes 6291456 | tf_op jit(solution)/shard_map/attention/pallas_call | solution.py:180
  19.4 1.9 %collective-permute-start = (bf16[4,2,128,384]{3,2,1,0:T(8,128)(2,1)}, bf16[4,2,128,384]{3,2,1,0:T(8,128)(2,1)S(1)}, u32[]{:S(2)}, u32[]{:S(2)}) collective-permute-start(bf16[4,2,128,384]{3,2,1,0:T(8,128)(2,1)} %get-tuple-element.21), channel_id=1, source_target_pairs={{0,1},{1,0},{2,3},{3,2},{4,5},{5,4},{6,7},{7,6},{8,9},{9,8},{10,11... | collective-permute-start | bytes 2359304 | tf_op jit(solution)/shard_map/ppermute | solution.py:497
  21.3 0.0 copy-done.5
  21.3 2.4 %collective-permute-start.1 = (bf16[128,256]{1,0:T(8,128)(2,1)S(1)}, bf16[128,256]{1,0:T(8,128)(2,1)S(1)}, u32[]{:S(2)}, u32[]{:S(2)}) collective-permute-start(bf16[128,256]{1,0:T(8,128)(2,1)S(1)} %copy-done.5), channel_id=1, source_target_pairs={{0,1},{1,0},{2,3},{3,2},{4,5},{5,4},{6,7},{7,6},{8,9},{9,8},{10,11... | collective-permute-start | bytes 196616 | tf_op jit(solution)/shard_map/ppermute | solution.py:497
  23.7 0.9 collective-permute-done.1.wkv_c
  24.6 0.0 collective-permute-done.came
  24.6 0.0 copy-start.3
  24.6 1.1 copy-done.3
  25.7 1.0 pack.1
  26.7 0.0 copy-start.2
  26.8 1.0 copy-done.2
  27.7 6.2 %all-to-all-done.wq = bf16[4,2048,128]{2,1,0:T(8,128)(2,1)S(1)} async-done(((bf16[4,2048,128]{2,1,0:T(8,128)(2,1)}), bf16[4,2048,128]{2,1,0:T(8,128)(2,1)S(1)}, u32[]{:S(2)}, u32[]{:S(2)}) %all-to-all-start) | async-done | bytes 2097184 | tf_op jit(solution)/shard_map/all_to_all | solution.py:494
  33.9 11.6 %all_to_all.25.moved = bf16[4,256,256]{2,1,0:T(8,128)(2,1)} all-to-all(bf16[4,256,256]{2,1,0:T(8,128)(2,1)S(1)} %get-tuple-element.26), channel_id=1, replica_groups=mesh['dp'=8,'x'=4,'y'=4,'zh'=2,'core'=2] {'y'}, dimensions={0} | all-to-all | bytes 1048576 | tf_op jit(solution)/shard_map/all_to_all | solution.py:499
  45.6 1.9 %collective-permute-start.2 = (bf16[4,2048,128]{2,1,0:T(8,128)(2,1)S(1)}, bf16[4,2048,128]{2,1,0:T(8,128)(2,1)}, u32[]{:S(2)}, u32[]{:S(2)}) collective-permute-start(bf16[4,2048,128]{2,1,0:T(8,128)(2,1)S(1)} %all-to-all-done.wq), channel_id=1, source_target_pairs={{0,1},{1,0},{2,3},{3,2},{4,5},{5,4},{6,7},{7,6},{8,9},{9,8},{10,11... | collective-permute-start | bytes 6291464 | tf_op jit(solution)/shard_map/ppermute | solution.py:501
  47.5 3.5 %all-to-all-start.2 = ((bf16[4,512,256]{2,1,0:T(8,128)(2,1)}), bf16[4,512,256]{2,1,0:T(8,128)(2,1)S(1)}, u32[]{:S(2)}, u32[]{:S(2)}) async-start(bf16[4,512,256]{2,1,0:T(8,128)(2,1)} %copy-done.2), calls=%async_computation.2 | async-start | bytes 2097152 | tf_op jit(solution)/shard_map/all_to_all | solution.py:502
  51.0 0.0 copy-start
  51.0 1.0 copy-done
  52.1 0.1 partial.1.part
  52.2 14.8 %collective-permute-start.3 = (bf16[256,256]{1,0:T(8,128)(2,1)S(1)}, bf16[256,256]{1,0:T(8,128)(2,1)S(1)}, u32[]{:S(2)}, u32[]{:S(2)}) collective-permute-start(bf16[256,256]{1,0:T(8,128)(2,1)S(1)} %partial.1.part), channel_id=1, source_target_pairs={{0,2},{2,0},{1,3},{3,1},{4,6},{6,4},{5,7},{7,5},{8,10},{10,8},{9,1... | collective-permute-start | bytes 393224 | tf_op jit(solution)/shard_map/ppermute | solution.py:504
  67.0 0.1 all-to-all-done.2.moved
  67.0 0.0 collective-permute-done.2.wq_c
  67.0 3.1 %head_terms.1.acc = f32[4,128,512]{2,1,0:T(8,128)S(1)} custom-call(bf16[4,512,256]{2,1,0:T(8,128)(2,1)S(1)} %all-to-all-done.2.moved, bf16[4,2048,128]{2,1,0:T(8,128)(2,1)S(1)} %all-to-all-done.wq, bf16[4,2048,128]{2,1,0:T(8,128)(2,1)} %collective-permute-done.2.wq_c), custom_call_target="tpu_custom_call" | custom-call | flops 536870912 | bytes 6291456 | tf_op jit(solution)/shard_map/head_terms/pallas_call | solution.py:389
  70.1 9.6 %collective-permute-done.3.far = bf16[256,256]{1,0:T(8,128)(2,1)S(1)} collective-permute-done((bf16[256,256]{1,0:T(8,128)(2,1)S(1)}, bf16[256,256]{1,0:T(8,128)(2,1)S(1)}, u32[]{:S(2)}, u32[]{:S(2)}) %collective-permute-start.3) | collective-permute-done | bytes 131104 | tf_op jit(solution)/shard_map/ppermute | solution.py:504
  79.7 0.3 complete.1
  80.0 0.0 copy-start.1
  80.0 0.8 copy-done.1
  80.8 4.3 %all-to-all-start.3 = ((bf16[4,128,512]{2,1,0:T(8,128)(2,1)}), bf16[4,128,512]{2,1,0:T(8,128)(2,1)}, u32[]{:S(2)}, u32[]{:S(2)}) async-start(bf16[4,128,512]{2,1,0:T(8,128)(2,1)} %copy-done.1), calls=%async_computation.3 | async-start | bytes 1048576 | tf_op jit(solution)/shard_map/all_to_all | solution.py:508
  85.1 3.2 %project.1 = (bf16[4,128,512]{2,1,0:T(8,128)(2,1)S(1)}, bf16[128,256]{1,0:T(8,128)(2,1)}) custom-call(s32[1]{0:T(128)} %bitcast.place_s.spot, bf16[4,512,256]{2,1,0:T(8,128)(2,1)S(1)} %all-to-all-done.2.moved, bf16[256,256]{1,0:T(8,128)(2,1)S(1)} %partial.1.part, bf16[256,256]{1,0:T(8,128)(2,1)S(1)} %collective-permute-done.3.far, ...), custom_call_target="tpu_custom_call" | custom-call | flops 671088640 | bytes 6291456 | tf_op jit(solution)/shard_map/project/pallas_call | solution.py:352
  88.3 0.0 copy-start.4
  88.3 0.8 copy-done.4
  89.1 5.6 %all-to-all-done.3.terms = bf16[4,128,512]{2,1,0:T(8,128)(2,1)} async-done(((bf16[4,128,512]{2,1,0:T(8,128)(2,1)}), bf16[4,128,512]{2,1,0:T(8,128)(2,1)}, u32[]{:S(2)}, u32[]{:S(2)}) %all-to-all-start.3) | async-done | bytes 524320 | tf_op jit(solution)/shard_map/all_to_all | solution.py:508
  94.7 1.1 gather.1
  95.8 12.1 %collective-permute-start.4 = (bf16[128,512]{1,0:T(8,128)(2,1)S(1)}, bf16[128,512]{1,0:T(8,128)(2,1)S(1)}, u32[]{:S(2)}, u32[]{:S(2)}) collective-permute-start(bf16[128,512]{1,0:T(8,128)(2,1)S(1)} %gather.1), channel_id=1, source_target_pairs={{0,2},{2,0},{1,3},{3,1},{4,6},{6,4},{5,7},{7,5},{8,10},{10,8},{9,1... | collective-permute-start | bytes 393224 | tf_op jit(solution)/shard_map/ppermute | solution.py:512
  107.9 3.5 %all-to-all-start.4 = ((bf16[4,128,512]{2,1,0:T(8,128)(2,1)}), bf16[4,128,512]{2,1,0:T(8,128)(2,1)S(1)}, u32[]{:S(2)}, u32[]{:S(2)}) async-start(bf16[4,128,512]{2,1,0:T(8,128)(2,1)} %copy-done.4), calls=%async_computation.4 | async-start | bytes 1048576 | tf_op jit(solution)/shard_map/all_to_all | solution.py:513
  111.4 4.0 %collective-permute-done.4.far = bf16[128,512]{1,0:T(8,128)(2,1)S(1)} collective-permute-done((bf16[128,512]{1,0:T(8,128)(2,1)S(1)}, bf16[128,512]{1,0:T(8,128)(2,1)S(1)}, u32[]{:S(2)}, u32[]{:S(2)}) %collective-permute-start.4) | collective-permute-done | bytes 131104 | tf_op jit(solution)/shard_map/ppermute | solution.py:512
  115.5 4.0 %all-to-all-done.4.terms = bf16[4,128,512]{2,1,0:T(8,128)(2,1)S(1)} async-done(((bf16[4,128,512]{2,1,0:T(8,128)(2,1)}), bf16[4,128,512]{2,1,0:T(8,128)(2,1)S(1)}, u32[]{:S(2)}, u32[]{:S(2)}) %all-to-all-start.4) | async-done | bytes 524320 | tf_op jit(solution)/shard_map/all_to_all | solution.py:513
  119.4 0.7 finish.1
  (1 shorter events, 0.0 us)
Async XLA Ops:
  3.1 30.8 %all-to-all-start = ((bf16[4,2048,128]{2,1,0:T(8,128)(2,1)}), bf16[4,2048,128]{2,1,0:T(8,128)(2,1)S(1)}, u32[]{:S(2)}, u32[]{:S(2)}) async-start(bf16[4,2048,128]{2,1,0:T(8,128)(2,1)} %get-tuple-element.25), calls=%async_computation | async-start | bytes 4194304 | tf_op jit(solution)/shard_map/all_to_all | solution.py:494
  7.6 13.7 %copy-start.5 = (bf16[128,256]{1,0:T(8,128)(2,1)S(1)}, bf16[128,256]{1,0:T(8,128)(2,1)}, u32[]{:S(2)}) copy-start(bf16[128,256]{1,0:T(8,128)(2,1)} %get-tuple-element.22.wkv) | copy-start | bytes 196612
  19.4 5.2 %collective-permute-start = (bf16[4,2,128,384]{3,2,1,0:T(8,128)(2,1)}, bf16[4,2,128,384]{3,2,1,0:T(8,128)(2,1)S(1)}, u32[]{:S(2)}, u32[]{:S(2)}) collective-permute-start(bf16[4,2,128,384]{3,2,1,0:T(8,128)(2,1)} %get-tuple-element.21), channel_id=1, source_target_pairs={{0,1},{1,0},{2,3},{3,2},{4,5},{5,4},{6,7},{7,6},{8,9},{9,8},{10,11... | collective-permute-start | bytes 2359304 | tf_op jit(solution)/shard_map/ppermute | solution.py:497
  21.3 3.3 %collective-permute-start.1 = (bf16[128,256]{1,0:T(8,128)(2,1)S(1)}, bf16[128,256]{1,0:T(8,128)(2,1)S(1)}, u32[]{:S(2)}, u32[]{:S(2)}) collective-permute-start(bf16[128,256]{1,0:T(8,128)(2,1)S(1)} %copy-done.5), channel_id=1, source_target_pairs={{0,1},{1,0},{2,3},{3,2},{4,5},{5,4},{6,7},{7,6},{8,9},{9,8},{10,11... | collective-permute-start | bytes 196616 | tf_op jit(solution)/shard_map/ppermute | solution.py:497
  24.6 1.1 copy-start.3
  26.7 1.0 copy-start.2
  45.6 21.5 %collective-permute-start.2 = (bf16[4,2048,128]{2,1,0:T(8,128)(2,1)S(1)}, bf16[4,2048,128]{2,1,0:T(8,128)(2,1)}, u32[]{:S(2)}, u32[]{:S(2)}) collective-permute-start(bf16[4,2048,128]{2,1,0:T(8,128)(2,1)S(1)} %all-to-all-done.wq), channel_id=1, source_target_pairs={{0,1},{1,0},{2,3},{3,2},{4,5},{5,4},{6,7},{7,6},{8,9},{9,8},{10,11... | collective-permute-start | bytes 6291464 | tf_op jit(solution)/shard_map/ppermute | solution.py:501
  47.5 19.5 %all-to-all-start.2 = ((bf16[4,512,256]{2,1,0:T(8,128)(2,1)}), bf16[4,512,256]{2,1,0:T(8,128)(2,1)S(1)}, u32[]{:S(2)}, u32[]{:S(2)}) async-start(bf16[4,512,256]{2,1,0:T(8,128)(2,1)} %copy-done.2), calls=%async_computation.2 | async-start | bytes 2097152 | tf_op jit(solution)/shard_map/all_to_all | solution.py:502
  51.0 1.0 copy-start
  52.2 27.5 %collective-permute-start.3 = (bf16[256,256]{1,0:T(8,128)(2,1)S(1)}, bf16[256,256]{1,0:T(8,128)(2,1)S(1)}, u32[]{:S(2)}, u32[]{:S(2)}) collective-permute-start(bf16[256,256]{1,0:T(8,128)(2,1)S(1)} %partial.1.part), channel_id=1, source_target_pairs={{0,2},{2,0},{1,3},{3,1},{4,6},{6,4},{5,7},{7,5},{8,10},{10,8},{9,1... | collective-permute-start | bytes 393224 | tf_op jit(solution)/shard_map/ppermute | solution.py:504
  80.0 0.8 copy-start.1
  80.8 13.9 %all-to-all-start.3 = ((bf16[4,128,512]{2,1,0:T(8,128)(2,1)}), bf16[4,128,512]{2,1,0:T(8,128)(2,1)}, u32[]{:S(2)}, u32[]{:S(2)}) async-start(bf16[4,128,512]{2,1,0:T(8,128)(2,1)} %copy-done.1), calls=%async_computation.3 | async-start | bytes 1048576 | tf_op jit(solution)/shard_map/all_to_all | solution.py:508
  88.3 0.8 copy-start.4
  95.8 19.6 %collective-permute-start.4 = (bf16[128,512]{1,0:T(8,128)(2,1)S(1)}, bf16[128,512]{1,0:T(8,128)(2,1)S(1)}, u32[]{:S(2)}, u32[]{:S(2)}) collective-permute-start(bf16[128,512]{1,0:T(8,128)(2,1)S(1)} %gather.1), channel_id=1, source_target_pairs={{0,2},{2,0},{1,3},{3,1},{4,6},{6,4},{5,7},{7,5},{8,10},{10,8},{9,1... | collective-permute-start | bytes 393224 | tf_op jit(solution)/shard_map/ppermute | solution.py:512
  107.9 11.5 %all-to-all-start.4 = ((bf16[4,128,512]{2,1,0:T(8,128)(2,1)}), bf16[4,128,512]{2,1,0:T(8,128)(2,1)S(1)}, u32[]{:S(2)}, u32[]{:S(2)}) async-start(bf16[4,128,512]{2,1,0:T(8,128)(2,1)} %copy-done.4), calls=%async_computation.4 | async-start | bytes 1048576 | tf_op jit(solution)/shard_map/all_to_all | solution.py:513
